TPU v7x, 32 devices: a whole 2x2x4 slice. The times are simulated.
32 devices in a mesh: seq: 4 (over y, x), expert: 8 (over z, core).
Axes of the slice: x: 2, y: 2, z: 4, core: 2. Of those that a mesh axis runs over, the one named last changes fastest.
Arguments:
- tokens: bfloat16 [512, 2048], P(('seq', 'expert')), may hold values from -6 to 6
- out_grads: bfloat16 [512, 2048], P(('seq', 'expert')), may hold values from -6 to 6
- route_ids: int32 [512, 6], P(('seq', 'expert')), may hold values from 0 to 15, all different within a row; in each aligned block of 16 rows (0 to 15, 16 to 31, ...) at most 8 rows name the same one
- route_probs: bfloat16 [512, 6], P(('seq', 'expert')), may hold values from 0.049804688 to 1
- w_gate_up: bfloat16 [32, 2, 704, 2048], P(('seq', 'expert')), may hold values from -0.125 to 0.125
- w_down: bfloat16 [32, 704, 2048], P(('seq', 'expert')), may hold values from -0.15625 to 0.15625
Outputs:
- grad_tokens: bfloat16 [512, 2048], P(('seq', 'expert'))
- grad_probs: float32 [512, 6], P(('seq', 'expert'))
- grad_gate_up: bfloat16 [32, 2, 704, 2048], P(('seq', 'expert'))
- grad_down: bfloat16 [32, 704, 2048], P(('seq', 'expert'))
Inputs may be any that keep to these rules, and one draw needn't show every extreme that they name: `route_ids`: in the rows of one device (16 aligned rows) no expert is named by more than 8 routes, a bound that some block reaches; a token's 6 experts differ.
All inputs are finite; a program needn't handle non-finite values.
Results may differ from a plain program's by a relative error of at most 0.0065.
Values may be sent and summed in bfloat16 or wider, within the bound.
No kernel may reach another device: no remote copies, remote signals or barrier semaphores. Data moves between devices by JAX's collectives and lax.ppermute only.
A program may use at most 64 MiB of HBM per device.

v0:
```python
import jax
import jax.numpy as jnp
from jax import lax
from jax.sharding import PartitionSpec as P


def slot_picks(route_ids, experts, capacity):
    rows, top = route_ids.shape
    flat = route_ids.reshape(rows * top)
    onehot = (flat[:, None] == jnp.arange(experts, dtype=jnp.int32)[None, :]).astype(jnp.int32)
    rank = jnp.sum((jnp.cumsum(onehot, axis=0) - onehot) * onehot, axis=1)
    target = flat * capacity + rank
    return jnp.arange(experts * capacity, dtype=jnp.int32)[:, None] == target[None, :]


def expert_side(xs, dys, weights, w_gate_up, w_down):
    w_gate = w_gate_up[0, 0]
    w_up = w_gate_up[0, 1]
    w_out = w_down[0]
    contract = (((1,), (1,)), ((), ()))
    gate = lax.dot_general(xs, w_gate, contract, preferred_element_type=jnp.float32)
    upper = lax.dot_general(xs, w_up, contract, preferred_element_type=jnp.float32)
    sig = jax.nn.sigmoid(gate)
    act = gate * sig * upper
    err = lax.dot_general(dys, w_out, contract, preferred_element_type=jnp.float32)
    score = jnp.sum(err * act, axis=1)
    weight = weights.astype(jnp.float32)[:, None]
    delta = weight * err
    grad_g = (delta * upper * sig * (1.0 + gate * (1.0 - sig))).astype(jnp.bfloat16)
    grad_u = (delta * gate * sig).astype(jnp.bfloat16)
    scaled = (weight * dys.astype(jnp.float32)).astype(jnp.bfloat16)
    inner = (((0,), (0,)), ((), ()))
    grad_gate = lax.dot_general(grad_g, xs, inner, preferred_element_type=jnp.float32).astype(
        jnp.bfloat16
    )
    grad_up = lax.dot_general(grad_u, xs, inner, preferred_element_type=jnp.float32).astype(
        jnp.bfloat16
    )
    grad_gu = jnp.stack([grad_gate, grad_up], 0)[None]
    grad_out = lax.dot_general(
        act.astype(jnp.bfloat16), scaled, inner, preferred_element_type=jnp.float32
    ).astype(jnp.bfloat16)[None]
    dx_part = jnp.dot(grad_g, w_gate, preferred_element_type=jnp.float32) + jnp.dot(
        grad_u, w_up, preferred_element_type=jnp.float32
    )
    return (dx_part, score, grad_gu, grad_out)


def body(tokens, out_grads, route_ids, route_probs, w_gate_up, w_down):
    rows, width = tokens.shape
    top = route_ids.shape[1]
    columns = lax.axis_size("expert")
    groups = lax.axis_size("seq")
    slices = columns // 4
    experts = groups * 4
    capacity = max(2, (rows * top * 4 // 3 + experts - 1) // experts)
    picks = slot_picks(route_ids, experts, capacity)
    token_pick = jnp.any(picks.reshape(experts * capacity, rows, top), axis=2).astype(jnp.bfloat16)
    pick_float = picks.astype(jnp.float32)
    send_x = jnp.dot(token_pick, tokens, preferred_element_type=jnp.float32).astype(jnp.bfloat16)
    send_dy = jnp.dot(token_pick, out_grads, preferred_element_type=jnp.float32).astype(
        jnp.bfloat16
    )
    send_p = jnp.sum(
        pick_float * route_probs.reshape(1, rows * top).astype(jnp.float32), axis=1
    ).astype(jnp.bfloat16)
    arrived = (
        lax.all_to_all(
            send_x.reshape(groups, 4 * capacity, width),
            "seq",
            split_axis=0,
            concat_axis=0,
            tiled=True,
        ),
        lax.all_to_all(
            send_dy.reshape(groups, 4 * capacity, width),
            "seq",
            split_axis=0,
            concat_axis=0,
            tiled=True,
        ),
        lax.all_to_all(
            send_p.reshape(groups, 4 * capacity), "seq", split_axis=0, concat_axis=0, tiled=True
        ),
    )
    arrived_x = arrived[0].reshape(groups, 4, capacity, width)
    arrived_dy = arrived[1].reshape(groups, 4, capacity, width)
    fan_p = jnp.repeat(jnp.moveaxis(arrived[2].reshape(groups, 4, capacity), 1, 0), slices, axis=0)
    total_rows = columns * groups * capacity
    fan_x = jnp.repeat(jnp.moveaxis(arrived_x, 1, 0), slices, axis=0)
    fan_dy = jnp.repeat(jnp.moveaxis(arrived_dy, 1, 0), slices, axis=0)
    got = (
        lax.all_to_all(fan_x, "expert", split_axis=0, concat_axis=0, tiled=True),
        lax.all_to_all(fan_dy, "expert", split_axis=0, concat_axis=0, tiled=True),
        lax.all_to_all(fan_p, "expert", split_axis=0, concat_axis=0, tiled=True),
    )
    xs = got[0].reshape(total_rows, width)
    dys = got[1].reshape(total_rows, width)
    weights = got[2].reshape(total_rows)
    dx_part, score, grad_gu, grad_out = expert_side(xs, dys, weights, w_gate_up, w_down)
    back = (
        lax.all_to_all(
            dx_part.astype(jnp.bfloat16).reshape(columns, groups, capacity, width),
            "expert",
            split_axis=0,
            concat_axis=0,
            tiled=True,
        ),
        lax.all_to_all(
            score.astype(jnp.bfloat16).reshape(columns, groups, capacity),
            "expert",
            split_axis=0,
            concat_axis=0,
            tiled=True,
        ),
    )
    dx_sum = jnp.sum(
        back[0].reshape(4, slices, groups, capacity, width).astype(jnp.float32), axis=1
    ).astype(jnp.bfloat16)
    score_sum = jnp.sum(
        back[1].reshape(4, slices, groups, capacity).astype(jnp.float32), axis=1
    ).astype(jnp.bfloat16)
    home = (
        lax.all_to_all(dx_sum, "seq", split_axis=1, concat_axis=0, tiled=True),
        lax.all_to_all(score_sum, "seq", split_axis=1, concat_axis=0, tiled=True),
    )
    slot_dx = home[0].reshape(experts * capacity, width)
    slot_score = home[1].reshape(experts * capacity)
    grad_tokens = lax.dot_general(
        token_pick, slot_dx, (((0,), (0,)), ((), ())), preferred_element_type=jnp.float32
    ).astype(jnp.bfloat16)
    grad_probs = jnp.sum(pick_float * slot_score.astype(jnp.float32)[:, None], axis=0).reshape(
        rows, top
    )
    return (grad_tokens, grad_probs, grad_gu, grad_out)


def solution(mesh):
    in_specs = (
        P(("seq", "expert"), None),
        P(("seq", "expert"), None),
        P(("seq", "expert"), None),
        P(("seq", "expert"), None),
        P(("seq", "expert"), None, None, None),
        P(("seq", "expert"), None, None),
    )
    out_specs = (
        P(("seq", "expert"), None),
        P(("seq", "expert"), None),
        P(("seq", "expert"), None, None, None),
        P(("seq", "expert"), None, None),
    )
    return jax.shard_map(body, mesh=mesh, in_specs=in_specs, out_specs=out_specs, check_vma=False)
```

profile of v0, /device:TPU:0, one launch (start us, length us, event | category | flops | bytes accessed | tf_op | source)
XLA Modules:
  0.0 186.0 jit_solution(12670934584960607892)
XLA Ops:
  5.0 5.2 %all-to-all-start.4 = ((bf16[4,32,2048]{2,1,0:T(8,128)(2,1)}), bf16[4,32,2048]{2,1,0:T(8,128)(2,1)S(1)}, u32[]{:S(2)}, u32[]{:S(2)}) async-start(bf16[4,32,2048]{2,1,0:T(8,128)(2,1)} %bitcast.79), calls=%async_computation.4 | async-start | bytes 1048576 | tf_op jit(solution)/shard_map/all_to_all | solution.py:68
  12.1 6.0 %all-to-all-done.4 = bf16[4,32,2048]{2,1,0:T(8,128)(2,1)S(1)} async-done(((bf16[4,32,2048]{2,1,0:T(8,128)(2,1)}), bf16[4,32,2048]{2,1,0:T(8,128)(2,1)S(1)}, u32[]{:S(2)}, u32[]{:S(2)}) %all-to-all-start.4) | async-done | bytes 524320 | tf_op jit(solution)/shard_map/all_to_all | solution.py:68
  18.2 4.1 %all-to-all-start.2 = ((bf16[4,32,2048]{2,1,0:T(8,128)(2,1)}), bf16[4,32,2048]{2,1,0:T(8,128)(2,1)}, u32[]{:S(2)}, u32[]{:S(2)}) async-start(bf16[4,32,2048]{2,1,0:T(8,128)(2,1)} %bitcast.78), calls=%async_computation.2 | async-start | bytes 1048576 | tf_op jit(solution)/shard_map/all_to_all | solution.py:75
  23.4 6.1 %all-to-all-done.2 = bf16[4,32,2048]{2,1,0:T(8,128)(2,1)} async-done(((bf16[4,32,2048]{2,1,0:T(8,128)(2,1)}), bf16[4,32,2048]{2,1,0:T(8,128)(2,1)}, u32[]{:S(2)}, u32[]{:S(2)}) %all-to-all-start.2) | async-done | bytes 524320 | tf_op jit(solution)/shard_map/all_to_all | solution.py:75
  30.6 4.9 %all-to-all-start.5 = ((bf16[8,4,8,2048]{3,2,1,0:T(8,128)(2,1)}), bf16[8,4,8,2048]{3,2,1,0:T(8,128)(2,1)}, u32[]{:S(2)}, u32[]{:S(2)}) async-start(bf16[8,4,8,2048]{3,2,1,0:T(8,128)(2,1)} %bitcast.74), calls=%async_computation.5 | async-start | bytes 2097152 | tf_op jit(solution)/shard_map/all_to_all | solution.py:93
  36.6 25.6 %all-to-all-done.5 = bf16[8,4,8,2048]{3,2,1,0:T(8,128)(2,1)} async-done(((bf16[8,4,8,2048]{3,2,1,0:T(8,128)(2,1)}), bf16[8,4,8,2048]{3,2,1,0:T(8,128)(2,1)}, u32[]{:S(2)}, u32[]{:S(2)}) %all-to-all-start.5) | async-done | bytes 1048608 | tf_op jit(solution)/shard_map/all_to_all | solution.py:93
  63.3 4.2 %all-to-all-start.3 = ((bf16[8,4,8,2048]{3,2,1,0:T(8,128)(2,1)}), bf16[8,4,8,2048]{3,2,1,0:T(8,128)(2,1)}, u32[]{:S(2)}, u32[]{:S(2)}) async-start(bf16[8,4,8,2048]{3,2,1,0:T(8,128)(2,1)} %bitcast.75), calls=%async_computation.3 | async-start | bytes 2097152 | tf_op jit(solution)/shard_map/all_to_all | solution.py:94
  67.6 4.0 %fusion.5 = f32[256,704]{0,1:T(8,128)} fusion(bf16[256,2048]{1,0:T(8,128)(2,1)} %bitcast.12, bf16[1,2,704,2048]{3,2,1,0:T(8,128)(2,1)} %param.10), kind=kOutput, calls=%fused_computation.9 | convolution fusion | flops 738197504 | bytes 4653056 | tf_op jit(solution)/shard_map/dot_general | solution.py:21
  71.5 4.0 %fusion.9 = f32[256,704]{0,1:T(8,128)} fusion(bf16[256,2048]{1,0:T(8,128)(2,1)} %bitcast.12, bf16[1,2,704,2048]{3,2,1,0:T(8,128)(2,1)} %param.10), kind=kOutput, calls=%fused_computation.13 | convolution fusion | flops 738197504 | bytes 4653056 | tf_op jit(solution)/shard_map/dot_general | solution.py:22
  75.5 18.7 %all-to-all-done.3 = bf16[8,4,8,2048]{3,2,1,0:T(8,128)(2,1)} async-done(((bf16[8,4,8,2048]{3,2,1,0:T(8,128)(2,1)}), bf16[8,4,8,2048]{3,2,1,0:T(8,128)(2,1)}, u32[]{:S(2)}, u32[]{:S(2)}) %all-to-all-start.3) | async-done | bytes 1048608 | tf_op jit(solution)/shard_map/all_to_all | solution.py:94
  94.2 3.5 %multiply_reduce_fusion = (bf16[256]{0:T(256)(128)(2,1)S(1)}, f32[256,704]{0,1:T(8,128)}) fusion(f32[256,704]{0,1:T(8,128)} %fusion.9, f32[256,704]{0,1:T(8,128)} %fusion.5, bf16[256,2048]{1,0:T(8,128)(2,1)} %bitcast.6, bf16[1,704,2048]{2,1,0:T(8,128)(2,1)S(1)} %copy-done), kind=kOutput, calls=%fused_computation.29 | convolution fusion | flops 739458816 | bytes 6095360 | tf_op jit(solution)/shard_map/dot_general | solution.py:25
  98.4 3.3 %all-to-all-start.8 = ((bf16[8,4,8]{2,1,0:T(4,128)(2,1)}), bf16[8,4,8]{2,1,0:T(4,128)(2,1)S(1)}, u32[]{:S(2)}, u32[]{:S(2)}) async-start(bf16[8,4,8]{2,1,0:T(4,128)(2,1)} %convert_element_type.117), calls=%async_computation.8 | async-start | bytes 16384 | tf_op jit(solution)/shard_map/all_to_all | solution.py:109
  101.7 5.5 %all-to-all-done.8 = bf16[8,4,8]{2,1,0:T(4,128)(2,1)S(1)} async-done(((bf16[8,4,8]{2,1,0:T(4,128)(2,1)}), bf16[8,4,8]{2,1,0:T(4,128)(2,1)S(1)}, u32[]{:S(2)}, u32[]{:S(2)}) %all-to-all-start.8) | async-done | bytes 544 | tf_op jit(solution)/shard_map/all_to_all | solution.py:109
  107.9 3.2 %all-to-all-start.9 = ((bf16[4,4,8]{2,0,1:T(4,128)(2,1)}), bf16[4,4,8]{2,0,1:T(4,128)(2,1)S(1)}, u32[]{:S(2)}, u32[]{:S(2)}) async-start(bf16[4,4,8]{2,0,1:T(4,128)(2,1)} %copy.80), calls=%async_computation.9 | async-start | bytes 8192 | tf_op jit(solution)/shard_map/all_to_all | solution.py:125
  111.3 4.5 %all-to-all-done.9 = bf16[4,4,8]{2,0,1:T(4,128)(2,1)S(1)} async-done(((bf16[4,4,8]{2,0,1:T(4,128)(2,1)}), bf16[4,4,8]{2,0,1:T(4,128)(2,1)S(1)}, u32[]{:S(2)}, u32[]{:S(2)}) %all-to-all-start.9) | async-done | bytes 288 | tf_op jit(solution)/shard_map/all_to_all | solution.py:125
  116.1 7.0 %all_to_all.65 = bf16[4,1,32]{2,1,0:T(2,128)(2,1)S(1)} all-to-all(bf16[4,1,32]{2,1,0:T(2,128)(2,1)S(1)} %convert_element_type.133), channel_id=1, replica_groups=mesh['seq'=4,'expert'=8] {'seq'}, dimensions={0} | all-to-all | bytes 512 | tf_op jit(solution)/shard_map/all_to_all | solution.py:82
  123.2 8.0 %all_to_all.66 = bf16[8,4,8]{2,1,0:T(4,128)(2,1)S(1)} all-to-all(bf16[8,4,8]{2,1,0:T(4,128)(2,1)S(1)} %bitcast.81), channel_id=1, replica_groups=mesh['seq'=4,'expert'=8] {'expert'}, dimensions={0} | all-to-all | bytes 1024 | tf_op jit(solution)/shard_map/all_to_all | solution.py:95
  136.7 3.8 %fusion.16 = bf16[256,2048]{1,0:T(8,128)(2,1)} fusion(f32[256,2048]{1,0:T(8,128)S(1)} %fusion.3, bf16[256,704]{0,1:T(8,128)(2,1)S(1)} %get-tuple-element.34, bf16[1,2,704,2048]{3,2,1,0:T(8,128)(2,1)} %param.10), kind=kOutput, calls=%fused_computation.18 | convolution fusion | flops 739246080 | bytes 6389760 | tf_op jit(solution)/shard_map/dot_general | solution.py:43
  140.6 4.2 %all-to-all-start.6 = ((bf16[8,4,8,2048]{3,2,1,0:T(8,128)(2,1)}), bf16[8,4,8,2048]{3,2,1,0:T(8,128)(2,1)}, u32[]{:S(2)}, u32[]{:S(2)}) async-start(bf16[8,4,8,2048]{3,2,1,0:T(8,128)(2,1)} %bitcast.73), calls=%async_computation.6 | async-start | bytes 2097152 | tf_op jit(solution)/shard_map/all_to_all | solution.py:102
  145.6 3.8 %fusion.1 = bf16[1,704,2048]{2,1,0:T(8,128)(2,1)} fusion(bf16[256,704]{0,1:T(8,128)(2,1)S(1)} %get-tuple-element.34, bf16[256,2048]{1,0:T(8,128)(2,1)} %bitcast.12), kind=kOutput, calls=%fused_computation.5 | convolution fusion | flops 739639296 | bytes 4292608 | tf_op jit(solution)/shard_map/dot_general | solution.py:36
  149.4 3.9 %fusion.2 = bf16[1,704,2048]{2,1,0:T(8,128)(2,1)} fusion(bf16[256,2048]{1,0:T(8,128)(2,1)} %bitcast.6, f32[256]{0:T(256)S(1)} %reshape.138, f32[256,704]{0,1:T(8,128)S(1)} %copy-done.5, f32[256,704]{0,1:T(8,128)S(1)} %copy-done.4), kind=kOutput, calls=%fused_computation.6 | convolution fusion | flops 742293504 | bytes 5374976 | tf_op jit(solution)/shard_map/dot_general | solution.py:40
  153.3 18.1 %all-to-all-done.6 = bf16[8,4,8,2048]{3,2,1,0:T(8,128)(2,1)} async-done(((bf16[8,4,8,2048]{3,2,1,0:T(8,128)(2,1)}), bf16[8,4,8,2048]{3,2,1,0:T(8,128)(2,1)}, u32[]{:S(2)}, u32[]{:S(2)}) %all-to-all-start.6) | async-done | bytes 1048608 | tf_op jit(solution)/shard_map/all_to_all | solution.py:102
  173.7 3.5 %all-to-all-start.7 = ((bf16[4,4,8,2048]{3,2,0,1:T(8,128)(2,1)}), bf16[4,4,8,2048]{3,2,0,1:T(8,128)(2,1)S(1)}, u32[]{:S(2)}, u32[]{:S(2)}) async-start(bf16[4,4,8,2048]{3,2,0,1:T(8,128)(2,1)} %copy.79), calls=%async_computation.7 | async-start | bytes 1048576 | tf_op jit(solution)/shard_map/all_to_all | solution.py:124
  179.6 3.0 %maximum_bitcast_fusion = bf16[1,2,704,2048]{3,2,1,0:T(8,128)(2,1)} fusion(bf16[1,704,2048]{2,1,0:T(8,128)(2,1)S(1)} %copy-done.1, bf16[1,704,2048]{2,1,0:T(8,128)(2,1)S(1)} %fusion), kind=kLoop, calls=%fused_computation | loop fusion | flops 2883584 | bytes 11534336 | tf_op jit(solution)/shard_map/broadcast_in_dim | solution.py:39
  (54 shorter events, 27.0 us)
Async XLA Ops:
  0.6 93.6 %copy-start = (bf16[1,704,2048]{2,1,0:T(8,128)(2,1)S(1)}, bf16[1,704,2048]{2,1,0:T(8,128)(2,1)}, u32[]{:S(2)}) copy-start(bf16[1,704,2048]{2,1,0:T(8,128)(2,1)} %param.11) | copy-start | bytes 8650756
  5.0 13.2 %all-to-all-start.4 = ((bf16[4,32,2048]{2,1,0:T(8,128)(2,1)}), bf16[4,32,2048]{2,1,0:T(8,128)(2,1)S(1)}, u32[]{:S(2)}, u32[]{:S(2)}) async-start(bf16[4,32,2048]{2,1,0:T(8,128)(2,1)} %bitcast.79), calls=%async_computation.4 | async-start | bytes 1048576 | tf_op jit(solution)/shard_map/all_to_all | solution.py:68
  18.2 4.1 %copy-start.2 = (bf16[4,32,2048]{2,1,0:T(8,128)(2,1)}, bf16[4,32,2048]{2,1,0:T(8,128)(2,1)S(1)}, u32[]{:S(2)}) copy-start(bf16[4,32,2048]{2,1,0:T(8,128)(2,1)S(1)} %all-to-all-done.4) | copy-start | bytes 1572868
  18.2 11.3 %all-to-all-start.2 = ((bf16[4,32,2048]{2,1,0:T(8,128)(2,1)}), bf16[4,32,2048]{2,1,0:T(8,128)(2,1)}, u32[]{:S(2)}, u32[]{:S(2)}) async-start(bf16[4,32,2048]{2,1,0:T(8,128)(2,1)} %bitcast.78), calls=%async_computation.2 | async-start | bytes 1048576 | tf_op jit(solution)/shard_map/all_to_all | solution.py:75
  30.6 31.6 %all-to-all-start.5 = ((bf16[8,4,8,2048]{3,2,1,0:T(8,128)(2,1)}), bf16[8,4,8,2048]{3,2,1,0:T(8,128)(2,1)}, u32[]{:S(2)}, u32[]{:S(2)}) async-start(bf16[8,4,8,2048]{3,2,1,0:T(8,128)(2,1)} %bitcast.74), calls=%async_computation.5 | async-start | bytes 2097152 | tf_op jit(solution)/shard_map/all_to_all | solution.py:93
  63.3 30.8 %all-to-all-start.3 = ((bf16[8,4,8,2048]{3,2,1,0:T(8,128)(2,1)}), bf16[8,4,8,2048]{3,2,1,0:T(8,128)(2,1)}, u32[]{:S(2)}, u32[]{:S(2)}) async-start(bf16[8,4,8,2048]{3,2,1,0:T(8,128)(2,1)} %bitcast.75), calls=%async_computation.3 | async-start | bytes 2097152 | tf_op jit(solution)/shard_map/all_to_all | solution.py:94
  94.2 16.9 %copy-start.6 = (bf16[16,6]{0,1:T(8,128)(2,1)S(1)}, bf16[16,6]{0,1:T(8,128)(2,1)}, u32[]{:S(2)}) copy-start(bf16[16,6]{0,1:T(8,128)(2,1)} %param.9) | copy-start | bytes 580
  98.4 8.9 %all-to-all-start.8 = ((bf16[8,4,8]{2,1,0:T(4,128)(2,1)}), bf16[8,4,8]{2,1,0:T(4,128)(2,1)S(1)}, u32[]{:S(2)}, u32[]{:S(2)}) async-start(bf16[8,4,8]{2,1,0:T(4,128)(2,1)} %convert_element_type.117), calls=%async_computation.8 | async-start | bytes 16384 | tf_op jit(solution)/shard_map/all_to_all | solution.py:109
  107.9 7.9 %all-to-all-start.9 = ((bf16[4,4,8]{2,0,1:T(4,128)(2,1)}), bf16[4,4,8]{2,0,1:T(4,128)(2,1)S(1)}, u32[]{:S(2)}, u32[]{:S(2)}) async-start(bf16[4,4,8]{2,0,1:T(4,128)(2,1)} %copy.80), calls=%async_computation.9 | async-start | bytes 8192 | tf_op jit(solution)/shard_map/all_to_all | solution.py:125
  133.2 0.7 copy-start.3
  140.6 30.8 %all-to-all-start.6 = ((bf16[8,4,8,2048]{3,2,1,0:T(8,128)(2,1)}), bf16[8,4,8,2048]{3,2,1,0:T(8,128)(2,1)}, u32[]{:S(2)}, u32[]{:S(2)}) async-start(bf16[8,4,8,2048]{3,2,1,0:T(8,128)(2,1)} %bitcast.73), calls=%async_computation.6 | async-start | bytes 2097152 | tf_op jit(solution)/shard_map/all_to_all | solution.py:102
  145.6 3.8 %copy-start.4 = (f32[256,704]{0,1:T(8,128)S(1)}, f32[256,704]{0,1:T(8,128)}, u32[]{:S(2)}) copy-start(f32[256,704]{0,1:T(8,128)} %fusion.5) | copy-start | bytes 2162692
  145.6 3.8 %copy-start.5 = (f32[256,704]{0,1:T(8,128)S(1)}, f32[256,704]{0,1:T(8,128)}, u32[]{:S(2)}) copy-start(f32[256,704]{0,1:T(8,128)} %fusion.9) | copy-start | bytes 2162692
  173.7 11.5 %all-to-all-start.7 = ((bf16[4,4,8,2048]{3,2,0,1:T(8,128)(2,1)}), bf16[4,4,8,2048]{3,2,0,1:T(8,128)(2,1)S(1)}, u32[]{:S(2)}, u32[]{:S(2)}) async-start(bf16[4,4,8,2048]{3,2,0,1:T(8,128)(2,1)} %copy.79), calls=%async_computation.7 | async-start | bytes 1048576 | tf_op jit(solution)/shard_map/all_to_all | solution.py:124
  177.1 2.4 %copy-start.1 = (bf16[1,704,2048]{2,1,0:T(8,128)(2,1)S(1)}, bf16[1,704,2048]{2,1,0:T(8,128)(2,1)}, u32[]{:S(2)}) copy-start(bf16[1,704,2048]{2,1,0:T(8,128)(2,1)} %fusion.1) | copy-start | bytes 8650756
where the time goes:
time: 187 us; the launch traced here: 186 us
  waiting for transfers between devices  87.1 us (47%)
  matrix products  32.9 us (18%)
  starting transfers between devices  32.7 us (17%)
  blocking collectives  14.9 us (8%)
  local copies, waits for them, and re-layouts  9.77 us (5%)
  other arithmetic  7.7 us (4%)
    all_to_all x1, waiting for transfers between devices, body(): lax.all_to_all(fan_x, 'expert', split_axis=0, concat_axis=0, tiled=True)  25.6 us
    all_to_all x1, waiting for transfers between devices, body(): lax.all_to_all(fan_dy, 'expert', split_axis=0, concat_axis=0, tiled=True)  18.7 us
    all_to_all x1, waiting for transfers between devices, body(): lax.all_to_all(dx_part.astype(jnp.bfloat16).reshape(columns, groups, capa...  18.1 us
    all_to_all x1, blocking collectives, body(): lax.all_to_all(fan_p, 'expert', split_axis=0, concat_axis=0, tiled=True)  7.97 us
    all_to_all x1, blocking collectives, body(): lax.all_to_all(send_p.reshape(groups, 4 * capacity), 'seq', split_axis=0,...  6.98 us
    all_to_all x1, waiting for transfers between devices, body(): lax.all_to_all(send_dy.reshape(groups, 4 * capacity, width), 'seq', split...  6.11 us
    all_to_all x1, waiting for transfers between devices, body(): lax.all_to_all(send_x.reshape(groups, 4 * capacity, width), 'seq', split_...  6.04 us
    all_to_all x1, waiting for transfers between devices, body(): lax.all_to_all(score.astype(jnp.bfloat16).reshape(columns, groups, capaci...  5.52 us
  transfers between devices with their start and end apart: 8, of which 8 were waited for; matrix products, arithmetic and copies ran while one was open for 14% of the time, Pallas kernels for 0%

commit v1 on v0

v1 whole, which is shorter than its diff:
```python
import jax
import jax.numpy as jnp
from jax import lax
from jax.experimental import pallas as pl
from jax.experimental.pallas import tpu as pltpu
from jax.sharding import Mesh
from jax.sharding import PartitionSpec as P

LANES = 128
LIMIT = 50 * 1024 * 1024
F32, BF16 = jnp.float32, jnp.bfloat16


def dot(a, b, ca, cb):
    return lax.dot_general(a, b, (((ca,), (cb,)), ((), ())), preferred_element_type=F32)


def slot_table(ids, capacity, slots):
    rows, top = ids.shape
    lane = lax.broadcasted_iota(jnp.int32, (rows, slots), 1)
    expert, place = lane // capacity, lane % capacity
    named = jnp.zeros((rows, slots), F32)
    for k in range(top):
        named = named + (ids[:, k : k + 1] == expert).astype(F32)
    earlier = lax.broadcasted_iota(jnp.int32, (rows, rows), 1) < lax.broadcasted_iota(
        jnp.int32, (rows, rows), 0
    )
    rank = dot(earlier.astype(BF16), named.astype(BF16), 1, 0)
    held = jnp.where(rank == place.astype(F32), named, 0.0)
    return expert, held


def pack_kernel(capacity, x_ref, dy_ref, ids_ref, p_ref, out_ref):
    slots, width = out_ref.shape[0], x_ref.shape[1]
    ids = ids_ref[...]
    expert, held = slot_table(ids, capacity, slots)
    probs = p_ref[...].astype(F32)
    weight = jnp.zeros(held.shape, F32)
    for k in range(ids.shape[1]):
        weight = weight + jnp.where(ids[:, k : k + 1] == expert, probs[:, k : k + 1], 0.0)
    pick = held.astype(BF16)
    out_ref[:, :width] = dot(pick, x_ref[...], 0, 0).astype(BF16)
    out_ref[:, width : 2 * width] = dot(pick, dy_ref[...], 0, 0).astype(BF16)
    ones = jnp.ones((ids.shape[0], LANES), BF16)
    out_ref[:, 2 * width :] = dot((held * weight).astype(BF16), ones, 0, 0).astype(BF16)


def main_kernel(parts, *refs):
    got = refs[:parts]
    wgu_hbm, wd_hbm = refs[parts : parts + 2]
    dx_out = refs[parts + 2 : 2 * parts + 2]
    gg_ref, gu_ref, act_ref, x_out, scaled_ref = refs[2 * parts + 2 : 2 * parts + 7]
    rows_ref, wg, wu, wd, sems = refs[2 * parts + 7 :]
    slots, width = got[0].shape[0], wg.shape[1]
    row_copies = [
        pltpu.make_async_copy(got[i], rows_ref.at[pl.ds(i * slots, slots)], sems.at[3 + i])
        for i in range(parts)
    ]
    w_copies = [
        pltpu.make_async_copy(wgu_hbm.at[0, 0], wg, sems.at[0]),
        pltpu.make_async_copy(wgu_hbm.at[0, 1], wu, sems.at[1]),
        pltpu.make_async_copy(wd_hbm.at[0], wd, sems.at[2]),
    ]
    for c in row_copies:
        c.start()
    for c in w_copies:
        c.start()
    for c in row_copies:
        c.wait()
    w_copies[0].wait()
    gate = dot(wg[...], rows_ref[:, :width], 1, 1)
    w_copies[1].wait()
    upper = dot(wu[...], rows_ref[:, :width], 1, 1)
    w_copies[2].wait()
    err = dot(wd[...], rows_ref[:, width : 2 * width], 1, 1)
    weight_col = rows_ref[:, 2 * width :].astype(F32)
    weight = jnp.transpose(weight_col)[0:1, :]
    sig = jax.nn.sigmoid(gate)
    silu = gate * sig
    act = silu * upper
    score = jnp.sum(err * act, axis=0, keepdims=True)
    delta = weight * err
    gg = (delta * upper * sig * (1.0 + gate * (1.0 - sig))).astype(BF16)
    gu = (delta * silu).astype(BF16)
    gg_ref[...] = gg
    gu_ref[...] = gu
    act_ref[...] = act.astype(BF16)
    score_col = jnp.transpose(jnp.broadcast_to(score, (LANES, score.shape[1]))).astype(BF16)
    dx = (dot(gg, wg[...], 0, 0) + dot(gu, wu[...], 0, 0)).astype(BF16)
    for i in range(parts):
        dx_out[i][:, :width] = dx[i * slots : (i + 1) * slots]
        dx_out[i][:, width:] = score_col[i * slots : (i + 1) * slots]
    x_out[...] = rows_ref[:, :width]
    dys = rows_ref[:, width : 2 * width].astype(F32)
    scaled_ref[...] = (weight_col[:, 0:1] * dys).astype(BF16)


def weights_kernel(gg_ref, gu_ref, act_ref, x_ref, scaled_ref, dgu_hbm, dd_hbm, buf, sems):
    copies = [
        pltpu.make_async_copy(buf.at[0], dgu_hbm.at[0, 0], sems.at[0]),
        pltpu.make_async_copy(buf.at[1], dgu_hbm.at[0, 1], sems.at[1]),
        pltpu.make_async_copy(buf.at[2], dd_hbm.at[0], sems.at[2]),
    ]
    for i, (lhs, rhs) in enumerate(((gg_ref, x_ref), (gu_ref, x_ref), (act_ref, scaled_ref))):
        buf[i] = dot(lhs[...], rhs[...], 1, 0).astype(BF16)
        copies[i].start()
    for c in copies:
        c.wait()


def add_kernel(parts, *refs):
    total = refs[0][...].astype(F32)
    for r in refs[1:parts]:
        total = total + r[...].astype(F32)
    refs[parts][...] = total.astype(BF16)


def final_kernel(capacity, back_ref, ids_ref, dx_ref, dp_ref):
    slots, width = back_ref.shape[0], dx_ref.shape[1]
    ids = ids_ref[...]
    rows, top = ids.shape
    expert, held = slot_table(ids, capacity, slots)
    dx_ref[...] = dot(held.astype(BF16), back_ref[:, :width], 1, 0).astype(BF16)
    score = back_ref[:, width:]
    lane = lax.broadcasted_iota(jnp.int32, (rows, LANES), 1)
    probs = jnp.zeros((rows, LANES), F32)
    for k in range(top):
        mine = jnp.where(ids[:, k : k + 1] == expert, held, 0.0).astype(BF16)
        probs = jnp.where(lane == k, dot(mine, score, 1, 0), probs)
    dp_ref[...] = probs[:, :top]


def params():
    return pltpu.CompilerParams(vmem_limit_bytes=LIMIT)


VMEM = pl.BlockSpec(memory_space=pltpu.VMEM)
ANY = pl.BlockSpec(memory_space=pl.ANY)


def body(tokens, out_grads, route_ids, route_probs, w_gate_up, w_down):
    rows, width = tokens.shape
    top = route_ids.shape[1]
    groups, deep, parts = lax.axis_size("seq"), lax.axis_size("z"), lax.axis_size("slice")
    experts = groups * deep
    hidden = w_down.shape[1]
    capacity = max(2, (rows * top * 4 // 3 + experts - 1) // experts)
    slots = experts * capacity
    total = slots * parts

    def everywhere(v):
        return lax.all_to_all(
            v.reshape(experts, capacity, v.shape[1]),
            ("seq", "z"),
            split_axis=0,
            concat_axis=0,
            tiled=True,
        ).reshape(v.shape)

    def across(v, step):
        return lax.ppermute(v, "slice", [(i, (i + step) % parts) for i in range(parts)])

    packed = pl.pallas_call(
        lambda *r: pack_kernel(capacity, *r),
        out_shape=jax.ShapeDtypeStruct((slots, 2 * width + LANES), BF16),
        in_specs=[VMEM] * 4,
        out_specs=VMEM,
        compiler_params=params(),
        name="pack",
    )(tokens, out_grads, route_ids, route_probs)
    mine = everywhere(packed)
    got = [mine] + [across(mine, i) for i in range(1, parts)]

    sd = jax.ShapeDtypeStruct
    outs = pl.pallas_call(
        lambda *r: main_kernel(parts, *r),
        out_shape=[sd((slots, width + LANES), BF16)] * parts
        + [sd((hidden, total), BF16)] * 3
        + [sd((total, width), BF16)] * 2,
        in_specs=[ANY] * (parts + 2),
        out_specs=[VMEM] * (parts + 5),
        scratch_shapes=[
            pltpu.VMEM((total, 2 * width + LANES), BF16),
            pltpu.VMEM((hidden, width), BF16),
            pltpu.VMEM((hidden, width), BF16),
            pltpu.VMEM((hidden, width), BF16),
            pltpu.SemaphoreType.DMA((3 + parts,)),
        ],
        compiler_params=params(),
        name="expert",
    )(*got, w_gate_up, w_down)
    dx_parts, (gg, gu, act, xs, scaled) = outs[:parts], outs[parts:]
    returned = [dx_parts[0]] + [across(dx_parts[i], -i) for i in range(1, parts)]
    summed = pl.pallas_call(
        lambda *r: add_kernel(parts, *r),
        out_shape=sd((slots, width + LANES), BF16),
        in_specs=[VMEM] * parts,
        out_specs=VMEM,
        compiler_params=params(),
        name="add",
    )(*returned)
    back = everywhere(summed)
    grad_gu, grad_down = pl.pallas_call(
        weights_kernel,
        out_shape=[sd(w_gate_up.shape, BF16), sd(w_down.shape, BF16)],
        in_specs=[VMEM] * 5,
        out_specs=[ANY] * 2,
        scratch_shapes=[
            pltpu.VMEM((3, hidden, width), BF16),
            pltpu.SemaphoreType.DMA((3,)),
        ],
        compiler_params=params(),
        cost_estimate=pl.CostEstimate(
            flops=6 * hidden * total * width,
            bytes_accessed=10 * hidden * width,
            transcendentals=0,
        ),
        name="weights",
    )(gg, gu, act, xs, scaled)
    grad_tokens, grad_probs = pl.pallas_call(
        lambda *r: final_kernel(capacity, *r),
        out_shape=[sd((rows, width), BF16), sd((rows, top), F32)],
        in_specs=[VMEM] * 2,
        out_specs=[VMEM] * 2,
        compiler_params=params(),
        name="final",
    )(back, route_ids)
    return grad_tokens, grad_probs, grad_gu, grad_down


def solution(mesh):
    groups, columns = mesh.devices.shape
    split = Mesh(mesh.devices.reshape(groups, 4, columns // 4), ("seq", "z", "slice"))
    every = ("seq", "z", "slice")

    def spec(rank):
        return P(every, *([None] * (rank - 1)))

    return jax.shard_map(
        body,
        mesh=split,
        in_specs=(spec(2), spec(2), spec(2), spec(2), spec(4), spec(3)),
        out_specs=(spec(2), spec(2), spec(4), spec(3)),
        check_vma=False,
    )
```

time: 187 us -> 82 us (0.44)
  waiting for transfers between devices: 87.1 us -> 16.3 us
  matrix products: 32.9 us -> 0 us
  starting transfers between devices: 32.7 us -> 3.78 us
  blocking collectives: 14.9 us -> 36.2 us
  Pallas kernels: 0 us -> 18.5 us
  other arithmetic: 7.7 us -> 0 us
  local copies, waits for them, and re-layouts: 9.77 us -> 6.08 us
    all_to_all x8 -> x1, waiting for transfers between devices: 87.1 us -> 11.8 us  [everywhere(): lax.all_to_all(v.reshape(experts, capacity, v.shape[1]), ('seq', 'z'), sp...]
    dot_general x11 -> x0, matrix products: 32.9 us -> none  [the longest x1 3.96 us: expert_side(): lax.dot_general(xs, w_up, contract, preferred_element_type=jnp.float32)]
    all_to_all x8 -> x1, starting transfers between devices: 32.7 us -> 3.58 us  [everywhere(): lax.all_to_all(v.reshape(experts, capacity, v.shape[1]), ('seq', 'z'), sp...]
    all_to_all x2 -> x1, blocking collectives: 14.9 us -> 36.2 us  [everywhere(): lax.all_to_all(v.reshape(experts, capacity, v.shape[1]), ('seq', 'z'), sp...]
    pallas_call x0 -> x5, Pallas kernels: none -> 18.5 us  [the longest x1 11.5 us: body(): pl.pallas_call(lambda *r: main_kernel(parts, *r), out_shape=[sd((slots, w...]
    ppermute x0 -> x2, waiting for transfers between devices: none -> 4.52 us  [across(): lax.ppermute(v, 'slice', [(i, (i + step) % parts) for i in range(parts)])]
    unnamed x16 -> x13, local copies, waits for them, and re-layouts: 2.37 us -> 6.08 us
    broadcast_in_dim x1 -> x0, other arithmetic: 3.03 us -> none  [expert_side(): grad_gu = jnp.stack([grad_gate, grad_up], 0)[None]]
  transfers between devices with their start and end apart: 8 -> 3, of which waited for: 8 -> 3; matrix products, arithmetic and copies ran while one was open for 14% -> 0% of each run, Pallas kernels for 0% -> 5%
where the time goes in v1:
time: 82 us; the launch traced here: 81.6 us
  blocking collectives  36.2 us (44%)
  Pallas kernels  18.5 us (23%)
  waiting for transfers between devices  16.3 us (20%)
  local copies, waits for them, and re-layouts  6.08 us (7%)
  starting transfers between devices  3.78 us (5%)
    all_to_all x1, blocking collectives, everywhere(): lax.all_to_all(v.reshape(experts, capacity, v.shape[1]), ('seq', 'z'), sp...  36.2 us
    all_to_all x1, waiting for transfers between devices, everywhere(): lax.all_to_all(v.reshape(experts, capacity, v.shape[1]), ('seq', 'z'), sp...  11.8 us
    pallas_call x1, Pallas kernels, body(): pl.pallas_call(lambda *r: main_kernel(parts, *r), out_shape=[sd((slots, w...  11.5 us
    unnamed x13, local copies, waits for them, and re-layouts  6.08 us
    ppermute x2, waiting for transfers between devices, across(): lax.ppermute(v, 'slice', [(i, (i + step) % parts) for i in range(parts)])  4.52 us
    pallas_call x1, Pallas kernels, body(): pl.pallas_call(weights_kernel, out_shape=[sd(w_gate_up.shape, BF16), sd(w...  4.42 us
    all_to_all x1, starting transfers between devices, everywhere(): lax.all_to_all(v.reshape(experts, capacity, v.shape[1]), ('seq', 'z'), sp...  3.58 us
  transfers between devices with their start and end apart: 3, of which 3 were waited for; matrix products, arithmetic and copies ran while one was open for 0% of the time, Pallas kernels for 5%

profile of v1, /device:TPU:0, one launch (start us, length us, event | category | flops | bytes accessed | tf_op | source)
XLA Modules:
  0.0 81.6 jit_solution(645356552769260195)
XLA Ops:
  0.6 0.8 copy.11.r_3_
  1.4 0.8 copy.10.r_2_.r_1_
  2.2 0.0 copy-start
  2.2 0.8 %copy-done = bf16[16,2048]{1,0:T(8,128)(2,1)S(1)} copy-done((bf16[16,2048]{1,0:T(8,128)(2,1)S(1)}, bf16[16,2048]{1,0:T(8,128)(2,1)}, u32[]{:S(2)}) %copy-start) | copy-done | bytes 65560
  3.0 0.0 copy-start.1
  3.0 0.8 %copy-done.1 = bf16[16,2048]{1,0:T(8,128)(2,1)S(1)} copy-done((bf16[16,2048]{1,0:T(8,128)(2,1)S(1)}, bf16[16,2048]{1,0:T(8,128)(2,1)}, u32[]{:S(2)}) %copy-start.1) | copy-done | bytes 65560
  3.8 0.7 pack.1
  4.5 36.2 %all_to_all.10 = bf16[16,8,4224]{2,1,0:T(8,128)(2,1)S(1)} all-to-all(bf16[16,8,4224]{2,1,0:T(8,128)(2,1)S(1)} %bitcast.4), channel_id=1, replica_groups=mesh['seq'=4,'z'=4,'slice'=2] {'seq','z'}, dimensions={0} | all-to-all | bytes 2162688 | tf_op jit(solution)/shard_map/all_to_all | solution.py:152
  40.8 0.0 copy-start.3
  40.8 0.0 collective-permute-start
  40.8 2.7 %collective-permute-done.r_1_ = bf16[128,4224]{1,0:T(8,128)(2,1)S(1)} collective-permute-done((bf16[128,4224]{1,0:T(8,128)(2,1)S(1)}, bf16[128,4224]{1,0:T(8,128)(2,1)S(1)}, u32[]{:S(2)}, u32[]{:S(2)}) %collective-permute-start) | collective-permute-done | bytes 1081376 | tf_op jit(solution)/shard_map/ppermute | solution.py:161
  43.5 0.0 copy-done.3
  43.5 1.0 %copy-done.4 = bf16[128,4224]{1,0:T(8,128)(2,1)} copy-done((bf16[128,4224]{1,0:T(8,128)(2,1)}, bf16[128,4224]{1,0:T(8,128)(2,1)S(1)}, u32[]{:S(2)}) %copy-start.4) | copy-done | bytes 1081368
  44.5 11.5 %expert.1 = (bf16[128,2176]{1,0:T(8,128)(2,1)S(1)}, bf16[128,2176]{1,0:T(8,128)(2,1)S(1)}, bf16[704,256]{1,0:T(8,128)(2,1)S(1)}, bf16[704,256]{1,0:T(8,128)(2,1)...) custom-call(bf16[128,4224]{1,0:T(8,128)(2,1)} %bitcast.7, ...), custom_call_target="tpu_custom_call" | custom-call | tf_op jit(solution)/shard_map/expert/pallas_call | solution.py:175
  55.9 0.2 collective-permute-start.1
  56.1 1.8 %collective-permute-done.1.r_1_ = bf16[128,2176]{1,0:T(8,128)(2,1)S(1)} collective-permute-done((bf16[128,2176]{1,0:T(8,128)(2,1)S(1)}, bf16[128,2176]{1,0:T(8,128)(2,1)S(1)}, u32[]{:S(2)}, u32[]{:S(2)}) %collective-permute-start.1) | collective-permute-done | bytes 557088 | tf_op jit(solution)/shard_map/ppermute | solution.py:161
  57.9 1.0 %add.1 = bf16[128,2176]{1,0:T(8,128)(2,1)} custom-call(bf16[128,2176]{1,0:T(8,128)(2,1)S(1)} %get-tuple-element.15.r_0_, bf16[128,2176]{1,0:T(8,128)(2,1)S(1)} %collective-permute-done.1.r_1_), custom_call_target="tpu_custom_call" | custom-call | tf_op jit(solution)/shard_map/add/pallas_call | solution.py:194
  58.9 3.6 %all-to-all-start.1 = ((bf16[16,8,2176]{2,1,0:T(8,128)(2,1)}), bf16[16,8,2176]{2,1,0:T(8,128)(2,1)S(1)}, u32[]{:S(2)}, u32[]{:S(2)}) async-start(bf16[16,8,2176]{2,1,0:T(8,128)(2,1)} %bitcast.2), calls=%async_computation.1 | async-start | bytes 1114112 | tf_op jit(solution)/shard_map/all_to_all | solution.py:152
  62.5 0.0 copy-start.2
  62.5 1.2 %copy-done.2 = bf16[256,2048]{1,0:T(8,128)(2,1)S(1)} copy-done((bf16[256,2048]{1,0:T(8,128)(2,1)S(1)}, bf16[256,2048]{1,0:T(8,128)(2,1)}, u32[]{:S(2)}) %copy-start.2) | copy-done | bytes 1048600
  63.7 4.4 %weights.1 = (bf16[1,2,704,2048]{3,2,1,0:T(8,128)(2,1)}, bf16[1,704,2048]{2,1,0:T(8,128)(2,1)}) custom-call(bf16[704,256]{1,0:T(8,128)(2,1)S(1)} %get-tuple-element.19.gg_ref, bf16[704,256]{1,0:T(8,128)(2,1)S(1)} %get-tuple-element.20.gu_ref, bf16[704,256]{1,0:T(8,128)(2,1)S(1)} %get-tuple-element.21.act_ref, bf16[256,2048]{1,0:T(8,128)(2,1)S(1)} %get-tuple-element.22.x_ref, ...), custom_call_target="tpu_custom_call" | custom-call | flops 2214592512 | bytes 14417920 | tf_op jit(solution)/shard_map/weights/pallas_call | solution.py:203
  68.2 11.8 %all-to-all-done.1 = bf16[16,8,2176]{2,1,0:T(8,128)(2,1)S(1)} async-done(((bf16[16,8,2176]{2,1,0:T(8,128)(2,1)}), bf16[16,8,2176]{2,1,0:T(8,128)(2,1)S(1)}, u32[]{:S(2)}, u32[]{:S(2)}) %all-to-all-start.1) | async-done | bytes 557088 | tf_op jit(solution)/shard_map/all_to_all | solution.py:152
  79.9 1.0 %final.1 = (bf16[16,2048]{1,0:T(8,128)(2,1)}, f32[16,6]{1,0:T(8,128)S(1)}) custom-call(bf16[128,2176]{1,0:T(8,128)(2,1)S(1)} %bitcast.5, s32[16,6]{1,0:T(8,128)S(1)} %copy.10.r_2_.r_1_), custom_call_target="tpu_custom_call" | custom-call | tf_op jit(solution)/shard_map/final/pallas_call | solution.py:220
  80.9 0.7 copy.13
  (1 shorter events, 0.0 us)
Async XLA Ops:
  2.2 0.8 %copy-start = (bf16[16,2048]{1,0:T(8,128)(2,1)S(1)}, bf16[16,2048]{1,0:T(8,128)(2,1)}, u32[]{:S(2)}) copy-start(bf16[16,2048]{1,0:T(8,128)(2,1)} %r_0_.1) | copy-start | bytes 196612
  3.0 0.8 %copy-start.1 = (bf16[16,2048]{1,0:T(8,128)(2,1)S(1)}, bf16[16,2048]{1,0:T(8,128)(2,1)}, u32[]{:S(2)}) copy-start(bf16[16,2048]{1,0:T(8,128)(2,1)} %r_1_.2) | copy-start | bytes 196612
  40.8 2.7 %copy-start.3 = (bf16[16,8,4224]{2,1,0:T(8,128)(2,1)}, bf16[16,8,4224]{2,1,0:T(8,128)(2,1)S(1)}, u32[]{:S(2)}) copy-start(bf16[16,8,4224]{2,1,0:T(8,128)(2,1)S(1)} %all_to_all.10) | copy-start | bytes 3244036
  40.8 2.7 %collective-permute-start = (bf16[128,4224]{1,0:T(8,128)(2,1)S(1)}, bf16[128,4224]{1,0:T(8,128)(2,1)S(1)}, u32[]{:S(2)}, u32[]{:S(2)}) collective-permute-start(bf16[128,4224]{1,0:T(8,128)(2,1)S(1)} %bitcast.6), channel_id=1, source_target_pairs={{0,1},{1,0},{2,3},{3,2},{4,5},{5,4},{6,7},{7,6},{8,9},{9,8},{10,11... | collective-permute-start | bytes 3244040 | tf_op jit(solution)/shard_map/ppermute | solution.py:161
  43.5 1.0 %copy-start.4 = (bf16[128,4224]{1,0:T(8,128)(2,1)}, bf16[128,4224]{1,0:T(8,128)(2,1)S(1)}, u32[]{:S(2)}) copy-start(bf16[128,4224]{1,0:T(8,128)(2,1)S(1)} %collective-permute-done.r_1_) | copy-start | bytes 3244036
  55.9 2.0 %collective-permute-start.1 = (bf16[128,2176]{1,0:T(8,128)(2,1)S(1)}, bf16[128,2176]{1,0:T(8,128)(2,1)S(1)}, u32[]{:S(2)}, u32[]{:S(2)}) collective-permute-start(bf16[128,2176]{1,0:T(8,128)(2,1)S(1)} %get-tuple-element.16), channel_id=1, source_target_pairs={{0,1},{1,0},{2,3},{3,2},{4,5},{5,4},{6,7},{7,6},{8,9},{9,8},{10,11... | collective-permute-start | bytes 1671176 | tf_op jit(solution)/shard_map/ppermute | solution.py:161
  58.9 21.0 %all-to-all-start.1 = ((bf16[16,8,2176]{2,1,0:T(8,128)(2,1)}), bf16[16,8,2176]{2,1,0:T(8,128)(2,1)S(1)}, u32[]{:S(2)}, u32[]{:S(2)}) async-start(bf16[16,8,2176]{2,1,0:T(8,128)(2,1)} %bitcast.2), calls=%async_computation.1 | async-start | bytes 1114112 | tf_op jit(solution)/shard_map/all_to_all | solution.py:152
  62.5 1.2 %copy-start.2 = (bf16[256,2048]{1,0:T(8,128)(2,1)S(1)}, bf16[256,2048]{1,0:T(8,128)(2,1)}, u32[]{:S(2)}) copy-start(bf16[256,2048]{1,0:T(8,128)(2,1)} %get-tuple-element.23.scaled_ref) | copy-start | bytes 3145732

commit v2 on v1

v2 whole, which is shorter than its diff:
```python
import jax
import jax.numpy as jnp
from jax import lax
from jax.experimental import pallas as pl
from jax.experimental.pallas import tpu as pltpu
from jax.sharding import Mesh
from jax.sharding import PartitionSpec as P

LANES = 128
F32, BF16 = jnp.float32, jnp.bfloat16


def dot(a, b, ca, cb):
    return lax.dot_general(a, b, (((ca,), (cb,)), ((), ())), preferred_element_type=F32)


def lane_map(count, start):
    row = lax.broadcasted_iota(jnp.int32, (count, LANES), 0)
    lane = lax.broadcasted_iota(jnp.int32, (count, LANES), 1)
    return (lane == row + start).astype(BF16)


def slot_table(meta, top, upper_half, which, capacity, slots):
    rows = meta.shape[0]
    lane = lax.broadcasted_iota(jnp.int32, (rows, slots), 1)
    device = lane // (2 * capacity)
    expert = ((device // 2) * 4 + upper_half * 2 + device % 2).astype(F32)
    mine = (lane // capacity) % 2 == which
    place = (lane % capacity).astype(F32)
    match = [meta[:, k : k + 1] == expert for k in range(top)]
    named = jnp.zeros((rows, slots), F32)
    for m in match:
        named = named + m.astype(F32)
    earlier = lax.broadcasted_iota(jnp.int32, (rows, rows), 1) < lax.broadcasted_iota(
        jnp.int32, (rows, rows), 0
    )
    rank = dot(earlier.astype(BF16), named.astype(BF16), 1, 0)
    held = jnp.where(mine & (rank == place), named, 0.0)
    return match, held


def pack_kernel(x_hbm, dy_hbm, ids_ref, p_ref, out_ref, sems):
    width, top = x_hbm.shape[1], ids_ref.shape[0]
    copies = [
        pltpu.make_async_copy(x_hbm, out_ref.at[:, pl.ds(0, width)], sems.at[0]),
        pltpu.make_async_copy(dy_hbm, out_ref.at[:, pl.ds(width, width)], sems.at[1]),
    ]
    for c in copies:
        c.start()
    ids = ids_ref[...].astype(F32).astype(BF16)
    meta = dot(ids, lane_map(top, 0), 0, 0) + dot(p_ref[...], lane_map(top, top), 0, 0)
    out_ref[:, 2 * width :] = meta.astype(BF16)
    for c in copies:
        c.wait()


def select_kernel(top, capacity, half_ref, own_ref, far_ref, out_ref):
    slots, width = out_ref.shape[0], (out_ref.shape[1] - LANES) // 2
    picks, weighted = [], []
    for which, ref in enumerate((own_ref, far_ref)):
        meta = ref[:, 2 * width :].astype(F32)
        match, held = slot_table(meta, top, half_ref[0], which, capacity, slots)
        weight = jnp.zeros(held.shape, F32)
        for k in range(top):
            weight = weight + jnp.where(match[k], meta[:, top + k : top + k + 1], 0.0)
        picks.append(held)
        weighted.append(held * weight)
    pick = jnp.concatenate(picks, 0).astype(BF16)
    rows = jnp.concatenate([own_ref[:, : 2 * width], far_ref[:, : 2 * width]], 0)
    out_ref[:, : 2 * width] = dot(pick, rows, 0, 0).astype(BF16)
    ones = jnp.ones((pick.shape[0], LANES), BF16)
    weights = jnp.concatenate(weighted, 0).astype(BF16)
    out_ref[:, 2 * width :] = dot(weights, ones, 0, 0).astype(BF16)


def expert_kernel(parts, *refs):
    got = refs[:parts]
    wgu_ref, wd_ref = refs[parts : parts + 2]
    dx_out = refs[parts + 2 : 2 * parts + 2]
    gg_ref, gu_ref, act_ref = refs[2 * parts + 2 :]
    width = wd_ref.shape[2]
    slots = got[0].shape[0]
    xs = jnp.concatenate([r[:, :width] for r in got], 0)
    dys = jnp.concatenate([r[:, width : 2 * width] for r in got], 0)
    weight = jnp.concatenate([r[:, 2 * width :] for r in got], 0).astype(F32)[:, 0:1]
    gate = dot(xs, wgu_ref[0, 0], 1, 1)
    upper = dot(xs, wgu_ref[0, 1], 1, 1)
    err = dot(dys, wd_ref[0], 1, 1)
    sig = jax.nn.sigmoid(gate)
    silu = gate * sig
    act = silu * upper
    score = jnp.sum(err * act, axis=1, keepdims=True)
    delta = weight * err
    gg = (delta * upper * sig * (1.0 + gate * (1.0 - sig))).astype(BF16)
    gu = (delta * silu).astype(BF16)
    gg_ref[...] = gg
    gu_ref[...] = gu
    act_ref[...] = act.astype(BF16)
    score_col = jnp.broadcast_to(score, (score.shape[0], LANES)).astype(BF16)
    dx = (dot(gg, wgu_ref[0, 0], 1, 0) + dot(gu, wgu_ref[0, 1], 1, 0)).astype(BF16)
    for i in range(parts):
        dx_out[i][:, :width] = dx[i * slots : (i + 1) * slots]
        dx_out[i][:, width:] = score_col[i * slots : (i + 1) * slots]


def weights_kernel(parts, *refs):
    got = refs[:parts]
    gg_ref, gu_ref, act_ref, dgu_hbm, dd_hbm, buf, sems = refs[parts:]
    width = buf.shape[2]
    copies = [
        pltpu.make_async_copy(buf.at[0], dgu_hbm.at[0, 0], sems.at[0]),
        pltpu.make_async_copy(buf.at[1], dgu_hbm.at[0, 1], sems.at[1]),
        pltpu.make_async_copy(buf.at[2], dd_hbm.at[0], sems.at[2]),
    ]
    xs = jnp.concatenate([r[:, :width] for r in got], 0)
    buf[0] = dot(gg_ref[...], xs, 0, 0).astype(BF16)
    copies[0].start()
    buf[1] = dot(gu_ref[...], xs, 0, 0).astype(BF16)
    copies[1].start()
    scaled = jnp.concatenate(
        [
            (r[:, 2 * width : 2 * width + 1].astype(F32) * r[:, width : 2 * width].astype(F32)).astype(BF16)
            for r in got
        ],
        0,
    )
    buf[2] = dot(act_ref[...], scaled, 0, 0).astype(BF16)
    copies[2].start()
    for c in copies:
        c.wait()


def add_kernel(parts, *refs):
    total = refs[0][...].astype(F32)
    for r in refs[1:parts]:
        total = total + r[...].astype(F32)
    refs[parts][...] = total.astype(BF16)


def combine_kernel(top, capacity, half_ref, back_ref, own_ref, far_ref, own_out, far_out):
    slots, width = back_ref.shape[0], back_ref.shape[1] - LANES
    lane = lax.broadcasted_iota(jnp.int32, (own_ref.shape[0], LANES), 1)
    for which, (meta_ref, out_ref) in enumerate(((own_ref, own_out), (far_ref, far_out))):
        meta = meta_ref[:, 2 * width :].astype(F32)
        match, held = slot_table(meta, top, half_ref[0], which, capacity, slots)
        dx = dot(held.astype(BF16), back_ref[:, :width], 1, 0)
        probs = jnp.zeros(lane.shape, F32)
        for k in range(top):
            one = jnp.where(match[k], held, 0.0).astype(BF16)
            probs = jnp.where(lane == k, dot(one, back_ref[:, width:], 1, 0), probs)
        out_ref[:, :width] = dx.astype(out_ref.dtype)
        out_ref[:, width:] = probs.astype(out_ref.dtype)


def final_kernel(own_ref, far_ref, dx_ref, dp_ref):
    width, top = dx_ref.shape[1], dp_ref.shape[0]
    dx_ref[...] = (own_ref[:, :width] + far_ref[:, :width].astype(F32)).astype(BF16)
    probs = (own_ref[:, width:] + far_ref[:, width:].astype(F32)).astype(BF16)
    dp_ref[...] = dot(lane_map(top, 0), probs, 1, 1)


def params(mib):
    return pltpu.CompilerParams(vmem_limit_bytes=mib * 1024 * 1024)


VMEM = pl.BlockSpec(memory_space=pltpu.VMEM)
SMEM = pl.BlockSpec(memory_space=pltpu.SMEM)
ANY = pl.BlockSpec(memory_space=pl.ANY)


def body(tokens, out_grads, route_ids, route_probs, w_gate_up, w_down):
    rows, width = tokens.shape
    top = route_ids.shape[1]
    groups, parts = lax.axis_size("seq"), lax.axis_size("slice")
    experts = groups * 4
    hidden = w_down.shape[1]
    capacity = max(2, (rows * top * 4 // 3 + experts - 1) // experts)
    devices = groups * 2
    slots = devices * 2 * capacity
    total = slots * parts
    sd = jax.ShapeDtypeStruct

    def within_half(v):
        return lax.all_to_all(
            v.reshape(devices, 2 * capacity, v.shape[1]),
            ("seq", "zl"),
            split_axis=0,
            concat_axis=0,
            tiled=True,
        ).reshape(v.shape)

    def mirror(v):
        return lax.ppermute(v, ("zh", "zl"), [(i, 3 - i) for i in range(4)])

    def across(v, step):
        return lax.ppermute(v, "slice", [(i, (i + step) % parts) for i in range(parts)])

    half = lax.axis_index("zh").astype(jnp.int32).reshape(1)
    own = pl.pallas_call(
        pack_kernel,
        out_shape=sd((rows, 2 * width + LANES), BF16),
        in_specs=[ANY, ANY, VMEM, VMEM],
        out_specs=VMEM,
        scratch_shapes=[pltpu.SemaphoreType.DMA((2,))],
        compiler_params=params(4),
        name="pack",
    )(tokens, out_grads, route_ids.T, route_probs.T)
    far = mirror(own)
    picked = pl.pallas_call(
        lambda *r: select_kernel(top, capacity, *r),
        out_shape=sd((slots, 2 * width + LANES), BF16),
        in_specs=[SMEM, VMEM, VMEM],
        out_specs=VMEM,
        compiler_params=params(8),
        name="select",
    )(half, own, far)
    mine = within_half(picked)
    got = [mine] + [across(mine, i) for i in range(1, parts)]

    big = params(30)
    outs = pl.pallas_call(
        lambda *r: expert_kernel(parts, *r),
        out_shape=[sd((slots, width + LANES), BF16)] * parts + [sd((total, hidden), BF16)] * 3,
        in_specs=[VMEM] * (parts + 2),
        out_specs=[VMEM] * (parts + 3),
        compiler_params=big,
        name="expert",
    )(*got, w_gate_up, w_down)
    dx_parts, (gg, gu, act) = outs[:parts], outs[parts:]
    returned = [dx_parts[0]] + [across(dx_parts[i], -i) for i in range(1, parts)]
    summed = pl.pallas_call(
        lambda *r: add_kernel(parts, *r),
        out_shape=sd((slots, width + LANES), BF16),
        in_specs=[VMEM] * parts,
        out_specs=VMEM,
        compiler_params=params(12),
        name="add",
    )(*returned)
    back = within_half(summed)
    grad_gu, grad_down = pl.pallas_call(
        lambda *r: weights_kernel(parts, *r),
        out_shape=[sd(w_gate_up.shape, BF16), sd(w_down.shape, BF16)],
        in_specs=[VMEM] * (parts + 3),
        out_specs=[ANY] * 2,
        scratch_shapes=[
            pltpu.VMEM((3, hidden, width), BF16),
            pltpu.SemaphoreType.DMA((3,)),
        ],
        compiler_params=params(40),
        cost_estimate=pl.CostEstimate(
            flops=6 * hidden * total * width,
            bytes_accessed=10 * hidden * width,
            transcendentals=0,
        ),
        name="weights",
    )(*got, gg, gu, act)
    own_sum, far_sum = pl.pallas_call(
        lambda *r: combine_kernel(top, capacity, *r),
        out_shape=[sd((rows, width + LANES), F32), sd((rows, width + LANES), BF16)],
        in_specs=[SMEM] + [VMEM] * 3,
        out_specs=[VMEM] * 2,
        compiler_params=params(8),
        name="combine",
    )(half, back, own, far)
    home = mirror(far_sum)
    grad_tokens, grad_probs = pl.pallas_call(
        final_kernel,
        out_shape=[sd((rows, width), BF16), sd((top, rows), F32)],
        in_specs=[VMEM] * 2,
        out_specs=[VMEM] * 2,
        compiler_params=params(4),
        name="final",
    )(own_sum, home)
    return grad_tokens, grad_probs.T, grad_gu, grad_down


def solution(mesh):
    groups, columns = mesh.devices.shape
    every = ("seq", "zh", "zl", "slice")
    split = Mesh(mesh.devices.reshape(groups, 2, 2, columns // 4), every)

    def spec(rank):
        return P(every, *([None] * (rank - 1)))

    return jax.shard_map(
        body,
        mesh=split,
        in_specs=(spec(2), spec(2), spec(2), spec(2), spec(4), spec(3)),
        out_specs=(spec(2), spec(2), spec(4), spec(3)),
        check_vma=False,
    )
```

time: 82 us -> 67.7 us (0.83)
  waiting for transfers between devices: 16.3 us -> 8.48 us
  Pallas kernels: 18.5 us -> 12 us
  starting transfers between devices: 3.78 us -> 6.75 us
  blocking collectives: 36.2 us -> 33.6 us
    all_to_all x1 -> x0, waiting for transfers between devices: 11.8 us -> none  [everywhere(): lax.all_to_all(v.reshape(experts, capacity, v.shape[1]), ('seq', 'z'), sp...]
    ppermute x0 -> x2, starting transfers between devices: none -> 6.55 us  [mirror(): return lax.ppermute(v, ('zh', 'zl'), [(i, 3 - i) for i in range(4)])]
    pallas_call x4 -> x6, Pallas kernels: 17.5 us -> 11.9 us  [the longest x1 5.15 us: body(): pl.pallas_call(lambda *r: expert_kernel(parts, *r), out_shape=[sd((slots,...]
    ppermute x0 -> x2, waiting for transfers between devices: none -> 3.95 us  [mirror(): return lax.ppermute(v, ('zh', 'zl'), [(i, 3 - i) for i in range(4)])]
    all_to_all x1 -> x0, starting transfers between devices: 3.58 us -> none  [everywhere(): lax.all_to_all(v.reshape(experts, capacity, v.shape[1]), ('seq', 'z'), sp...]
    all_to_all x1 -> x2, blocking collectives: 36.2 us -> 33.6 us  [within_half(): lax.all_to_all(v.reshape(devices, 2 * capacity, v.shape[1]), ('seq', 'zl'...]
    pallas_call x1, Pallas kernels: 0.97 us -> 0.13 us  [body(): pl.pallas_call(lambda *r: add_kernel(parts, *r), out_shape=sd((slots, wid...]
    unnamed x13 -> x12, local copies, waits for them, and re-layouts: 6.08 us -> 5.83 us
  transfers between devices with their start and end apart: 3 -> 4, of which waited for: 3 -> 4; matrix products, arithmetic and copies ran while one was open for 0% -> 0% of each run, Pallas kernels for 5% -> 7%
where the time goes in v2:
time: 67.7 us; the launch traced here: 67.3 us
  blocking collectives  33.6 us (50%)
  Pallas kernels  12 us (18%)
  waiting for transfers between devices  8.48 us (13%)
  starting transfers between devices  6.75 us (10%)
  local copies, waits for them, and re-layouts  5.83 us (9%)
  between operations  0.69 us (1%)
    all_to_all x2, blocking collectives, within_half(): lax.all_to_all(v.reshape(devices, 2 * capacity, v.shape[1]), ('seq', 'zl'...  33.6 us
    ppermute x2, starting transfers between devices, mirror(): return lax.ppermute(v, ('zh', 'zl'), [(i, 3 - i) for i in range(4)])  6.55 us
    unnamed x12, local copies, waits for them, and re-layouts  5.83 us
    pallas_call x1, Pallas kernels, body(): pl.pallas_call(lambda *r: expert_kernel(parts, *r), out_shape=[sd((slots,...  5.15 us
    ppermute x2, waiting for transfers between devices, across(): lax.ppermute(v, 'slice', [(i, (i + step) % parts) for i in range(parts)])  4.53 us
    pallas_call x1, Pallas kernels, body(): pl.pallas_call(lambda *r: weights_kernel(parts, *r), out_shape=[sd(w_gate...  4.45 us
    ppermute x2, waiting for transfers between devices, mirror(): return lax.ppermute(v, ('zh', 'zl'), [(i, 3 - i) for i in range(4)])  3.95 us
  transfers between devices with their start and end apart: 4, of which 4 were waited for; matrix products, arithmetic and copies ran while one was open for 0% of the time, Pallas kernels for 7%

profile of v2, /device:TPU:0, one launch (start us, length us, event | category | flops | bytes accessed | tf_op | source)
XLA Modules:
  0.0 67.3 jit_solution(17492219569144347680)
XLA Ops:
  0.6 0.0 copy-start.1
  0.6 0.0 copy-start.2
  0.7 1.0 %copy-done.2 = bf16[16,2048]{1,0:T(8,128)(2,1)S(1)} copy-done((bf16[16,2048]{1,0:T(8,128)(2,1)S(1)}, bf16[16,2048]{1,0:T(8,128)(2,1)}, u32[]{:S(2)}) %copy-start.2) | copy-done | bytes 65560
  1.6 0.8 %copy-done.3 = bf16[16,2048]{1,0:T(8,128)(2,1)S(1)} copy-done((bf16[16,2048]{1,0:T(8,128)(2,1)S(1)}, bf16[16,2048]{1,0:T(8,128)(2,1)}, u32[]{:S(2)}) %copy-start.3) | copy-done | bytes 65560
  2.5 0.7 %copy-done.4 = s32[16,6]{0,1:T(8,128)S(1)} copy-done((s32[16,6]{0,1:T(8,128)S(1)}, s32[16,6]{0,1:T(8,128)}, u32[]{:S(2)}) %copy-start.4) | copy-done | bytes 408
  3.2 0.7 %copy-done.5 = bf16[16,6]{0,1:T(8,128)(2,1)S(1)} copy-done((bf16[16,6]{0,1:T(8,128)(2,1)S(1)}, bf16[16,6]{0,1:T(8,128)(2,1)}, u32[]{:S(2)}) %copy-start.5) | copy-done | bytes 216
  3.8 0.3 pack.1.r_1_.r_2_
  4.1 5.1 %collective-permute-start = (bf16[16,4224]{1,0:T(8,128)(2,1)S(1)}, bf16[16,4224]{1,0:T(8,128)(2,1)S(1)}, u32[]{:S(2)}, u32[]{:S(2)}) collective-permute-start(bf16[16,4224]{1,0:T(8,128)(2,1)S(1)} %pack.1.r_1_.r_2_), channel_id=1, source_target_pairs={{0,6},{2,4},{4,2},{6,0},{1,7},{3,5},{5,3},{7,1},{8,14},{10,12},{12... | collective-permute-start | bytes 405512 | tf_op jit(solution)/shard_map/ppermute | solution.py:193
  9.2 3.7 %collective-permute-done.r_2_.r_3_ = bf16[16,4224]{1,0:T(8,128)(2,1)S(1)} collective-permute-done((bf16[16,4224]{1,0:T(8,128)(2,1)S(1)}, bf16[16,4224]{1,0:T(8,128)(2,1)S(1)}, u32[]{:S(2)}, u32[]{:S(2)}) %collective-permute-start) | collective-permute-done | bytes 135200 | tf_op jit(solution)/shard_map/ppermute | solution.py:193
  12.9 0.7 select.1
  13.6 20.5 %all_to_all.10 = bf16[8,16,4224]{2,1,0:T(8,128)(2,1)S(1)} all-to-all(bf16[8,16,4224]{2,1,0:T(8,128)(2,1)S(1)} %bitcast.8), channel_id=1, replica_groups=mesh['seq'=4,'zh'=2,'zl'=2,'slice'=2] {'seq','zl'}, dimensions={0} | all-to-all | bytes 2162688 | tf_op jit(solution)/shard_map/all_to_all | solution.py:184
  34.1 0.0 collective-permute-start.1
  34.1 2.7 %collective-permute-done.1.r_1_ = bf16[128,4224]{1,0:T(8,128)(2,1)S(1)} collective-permute-done((bf16[128,4224]{1,0:T(8,128)(2,1)S(1)}, bf16[128,4224]{1,0:T(8,128)(2,1)S(1)}, u32[]{:S(2)}, u32[]{:S(2)}) %collective-permute-start.1) | collective-permute-done | bytes 1081376 | tf_op jit(solution)/shard_map/ppermute | solution.py:196
  36.8 2.6 %copy-done = bf16[1,2,704,2048]{3,2,1,0:T(8,128)(2,1)S(1)} copy-done((bf16[1,2,704,2048]{3,2,1,0:T(8,128)(2,1)S(1)}, bf16[1,2,704,2048]{3,2,1,0:T(8,128)(2,1)}, u32[]{:S(2)}) %copy-start) | copy-done | bytes 5767192
  39.5 5.1 %expert.1 = (bf16[128,2176]{1,0:T(8,128)(2,1)S(1)}, bf16[128,2176]{1,0:T(8,128)(2,1)S(1)}, bf16[256,704]{1,0:T(8,128)(2,1)S(1)}, bf16[256,704]{1,0:T(8,128)(2,1)S(1)}, bf16[256,704]{1,0:T(8,128)(2,1)S(1)}) custom-call(bf16[128,4224]{1,0:T(8,128)(2,1)S(1)} %bitcast.10, bf16[128,4224]{1,0:T(8,128)(2,1)S(1)} %collective-permute-done.1.r_1_, ...), custom_call_target="tpu_custom_call" | custom-call | tf_op jit(solution)/shard_map/expert/pallas_call | solution.py:221
  44.6 0.2 collective-permute-start.2
  44.8 1.8 %collective-permute-done.2.r_1_ = bf16[128,2176]{1,0:T(8,128)(2,1)S(1)} collective-permute-done((bf16[128,2176]{1,0:T(8,128)(2,1)S(1)}, bf16[128,2176]{1,0:T(8,128)(2,1)S(1)}, u32[]{:S(2)}, u32[]{:S(2)}) %collective-permute-start.2) | collective-permute-done | bytes 557088 | tf_op jit(solution)/shard_map/ppermute | solution.py:196
  46.6 0.1 add.1
  46.8 13.1 %all_to_all.11 = bf16[8,16,2176]{2,1,0:T(8,128)(2,1)S(1)} all-to-all(bf16[8,16,2176]{2,1,0:T(8,128)(2,1)S(1)} %bitcast.13), channel_id=1, replica_groups=mesh['seq'=4,'zh'=2,'zl'=2,'slice'=2] {'seq','zl'}, dimensions={0} | all-to-all | bytes 1114112 | tf_op jit(solution)/shard_map/all_to_all | solution.py:184
  59.9 0.6 combine.1
  60.5 1.4 %collective-permute-start.3 = (bf16[16,2176]{1,0:T(8,128)(2,1)S(1)}, bf16[16,2176]{1,0:T(8,128)(2,1)S(1)}, u32[]{:S(2)}, u32[]{:S(2)}) collective-permute-start(bf16[16,2176]{1,0:T(8,128)(2,1)S(1)} %get-tuple-element.18), channel_id=1, source_target_pairs={{0,6},{2,4},{4,2},{6,0},{1,7},{3,5},{5,3},{7,1},{8,14},{10,12},{12... | collective-permute-start | bytes 208904 | tf_op jit(solution)/shard_map/ppermute | solution.py:193
  61.9 4.5 %weights.1 = (bf16[1,2,704,2048]{3,2,1,0:T(8,128)(2,1)}, bf16[1,704,2048]{2,1,0:T(8,128)(2,1)}) custom-call(bf16[128,4224]{1,0:T(8,128)(2,1)S(1)} %bitcast.11, bf16[128,4224]{1,0:T(8,128)(2,1)S(1)} %collective-permute-done.1.r_1_, bf16[256,704]{1,0:T(8,128)(2,1)S(1)} %get-tuple-element.21.r_2_, bf16[256,704]{1,0:T(8,128)(2,1)S(1)} %get-tuple-element.22.r_3_, ...), custom_call_target="tpu_custom_call" | custom-call | flops 2214592512 | bytes 14417920 | tf_op jit(solution)/shard_map/weights/pallas_call | solution.py:240
  66.4 0.3 collective-permute-done.3.far_ref
  66.6 0.7 %final.1 = (bf16[16,2048]{1,0:T(8,128)(2,1)}, f32[6,16]{1,0:T(8,128)}) custom-call(f32[16,2176]{1,0:T(8,128)S(1)} %get-tuple-element.17.own_ref, bf16[16,2176]{1,0:T(8,128)(2,1)S(1)} %collective-permute-done.3.far_ref), custom_call_target="tpu_custom_call" | custom-call | tf_op jit(solution)/shard_map/final/pallas_call | solution.py:266
  (5 shorter events, 0.0 us)
Async XLA Ops:
  0.6 36.2 %copy-start.1 = (bf16[1,704,2048]{2,1,0:T(8,128)(2,1)S(1)}, bf16[1,704,2048]{2,1,0:T(8,128)(2,1)}, u32[]{:S(2)}) copy-start(bf16[1,704,2048]{2,1,0:T(8,128)(2,1)} %r_3_.1) | copy-start | bytes 8650756
  0.6 1.0 %copy-start.2 = (bf16[16,2048]{1,0:T(8,128)(2,1)S(1)}, bf16[16,2048]{1,0:T(8,128)(2,1)}, u32[]{:S(2)}) copy-start(bf16[16,2048]{1,0:T(8,128)(2,1)} %x_hbm.1) | copy-start | bytes 196612
  1.6 0.8 %copy-start.3 = (bf16[16,2048]{1,0:T(8,128)(2,1)S(1)}, bf16[16,2048]{1,0:T(8,128)(2,1)}, u32[]{:S(2)}) copy-start(bf16[16,2048]{1,0:T(8,128)(2,1)} %dy_hbm.1) | copy-start | bytes 196612
  2.5 0.7 %copy-start.4 = (s32[16,6]{0,1:T(8,128)S(1)}, s32[16,6]{0,1:T(8,128)}, u32[]{:S(2)}) copy-start(s32[16,6]{0,1:T(8,128)} %param.8) | copy-start | bytes 1156
  3.2 0.7 %copy-start.5 = (bf16[16,6]{0,1:T(8,128)(2,1)S(1)}, bf16[16,6]{0,1:T(8,128)(2,1)}, u32[]{:S(2)}) copy-start(bf16[16,6]{0,1:T(8,128)(2,1)} %param.9) | copy-start | bytes 580
  4.1 8.8 %collective-permute-start = (bf16[16,4224]{1,0:T(8,128)(2,1)S(1)}, bf16[16,4224]{1,0:T(8,128)(2,1)S(1)}, u32[]{:S(2)}, u32[]{:S(2)}) collective-permute-start(bf16[16,4224]{1,0:T(8,128)(2,1)S(1)} %pack.1.r_1_.r_2_), channel_id=1, source_target_pairs={{0,6},{2,4},{4,2},{6,0},{1,7},{3,5},{5,3},{7,1},{8,14},{10,12},{12... | collective-permute-start | bytes 405512 | tf_op jit(solution)/shard_map/ppermute | solution.py:193
  34.1 2.7 %collective-permute-start.1 = (bf16[128,4224]{1,0:T(8,128)(2,1)S(1)}, bf16[128,4224]{1,0:T(8,128)(2,1)S(1)}, u32[]{:S(2)}, u32[]{:S(2)}) collective-permute-start(bf16[128,4224]{1,0:T(8,128)(2,1)S(1)} %bitcast.9), channel_id=1, source_target_pairs={{0,1},{1,0},{2,3},{3,2},{4,5},{5,4},{6,7},{7,6},{8,9},{9,8},{10,11... | collective-permute-start | bytes 3244040 | tf_op jit(solution)/shard_map/ppermute | solution.py:196
  36.8 2.6 %copy-start = (bf16[1,2,704,2048]{3,2,1,0:T(8,128)(2,1)S(1)}, bf16[1,2,704,2048]{3,2,1,0:T(8,128)(2,1)}, u32[]{:S(2)}) copy-start(bf16[1,2,704,2048]{3,2,1,0:T(8,128)(2,1)} %r_2_.1) | copy-start | bytes 17301508
  44.6 2.0 %collective-permute-start.2 = (bf16[128,2176]{1,0:T(8,128)(2,1)S(1)}, bf16[128,2176]{1,0:T(8,128)(2,1)S(1)}, u32[]{:S(2)}, u32[]{:S(2)}) collective-permute-start(bf16[128,2176]{1,0:T(8,128)(2,1)S(1)} %get-tuple-element.16), channel_id=1, source_target_pairs={{0,1},{1,0},{2,3},{3,2},{4,5},{5,4},{6,7},{7,6},{8,9},{9,8},{10,11... | collective-permute-start | bytes 1671176 | tf_op jit(solution)/shard_map/ppermute | solution.py:196
  60.5 6.2 %collective-permute-start.3 = (bf16[16,2176]{1,0:T(8,128)(2,1)S(1)}, bf16[16,2176]{1,0:T(8,128)(2,1)S(1)}, u32[]{:S(2)}, u32[]{:S(2)}) collective-permute-start(bf16[16,2176]{1,0:T(8,128)(2,1)S(1)} %get-tuple-element.18), channel_id=1, source_target_pairs={{0,6},{2,4},{4,2},{6,0},{1,7},{3,5},{5,3},{7,1},{8,14},{10,12},{12... | collective-permute-start | bytes 208904 | tf_op jit(solution)/shard_map/ppermute | solution.py:193

commit v3 on v2

--- a/solution.py
+++ b/solution.py
@@ -39,19 +39,31 @@
     return match, held
 
 
-def pack_kernel(x_hbm, dy_hbm, ids_ref, p_ref, out_ref, sems):
+def pack_kernel(x_hbm, dy_hbm, ids_hbm, p_hbm, out_ref, ids_ref, p_ref, sems):
     width, top = x_hbm.shape[1], ids_ref.shape[0]
+    small = [
+        pltpu.make_async_copy(ids_hbm, ids_ref, sems.at[2]),
+        pltpu.make_async_copy(p_hbm, p_ref, sems.at[3]),
+    ]
     copies = [
         pltpu.make_async_copy(x_hbm, out_ref.at[:, pl.ds(0, width)], sems.at[0]),
         pltpu.make_async_copy(dy_hbm, out_ref.at[:, pl.ds(width, width)], sems.at[1]),
     ]
-    for c in copies:
+    for c in small + copies:
         c.start()
+    for c in small:
+        c.wait()
     ids = ids_ref[...].astype(F32).astype(BF16)
     meta = dot(ids, lane_map(top, 0), 0, 0) + dot(p_ref[...], lane_map(top, top), 0, 0)
     out_ref[:, 2 * width :] = meta.astype(BF16)
     for c in copies:
         c.wait()
+
+
+def stage_kernel(src_hbm, out_ref, sem):
+    copy = pltpu.make_async_copy(src_hbm, out_ref, sem)
+    copy.start()
+    copy.wait()
 
 
 def select_kernel(top, capacity, half_ref, own_ref, far_ref, out_ref):
@@ -166,6 +178,7 @@
 VMEM = pl.BlockSpec(memory_space=pltpu.VMEM)
 SMEM = pl.BlockSpec(memory_space=pltpu.SMEM)
 ANY = pl.BlockSpec(memory_space=pl.ANY)
+HBM = pl.BlockSpec(memory_space=pltpu.HBM)
 
 
 def body(tokens, out_grads, route_ids, route_probs, w_gate_up, w_down):
@@ -199,13 +212,28 @@
     own = pl.pallas_call(
         pack_kernel,
         out_shape=sd((rows, 2 * width + LANES), BF16),
-        in_specs=[ANY, ANY, VMEM, VMEM],
+        in_specs=[HBM] * 4,
         out_specs=VMEM,
-        scratch_shapes=[pltpu.SemaphoreType.DMA((2,))],
-        compiler_params=params(4),
+        scratch_shapes=[
+            pltpu.VMEM((top, rows), jnp.int32),
+            pltpu.VMEM((top, rows), BF16),
+            pltpu.SemaphoreType.DMA((4,)),
+        ],
+        compiler_params=params(60),
         name="pack",
     )(tokens, out_grads, route_ids.T, route_probs.T)
     far = mirror(own)
+    staged = pl.pallas_call(
+        stage_kernel,
+        out_shape=sd(w_gate_up.shape, BF16),
+        in_specs=[HBM],
+        out_specs=VMEM,
+        scratch_shapes=[pltpu.SemaphoreType.DMA],
+        compiler_params=params(44),
+        cost_estimate=pl.CostEstimate(flops=0, bytes_accessed=8 * hidden * width, transcendentals=0),
+        name="stage",
+    )(w_gate_up)
+    far, staged = lax.optimization_barrier((far, staged))
     picked = pl.pallas_call(
         lambda *r: select_kernel(top, capacity, *r),
         out_shape=sd((slots, 2 * width + LANES), BF16),
@@ -225,7 +253,7 @@
         out_specs=[VMEM] * (parts + 3),
         compiler_params=big,
         name="expert",
-    )(*got, w_gate_up, w_down)
+    )(*got, staged, w_down)
     dx_parts, (gg, gu, act) = outs[:parts], outs[parts:]
     returned = [dx_parts[0]] + [across(dx_parts[i], -i) for i in range(1, parts)]
     summed = pl.pallas_call(

time: 67.7 us -> 63.3 us (0.935)
  local copies, waits for them, and re-layouts: 5.83 us -> 0.01 us
  Pallas kernels: 12 us -> 16 us
  waiting for transfers between devices: 8.48 us -> 5.98 us
    unnamed x12 -> x4, local copies, waits for them, and re-layouts: 5.83 us -> 0.01 us
    pallas_call x0 -> x1, Pallas kernels: none -> 2.68 us  [body(): pl.pallas_call(stage_kernel, out_shape=sd(w_gate_up.shape, BF16), in_spec...]
    ppermute x2, waiting for transfers between devices: 3.95 us -> 1.45 us  [mirror(): return lax.ppermute(v, ('zh', 'zl'), [(i, 3 - i) for i in range(4)])]
    pallas_call x1, Pallas kernels: 0.26 us -> 1.59 us  [body(): pl.pallas_call(pack_kernel, out_shape=sd((rows, 2 * width + LANES), BF16)...]
  transfers between devices with their start and end apart: 4 -> 4, of which waited for: 4 -> 4; matrix products, arithmetic and copies ran while one was open for 0% -> 0% of each run, Pallas kernels for 7% -> 11%
where the time goes in v3:
time: 63.3 us; the launch traced here: 63 us
  blocking collectives  33.6 us (53%)
  Pallas kernels  16 us (25%)
  starting transfers between devices  6.76 us (11%)
  waiting for transfers between devices  5.98 us (9%)
  between operations  0.69 us (1%)
    all_to_all x2, blocking collectives, within_half(): lax.all_to_all(v.reshape(devices, 2 * capacity, v.shape[1]), ('seq', 'zl'...  33.6 us
    ppermute x2, starting transfers between devices, mirror(): return lax.ppermute(v, ('zh', 'zl'), [(i, 3 - i) for i in range(4)])  6.56 us
    pallas_call x1, Pallas kernels, body(): pl.pallas_call(lambda *r: expert_kernel(parts, *r), out_shape=[sd((slots,...  5.15 us
    ppermute x2, waiting for transfers between devices, across(): lax.ppermute(v, 'slice', [(i, (i + step) % parts) for i in range(parts)])  4.53 us
    pallas_call x1, Pallas kernels, body(): pl.pallas_call(lambda *r: weights_kernel(parts, *r), out_shape=[sd(w_gate...  4.45 us
    pallas_call x1, Pallas kernels, body(): pl.pallas_call(stage_kernel, out_shape=sd(w_gate_up.shape, BF16), in_spec...  2.68 us
    pallas_call x1, Pallas kernels, body(): pl.pallas_call(pack_kernel, out_shape=sd((rows, 2 * width + LANES), BF16)...  1.59 us
    ppermute x2, waiting for transfers between devices, mirror(): return lax.ppermute(v, ('zh', 'zl'), [(i, 3 - i) for i in range(4)])  1.45 us
  transfers between devices with their start and end apart: 4, of which 4 were waited for; matrix products, arithmetic and copies ran while one was open for 0% of the time, Pallas kernels for 11%

profile of v3, /device:TPU:0, one launch (start us, length us, event | category | flops | bytes accessed | tf_op | source)
XLA Modules:
  0.0 63.0 jit_solution(12885417174202049579)
XLA Ops:
  0.6 1.6 %pack.1.r_1_.r_2_ = bf16[16,4224]{1,0:T(8,128)(2,1)} custom-call(bf16[16,2048]{1,0:T(8,128)(2,1)} %x_hbm.1, bf16[16,2048]{1,0:T(8,128)(2,1)} %dy_hbm.1, s32[6,16]{1,0:T(8,128)} %bitcast.14, bf16[6,16]{1,0:T(8,128)(2,1)} %bitcast.15), custom_call_target="tpu_custom_call" | custom-call | tf_op jit(solution)/shard_map/pack/pallas_call | solution.py:212
  2.2 5.1 %collective-permute-start = (bf16[16,4224]{1,0:T(8,128)(2,1)}, bf16[16,4224]{1,0:T(8,128)(2,1)S(1)}, u32[]{:S(2)}, u32[]{:S(2)}) collective-permute-start(bf16[16,4224]{1,0:T(8,128)(2,1)} %pack.1.r_1_.r_2_), channel_id=1, source_target_pairs={{0,6},{2,4},{4,2},{6,0},{1,7},{3,5},{5,3},{7,1},{8,14},{10,12},{12... | collective-permute-start | bytes 405512 | tf_op jit(solution)/shard_map/ppermute | solution.py:206
  7.3 0.0 copy-start.1
  7.3 2.7 %stage.1.r_2_ = bf16[1,2,704,2048]{3,2,1,0:T(8,128)(2,1)S(1)} custom-call(bf16[1,2,704,2048]{3,2,1,0:T(8,128)(2,1)} %src_hbm.1), custom_call_target="tpu_custom_call" | custom-call | bytes 11534336 | tf_op jit(solution)/shard_map/stage/pallas_call | solution.py:226
  10.0 0.0 copy-start
  10.0 1.2 %collective-permute-done.r_2_.r_3_ = bf16[16,4224]{1,0:T(8,128)(2,1)S(1)} collective-permute-done((bf16[16,4224]{1,0:T(8,128)(2,1)}, bf16[16,4224]{1,0:T(8,128)(2,1)S(1)}, u32[]{:S(2)}, u32[]{:S(2)}) %collective-permute-start) | collective-permute-done | bytes 135200 | tf_op jit(solution)/shard_map/ppermute | solution.py:206
  11.2 0.0 copy-done.1
  11.3 0.7 %select.1 = bf16[128,4224]{1,0:T(8,128)(2,1)S(1)} custom-call(s32[1]{0:T(128)} %bitcast.r_0_, bf16[16,4224]{1,0:T(8,128)(2,1)S(1)} %copy-done.1, bf16[16,4224]{1,0:T(8,128)(2,1)S(1)} %collective-permute-done.r_2_.r_3_), custom_call_target="tpu_custom_call" | custom-call | tf_op jit(solution)/shard_map/select/pallas_call | solution.py:237
  11.9 20.5 %all_to_all.10 = bf16[8,16,4224]{2,1,0:T(8,128)(2,1)S(1)} all-to-all(bf16[8,16,4224]{2,1,0:T(8,128)(2,1)S(1)} %bitcast.8), channel_id=1, replica_groups=mesh['seq'=4,'zh'=2,'zl'=2,'slice'=2] {'seq','zl'}, dimensions={0} | all-to-all | bytes 2162688 | tf_op jit(solution)/shard_map/all_to_all | solution.py:197
  32.4 0.0 collective-permute-start.1
  32.4 2.7 %collective-permute-done.1.r_1_ = bf16[128,4224]{1,0:T(8,128)(2,1)S(1)} collective-permute-done((bf16[128,4224]{1,0:T(8,128)(2,1)S(1)}, bf16[128,4224]{1,0:T(8,128)(2,1)S(1)}, u32[]{:S(2)}, u32[]{:S(2)}) %collective-permute-start.1) | collective-permute-done | bytes 1081376 | tf_op jit(solution)/shard_map/ppermute | solution.py:209
  35.1 0.0 copy-done
  35.1 5.1 %expert.1 = (bf16[128,2176]{1,0:T(8,128)(2,1)S(1)}, bf16[128,2176]{1,0:T(8,128)(2,1)S(1)}, bf16[256,704]{1,0:T(8,128)(2,1)S(1)}, bf16[256,704]{1,0:T(8,128)(2,1)S(1)}, bf16[256,704]{1,0:T(8,128)(2,1)S(1)}) custom-call(bf16[128,4224]{1,0:T(8,128)(2,1)S(1)} %bitcast.10, bf16[128,4224]{1,0:T(8,128)(2,1)S(1)} %collective-permute-done.1.r_1_, ...), custom_call_target="tpu_custom_call" | custom-call | tf_op jit(solution)/shard_map/expert/pallas_call | solution.py:249
  40.3 0.2 collective-permute-start.2
  40.5 1.8 %collective-permute-done.2.r_1_ = bf16[128,2176]{1,0:T(8,128)(2,1)S(1)} collective-permute-done((bf16[128,2176]{1,0:T(8,128)(2,1)S(1)}, bf16[128,2176]{1,0:T(8,128)(2,1)S(1)}, u32[]{:S(2)}, u32[]{:S(2)}) %collective-permute-start.2) | collective-permute-done | bytes 557088 | tf_op jit(solution)/shard_map/ppermute | solution.py:209
  42.3 0.1 add.1
  42.5 13.1 %all_to_all.11 = bf16[8,16,2176]{2,1,0:T(8,128)(2,1)S(1)} all-to-all(bf16[8,16,2176]{2,1,0:T(8,128)(2,1)S(1)} %bitcast.13), channel_id=1, replica_groups=mesh['seq'=4,'zh'=2,'zl'=2,'slice'=2] {'seq','zl'}, dimensions={0} | all-to-all | bytes 1114112 | tf_op jit(solution)/shard_map/all_to_all | solution.py:197
  55.5 0.6 combine.1
  56.2 1.4 %collective-permute-start.3 = (bf16[16,2176]{1,0:T(8,128)(2,1)S(1)}, bf16[16,2176]{1,0:T(8,128)(2,1)S(1)}, u32[]{:S(2)}, u32[]{:S(2)}) collective-permute-start(bf16[16,2176]{1,0:T(8,128)(2,1)S(1)} %get-tuple-element.22), channel_id=1, source_target_pairs={{0,6},{2,4},{4,2},{6,0},{1,7},{3,5},{5,3},{7,1},{8,14},{10,12},{12... | collective-permute-start | bytes 208904 | tf_op jit(solution)/shard_map/ppermute | solution.py:206
  57.6 4.5 %weights.1 = (bf16[1,2,704,2048]{3,2,1,0:T(8,128)(2,1)}, bf16[1,704,2048]{2,1,0:T(8,128)(2,1)}) custom-call(bf16[128,4224]{1,0:T(8,128)(2,1)S(1)} %bitcast.11, bf16[128,4224]{1,0:T(8,128)(2,1)S(1)} %collective-permute-done.1.r_1_, bf16[256,704]{1,0:T(8,128)(2,1)S(1)} %get-tuple-element.25.r_2_, bf16[256,704]{1,0:T(8,128)(2,1)S(1)} %get-tuple-element.26.r_3_, ...), custom_call_target="tpu_custom_call" | custom-call | flops 2214592512 | bytes 14417920 | tf_op jit(solution)/shard_map/weights/pallas_call | solution.py:268
  62.1 0.3 collective-permute-done.3.far_ref
  62.3 0.7 %final.1 = (bf16[16,2048]{1,0:T(8,128)(2,1)}, f32[6,16]{1,0:T(8,128)}) custom-call(f32[16,2176]{1,0:T(8,128)S(1)} %get-tuple-element.21.own_ref, bf16[16,2176]{1,0:T(8,128)(2,1)S(1)} %collective-permute-done.3.far_ref), custom_call_target="tpu_custom_call" | custom-call | tf_op jit(solution)/shard_map/final/pallas_call | solution.py:294
Async XLA Ops:
  2.2 9.0 %collective-permute-start = (bf16[16,4224]{1,0:T(8,128)(2,1)}, bf16[16,4224]{1,0:T(8,128)(2,1)S(1)}, u32[]{:S(2)}, u32[]{:S(2)}) collective-permute-start(bf16[16,4224]{1,0:T(8,128)(2,1)} %pack.1.r_1_.r_2_), channel_id=1, source_target_pairs={{0,6},{2,4},{4,2},{6,0},{1,7},{3,5},{5,3},{7,1},{8,14},{10,12},{12... | collective-permute-start | bytes 405512 | tf_op jit(solution)/shard_map/ppermute | solution.py:206
  7.3 3.9 %copy-start.1 = (bf16[16,4224]{1,0:T(8,128)(2,1)S(1)}, bf16[16,4224]{1,0:T(8,128)(2,1)}, u32[]{:S(2)}) copy-start(bf16[16,4224]{1,0:T(8,128)(2,1)} %pack.1.r_1_.r_2_) | copy-start | bytes 405508
  10.0 25.1 %copy-start = (bf16[1,704,2048]{2,1,0:T(8,128)(2,1)S(1)}, bf16[1,704,2048]{2,1,0:T(8,128)(2,1)}, u32[]{:S(2)}) copy-start(bf16[1,704,2048]{2,1,0:T(8,128)(2,1)} %r_3_.1) | copy-start | bytes 8650756
  32.4 2.7 %collective-permute-start.1 = (bf16[128,4224]{1,0:T(8,128)(2,1)S(1)}, bf16[128,4224]{1,0:T(8,128)(2,1)S(1)}, u32[]{:S(2)}, u32[]{:S(2)}) collective-permute-start(bf16[128,4224]{1,0:T(8,128)(2,1)S(1)} %bitcast.9), channel_id=1, source_target_pairs={{0,1},{1,0},{2,3},{3,2},{4,5},{5,4},{6,7},{7,6},{8,9},{9,8},{10,11... | collective-permute-start | bytes 3244040 | tf_op jit(solution)/shard_map/ppermute | solution.py:209
  40.3 2.0 %collective-permute-start.2 = (bf16[128,2176]{1,0:T(8,128)(2,1)S(1)}, bf16[128,2176]{1,0:T(8,128)(2,1)S(1)}, u32[]{:S(2)}, u32[]{:S(2)}) collective-permute-start(bf16[128,2176]{1,0:T(8,128)(2,1)S(1)} %get-tuple-element.20), channel_id=1, source_target_pairs={{0,1},{1,0},{2,3},{3,2},{4,5},{5,4},{6,7},{7,6},{8,9},{9,8},{10,11... | collective-permute-start | bytes 1671176 | tf_op jit(solution)/shard_map/ppermute | solution.py:209
  56.2 6.2 %collective-permute-start.3 = (bf16[16,2176]{1,0:T(8,128)(2,1)S(1)}, bf16[16,2176]{1,0:T(8,128)(2,1)S(1)}, u32[]{:S(2)}, u32[]{:S(2)}) collective-permute-start(bf16[16,2176]{1,0:T(8,128)(2,1)S(1)} %get-tuple-element.22), channel_id=1, source_target_pairs={{0,6},{2,4},{4,2},{6,0},{1,7},{3,5},{5,3},{7,1},{8,14},{10,12},{12... | collective-permute-start | bytes 208904 | tf_op jit(solution)/shard_map/ppermute | solution.py:206

commit v4 on v3

--- a/solution.py
+++ b/solution.py
@@ -171,6 +171,10 @@
     dp_ref[...] = dot(lane_map(top, 0), probs, 1, 1)
 
 
+def in_hbm(v):
+    return pltpu.with_memory_space_constraint(v, pltpu.HBM)
+
+
 def params(mib):
     return pltpu.CompilerParams(vmem_limit_bytes=mib * 1024 * 1024)
 
@@ -211,7 +215,7 @@
     half = lax.axis_index("zh").astype(jnp.int32).reshape(1)
     own = pl.pallas_call(
         pack_kernel,
-        out_shape=sd((rows, 2 * width + LANES), BF16),
+        out_shape=pltpu.VMEM((rows, 2 * width + LANES), BF16),
         in_specs=[HBM] * 4,
         out_specs=VMEM,
         scratch_shapes=[
@@ -219,20 +223,20 @@
             pltpu.VMEM((top, rows), BF16),
             pltpu.SemaphoreType.DMA((4,)),
         ],
-        compiler_params=params(60),
+        compiler_params=params(4),
         name="pack",
-    )(tokens, out_grads, route_ids.T, route_probs.T)
+    )(*[in_hbm(v) for v in (tokens, out_grads, route_ids.T, route_probs.T)])
     far = mirror(own)
     staged = pl.pallas_call(
         stage_kernel,
-        out_shape=sd(w_gate_up.shape, BF16),
+        out_shape=pltpu.VMEM(w_gate_up.shape, BF16),
         in_specs=[HBM],
         out_specs=VMEM,
         scratch_shapes=[pltpu.SemaphoreType.DMA],
-        compiler_params=params(44),
+        compiler_params=params(4),
         cost_estimate=pl.CostEstimate(flops=0, bytes_accessed=8 * hidden * width, transcendentals=0),
         name="stage",
-    )(w_gate_up)
+    )(in_hbm(w_gate_up))
     far, staged = lax.optimization_barrier((far, staged))
     picked = pl.pallas_call(
         lambda *r: select_kernel(top, capacity, *r),

time: 63.3 us -> 62.5 us (0.987)
  Pallas kernels: 16 us -> 15.3 us
    pallas_call x2, Pallas kernels: 4.27 us -> 3.58 us  [the longest x1 2.64 us: body(): pl.pallas_call(stage_kernel, out_shape=pltpu.VMEM(w_gate_up.shape, BF16),...]
where the time goes in v4:
time: 62.5 us; the launch traced here: 62.2 us
  blocking collectives  33.6 us (54%)
  Pallas kernels  15.3 us (24%)
  starting transfers between devices  6.77 us (11%)
  waiting for transfers between devices  5.81 us (9%)
  between operations  0.69 us (1%)
    all_to_all x2, blocking collectives, within_half(): lax.all_to_all(v.reshape(devices, 2 * capacity, v.shape[1]), ('seq', 'zl'...  33.6 us
    ppermute x2, starting transfers between devices, mirror(): return lax.ppermute(v, ('zh', 'zl'), [(i, 3 - i) for i in range(4)])  6.56 us
    pallas_call x1, Pallas kernels, body(): pl.pallas_call(lambda *r: expert_kernel(parts, *r), out_shape=[sd((slots,...  5.15 us
    ppermute x2, waiting for transfers between devices, across(): lax.ppermute(v, 'slice', [(i, (i + step) % parts) for i in range(parts)])  4.52 us
    pallas_call x1, Pallas kernels, body(): pl.pallas_call(lambda *r: weights_kernel(parts, *r), out_shape=[sd(w_gate...  4.44 us
    pallas_call x1, Pallas kernels, body(): pl.pallas_call(stage_kernel, out_shape=pltpu.VMEM(w_gate_up.shape, BF16),...  2.64 us
    ppermute x2, waiting for transfers between devices, mirror(): return lax.ppermute(v, ('zh', 'zl'), [(i, 3 - i) for i in range(4)])  1.28 us
  transfers between devices with their start and end apart: 4, of which 4 were waited for; matrix products, arithmetic and copies ran while one was open for 0% of the time, Pallas kernels for 11%

profile of v4, /device:TPU:0, one launch (start us, length us, event | category | flops | bytes accessed | tf_op | source)
XLA Modules:
  0.0 62.2 jit_solution(2702364612503518348)
XLA Ops:
  0.6 0.9 %pack.1.r_1_.r_2_ = bf16[16,4224]{1,0:T(8,128)(2,1)S(1)} custom-call(bf16[16,2048]{1,0:T(8,128)(2,1)} %x_hbm.1, bf16[16,2048]{1,0:T(8,128)(2,1)} %dy_hbm.1, s32[6,16]{1,0:T(8,128)} %bitcast.14, bf16[6,16]{1,0:T(8,128)(2,1)} %bitcast.15), custom_call_target="tpu_custom_call" | custom-call | tf_op jit(solution)/shard_map/pack/pallas_call | solution.py:216
  1.6 5.1 %collective-permute-start = (bf16[16,4224]{1,0:T(8,128)(2,1)S(1)}, bf16[16,4224]{1,0:T(8,128)(2,1)S(1)}, u32[]{:S(2)}, u32[]{:S(2)}) collective-permute-start(bf16[16,4224]{1,0:T(8,128)(2,1)S(1)} %pack.1.r_1_.r_2_), channel_id=1, source_target_pairs={{0,6},{2,4},{4,2},{6,0},{1,7},{3,5},{5,3},{7,1},{8,14},{10,12},{12... | collective-permute-start | bytes 405512 | tf_op jit(solution)/shard_map/ppermute | solution.py:210
  6.7 2.6 %stage.1.r_2_ = bf16[1,2,704,2048]{3,2,1,0:T(8,128)(2,1)S(1)} custom-call(bf16[1,2,704,2048]{3,2,1,0:T(8,128)(2,1)} %src_hbm.1), custom_call_target="tpu_custom_call" | custom-call | bytes 11534336 | tf_op jit(solution)/shard_map/stage/pallas_call | solution.py:230
  9.3 0.0 copy-start
  9.4 1.0 %collective-permute-done.r_2_.r_3_ = bf16[16,4224]{1,0:T(8,128)(2,1)S(1)} collective-permute-done((bf16[16,4224]{1,0:T(8,128)(2,1)S(1)}, bf16[16,4224]{1,0:T(8,128)(2,1)S(1)}, u32[]{:S(2)}, u32[]{:S(2)}) %collective-permute-start) | collective-permute-done | bytes 135200 | tf_op jit(solution)/shard_map/ppermute | solution.py:210
  10.4 0.7 %select.1 = bf16[128,4224]{1,0:T(8,128)(2,1)S(1)} custom-call(s32[1]{0:T(128)} %bitcast.r_0_, bf16[16,4224]{1,0:T(8,128)(2,1)S(1)} %pack.1.r_1_.r_2_, bf16[16,4224]{1,0:T(8,128)(2,1)S(1)} %collective-permute-done.r_2_.r_3_), custom_call_target="tpu_custom_call" | custom-call | tf_op jit(solution)/shard_map/select/pallas_call | solution.py:241
  11.1 20.5 %all_to_all.10 = bf16[8,16,4224]{2,1,0:T(8,128)(2,1)S(1)} all-to-all(bf16[8,16,4224]{2,1,0:T(8,128)(2,1)S(1)} %bitcast.8), channel_id=1, replica_groups=mesh['seq'=4,'zh'=2,'zl'=2,'slice'=2] {'seq','zl'}, dimensions={0} | all-to-all | bytes 2162688 | tf_op jit(solution)/shard_map/all_to_all | solution.py:201
  31.6 0.0 collective-permute-start.1
  31.6 2.7 %collective-permute-done.1.r_1_ = bf16[128,4224]{1,0:T(8,128)(2,1)S(1)} collective-permute-done((bf16[128,4224]{1,0:T(8,128)(2,1)S(1)}, bf16[128,4224]{1,0:T(8,128)(2,1)S(1)}, u32[]{:S(2)}, u32[]{:S(2)}) %collective-permute-start.1) | collective-permute-done | bytes 1081376 | tf_op jit(solution)/shard_map/ppermute | solution.py:213
  34.3 0.0 copy-done
  34.3 5.1 %expert.1 = (bf16[128,2176]{1,0:T(8,128)(2,1)S(1)}, bf16[128,2176]{1,0:T(8,128)(2,1)S(1)}, bf16[256,704]{1,0:T(8,128)(2,1)S(1)}, bf16[256,704]{1,0:T(8,128)(2,1)S(1)}, bf16[256,704]{1,0:T(8,128)(2,1)S(1)}) custom-call(bf16[128,4224]{1,0:T(8,128)(2,1)S(1)} %bitcast.10, bf16[128,4224]{1,0:T(8,128)(2,1)S(1)} %collective-permute-done.1.r_1_, ...), custom_call_target="tpu_custom_call" | custom-call | tf_op jit(solution)/shard_map/expert/pallas_call | solution.py:253
  39.4 0.2 collective-permute-start.2
  39.6 1.8 %collective-permute-done.2.r_1_ = bf16[128,2176]{1,0:T(8,128)(2,1)S(1)} collective-permute-done((bf16[128,2176]{1,0:T(8,128)(2,1)S(1)}, bf16[128,2176]{1,0:T(8,128)(2,1)S(1)}, u32[]{:S(2)}, u32[]{:S(2)}) %collective-permute-start.2) | collective-permute-done | bytes 557088 | tf_op jit(solution)/shard_map/ppermute | solution.py:213
  41.5 0.1 add.1
  41.6 13.1 %all_to_all.11 = bf16[8,16,2176]{2,1,0:T(8,128)(2,1)S(1)} all-to-all(bf16[8,16,2176]{2,1,0:T(8,128)(2,1)S(1)} %bitcast.13), channel_id=1, replica_groups=mesh['seq'=4,'zh'=2,'zl'=2,'slice'=2] {'seq','zl'}, dimensions={0} | all-to-all | bytes 1114112 | tf_op jit(solution)/shard_map/all_to_all | solution.py:201
  54.7 0.6 combine.1
  55.3 1.4 %collective-permute-start.3 = (bf16[16,2176]{1,0:T(8,128)(2,1)S(1)}, bf16[16,2176]{1,0:T(8,128)(2,1)S(1)}, u32[]{:S(2)}, u32[]{:S(2)}) collective-permute-start(bf16[16,2176]{1,0:T(8,128)(2,1)S(1)} %get-tuple-element.22), channel_id=1, source_target_pairs={{0,6},{2,4},{4,2},{6,0},{1,7},{3,5},{5,3},{7,1},{8,14},{10,12},{12... | collective-permute-start | bytes 208904 | tf_op jit(solution)/shard_map/ppermute | solution.py:210
  56.8 4.4 %weights.1 = (bf16[1,2,704,2048]{3,2,1,0:T(8,128)(2,1)}, bf16[1,704,2048]{2,1,0:T(8,128)(2,1)}) custom-call(bf16[128,4224]{1,0:T(8,128)(2,1)S(1)} %bitcast.11, bf16[128,4224]{1,0:T(8,128)(2,1)S(1)} %collective-permute-done.1.r_1_, bf16[256,704]{1,0:T(8,128)(2,1)S(1)} %get-tuple-element.25.r_2_, bf16[256,704]{1,0:T(8,128)(2,1)S(1)} %get-tuple-element.26.r_3_, ...), custom_call_target="tpu_custom_call" | custom-call | flops 2214592512 | bytes 14417920 | tf_op jit(solution)/shard_map/weights/pallas_call | solution.py:272
  61.2 0.3 collective-permute-done.3.far_ref
  61.5 0.7 %final.1 = (bf16[16,2048]{1,0:T(8,128)(2,1)}, f32[6,16]{1,0:T(8,128)}) custom-call(f32[16,2176]{1,0:T(8,128)S(1)} %get-tuple-element.21.own_ref, bf16[16,2176]{1,0:T(8,128)(2,1)S(1)} %collective-permute-done.3.far_ref), custom_call_target="tpu_custom_call" | custom-call | tf_op jit(solution)/shard_map/final/pallas_call | solution.py:298
Async XLA Ops:
  1.6 8.8 %collective-permute-start = (bf16[16,4224]{1,0:T(8,128)(2,1)S(1)}, bf16[16,4224]{1,0:T(8,128)(2,1)S(1)}, u32[]{:S(2)}, u32[]{:S(2)}) collective-permute-start(bf16[16,4224]{1,0:T(8,128)(2,1)S(1)} %pack.1.r_1_.r_2_), channel_id=1, source_target_pairs={{0,6},{2,4},{4,2},{6,0},{1,7},{3,5},{5,3},{7,1},{8,14},{10,12},{12... | collective-permute-start | bytes 405512 | tf_op jit(solution)/shard_map/ppermute | solution.py:210
  9.3 24.9 %copy-start = (bf16[1,704,2048]{2,1,0:T(8,128)(2,1)S(1)}, bf16[1,704,2048]{2,1,0:T(8,128)(2,1)}, u32[]{:S(2)}) copy-start(bf16[1,704,2048]{2,1,0:T(8,128)(2,1)} %r_3_.1) | copy-start | bytes 8650756
  31.6 2.7 %collective-permute-start.1 = (bf16[128,4224]{1,0:T(8,128)(2,1)S(1)}, bf16[128,4224]{1,0:T(8,128)(2,1)S(1)}, u32[]{:S(2)}, u32[]{:S(2)}) collective-permute-start(bf16[128,4224]{1,0:T(8,128)(2,1)S(1)} %bitcast.9), channel_id=1, source_target_pairs={{0,1},{1,0},{2,3},{3,2},{4,5},{5,4},{6,7},{7,6},{8,9},{9,8},{10,11... | collective-permute-start | bytes 3244040 | tf_op jit(solution)/shard_map/ppermute | solution.py:213
  39.4 2.0 %collective-permute-start.2 = (bf16[128,2176]{1,0:T(8,128)(2,1)S(1)}, bf16[128,2176]{1,0:T(8,128)(2,1)S(1)}, u32[]{:S(2)}, u32[]{:S(2)}) collective-permute-start(bf16[128,2176]{1,0:T(8,128)(2,1)S(1)} %get-tuple-element.20), channel_id=1, source_target_pairs={{0,1},{1,0},{2,3},{3,2},{4,5},{5,4},{6,7},{7,6},{8,9},{9,8},{10,11... | collective-permute-start | bytes 1671176 | tf_op jit(solution)/shard_map/ppermute | solution.py:213
  55.3 6.2 %collective-permute-start.3 = (bf16[16,2176]{1,0:T(8,128)(2,1)S(1)}, bf16[16,2176]{1,0:T(8,128)(2,1)S(1)}, u32[]{:S(2)}, u32[]{:S(2)}) collective-permute-start(bf16[16,2176]{1,0:T(8,128)(2,1)S(1)} %get-tuple-element.22), channel_id=1, source_target_pairs={{0,6},{2,4},{4,2},{6,0},{1,7},{3,5},{5,3},{7,1},{8,14},{10,12},{12... | collective-permute-start | bytes 208904 | tf_op jit(solution)/shard_map/ppermute | solution.py:210

commit v5 on v4

--- a/solution.py
+++ b/solution.py
@@ -39,24 +39,19 @@
     return match, held
 
 
-def pack_kernel(x_hbm, dy_hbm, ids_hbm, p_hbm, out_ref, ids_ref, p_ref, sems):
+def pack_kernel(x_hbm, dy_hbm, ids_hbm, out_ref, ids_ref, sems):
     width, top = x_hbm.shape[1], ids_ref.shape[0]
-    small = [
+    copies = [
         pltpu.make_async_copy(ids_hbm, ids_ref, sems.at[2]),
-        pltpu.make_async_copy(p_hbm, p_ref, sems.at[3]),
-    ]
-    copies = [
         pltpu.make_async_copy(x_hbm, out_ref.at[:, pl.ds(0, width)], sems.at[0]),
         pltpu.make_async_copy(dy_hbm, out_ref.at[:, pl.ds(width, width)], sems.at[1]),
     ]
-    for c in small + copies:
+    for c in copies:
         c.start()
-    for c in small:
-        c.wait()
+    copies[0].wait()
     ids = ids_ref[...].astype(F32).astype(BF16)
-    meta = dot(ids, lane_map(top, 0), 0, 0) + dot(p_ref[...], lane_map(top, top), 0, 0)
-    out_ref[:, 2 * width :] = meta.astype(BF16)
-    for c in copies:
+    out_ref[:, 2 * width :] = dot(ids, lane_map(top, 0), 0, 0).astype(BF16)
+    for c in copies[1:]:
         c.wait()
 
 
@@ -66,23 +61,22 @@
     copy.wait()
 
 
-def select_kernel(top, capacity, half_ref, own_ref, far_ref, out_ref):
-    slots, width = out_ref.shape[0], (out_ref.shape[1] - LANES) // 2
+def select_kernel(capacity, half_ref, own_ref, far_ref, own_p_ref, far_p_ref, out_ref):
+    slots, width, top = out_ref.shape[0], out_ref.shape[1] // 2, own_p_ref.shape[0]
     picks, weighted = [], []
-    for which, ref in enumerate((own_ref, far_ref)):
+    for which, (ref, p_ref) in enumerate(((own_ref, own_p_ref), (far_ref, far_p_ref))):
+        probs = dot(p_ref[...], lane_map(top, 0), 0, 0)
         meta = ref[:, 2 * width :].astype(F32)
         match, held = slot_table(meta, top, half_ref[0], which, capacity, slots)
         weight = jnp.zeros(held.shape, F32)
         for k in range(top):
-            weight = weight + jnp.where(match[k], meta[:, top + k : top + k + 1], 0.0)
+            weight = weight + jnp.where(match[k], probs[:, k : k + 1], 0.0)
         picks.append(held)
         weighted.append(held * weight)
-    pick = jnp.concatenate(picks, 0).astype(BF16)
-    rows = jnp.concatenate([own_ref[:, : 2 * width], far_ref[:, : 2 * width]], 0)
-    out_ref[:, : 2 * width] = dot(pick, rows, 0, 0).astype(BF16)
-    ones = jnp.ones((pick.shape[0], LANES), BF16)
-    weights = jnp.concatenate(weighted, 0).astype(BF16)
-    out_ref[:, 2 * width :] = dot(weights, ones, 0, 0).astype(BF16)
+    for i, mask in enumerate((picks, weighted)):
+        cut = slice(i * width, (i + 1) * width)
+        rows = jnp.concatenate([own_ref[:, cut], far_ref[:, cut]], 0)
+        out_ref[:, cut] = dot(jnp.concatenate(mask, 0).astype(BF16), rows, 0, 0).astype(BF16)
 
 
 def expert_kernel(parts, *refs):
@@ -93,8 +87,7 @@
     width = wd_ref.shape[2]
     slots = got[0].shape[0]
     xs = jnp.concatenate([r[:, :width] for r in got], 0)
-    dys = jnp.concatenate([r[:, width : 2 * width] for r in got], 0)
-    weight = jnp.concatenate([r[:, 2 * width :] for r in got], 0).astype(F32)[:, 0:1]
+    dys = jnp.concatenate([r[:, width:] for r in got], 0)
     gate = dot(xs, wgu_ref[0, 0], 1, 1)
     upper = dot(xs, wgu_ref[0, 1], 1, 1)
     err = dot(dys, wd_ref[0], 1, 1)
@@ -102,9 +95,8 @@
     silu = gate * sig
     act = silu * upper
     score = jnp.sum(err * act, axis=1, keepdims=True)
-    delta = weight * err
-    gg = (delta * upper * sig * (1.0 + gate * (1.0 - sig))).astype(BF16)
-    gu = (delta * silu).astype(BF16)
+    gg = (err * upper * sig * (1.0 + gate * (1.0 - sig))).astype(BF16)
+    gu = (err * silu).astype(BF16)
     gg_ref[...] = gg
     gu_ref[...] = gu
     act_ref[...] = act.astype(BF16)
@@ -118,26 +110,18 @@
 def weights_kernel(parts, *refs):
     got = refs[:parts]
     gg_ref, gu_ref, act_ref, dgu_hbm, dd_hbm, buf, sems = refs[parts:]
-    width = buf.shape[2]
-    copies = [
-        pltpu.make_async_copy(buf.at[0], dgu_hbm.at[0, 0], sems.at[0]),
-        pltpu.make_async_copy(buf.at[1], dgu_hbm.at[0, 1], sems.at[1]),
-        pltpu.make_async_copy(buf.at[2], dd_hbm.at[0], sems.at[2]),
-    ]
+    hidden, width = buf.shape[1:]
     xs = jnp.concatenate([r[:, :width] for r in got], 0)
-    buf[0] = dot(gg_ref[...], xs, 0, 0).astype(BF16)
-    copies[0].start()
-    buf[1] = dot(gu_ref[...], xs, 0, 0).astype(BF16)
-    copies[1].start()
-    scaled = jnp.concatenate(
-        [
-            (r[:, 2 * width : 2 * width + 1].astype(F32) * r[:, width : 2 * width].astype(F32)).astype(BF16)
-            for r in got
-        ],
-        0,
-    )
-    buf[2] = dot(act_ref[...], scaled, 0, 0).astype(BF16)
-    copies[2].start()
+    dys = jnp.concatenate([r[:, width:] for r in got], 0)
+    outs = ((gg_ref, xs, dgu_hbm.at[0, 0]), (gu_ref, xs, dgu_hbm.at[0, 1]), (act_ref, dys, dd_hbm.at[0]))
+    copies = []
+    for i, (lhs_ref, rhs, out) in enumerate(outs):
+        for j, start in enumerate(range(0, hidden, LANES)):
+            size = min(LANES, hidden - start)
+            buf[i, start : start + size, :] = dot(lhs_ref[:, start : start + size], rhs, 0, 0).astype(BF16)
+            cut = pl.ds(start, size)
+            copies.append(pltpu.make_async_copy(buf.at[i, cut], out.at[cut], sems.at[i, j]))
+            copies[-1].start()
     for c in copies:
         c.wait()
 
@@ -164,11 +148,11 @@
         out_ref[:, width:] = probs.astype(out_ref.dtype)
 
 
-def final_kernel(own_ref, far_ref, dx_ref, dp_ref):
+def final_kernel(own_ref, far_ref, p_ref, dx_ref, dp_ref):
     width, top = dx_ref.shape[1], dp_ref.shape[0]
     dx_ref[...] = (own_ref[:, :width] + far_ref[:, :width].astype(F32)).astype(BF16)
     probs = (own_ref[:, width:] + far_ref[:, width:].astype(F32)).astype(BF16)
-    dp_ref[...] = dot(lane_map(top, 0), probs, 1, 1)
+    dp_ref[...] = dot(lane_map(top, 0), probs, 1, 1) / p_ref[...].astype(F32)
 
 
 def in_hbm(v):
@@ -216,17 +200,13 @@
     own = pl.pallas_call(
         pack_kernel,
         out_shape=pltpu.VMEM((rows, 2 * width + LANES), BF16),
-        in_specs=[HBM] * 4,
+        in_specs=[HBM] * 3,
         out_specs=VMEM,
-        scratch_shapes=[
-            pltpu.VMEM((top, rows), jnp.int32),
-            pltpu.VMEM((top, rows), BF16),
-            pltpu.SemaphoreType.DMA((4,)),
-        ],
+        scratch_shapes=[pltpu.VMEM((top, rows), jnp.int32), pltpu.SemaphoreType.DMA((3,))],
         compiler_params=params(4),
         name="pack",
-    )(*[in_hbm(v) for v in (tokens, out_grads, route_ids.T, route_probs.T)])
-    far = mirror(own)
+    )(*[in_hbm(v) for v in (tokens, out_grads, route_ids.T)])
+    far, own_p, far_p = mirror(own), route_probs.T, mirror(route_probs).T
     staged = pl.pallas_call(
         stage_kernel,
         out_shape=pltpu.VMEM(w_gate_up.shape, BF16),
@@ -239,13 +219,13 @@
     )(in_hbm(w_gate_up))
     far, staged = lax.optimization_barrier((far, staged))
     picked = pl.pallas_call(
-        lambda *r: select_kernel(top, capacity, *r),
-        out_shape=sd((slots, 2 * width + LANES), BF16),
-        in_specs=[SMEM, VMEM, VMEM],
+        lambda *r: select_kernel(capacity, *r),
+        out_shape=sd((slots, 2 * width), BF16),
+        in_specs=[SMEM] + [VMEM] * 4,
         out_specs=VMEM,
         compiler_params=params(8),
         name="select",
-    )(half, own, far)
+    )(half, own, far, own_p, far_p)
     mine = within_half(picked)
     got = [mine] + [across(mine, i) for i in range(1, parts)]
 
@@ -276,7 +256,7 @@
         out_specs=[ANY] * 2,
         scratch_shapes=[
             pltpu.VMEM((3, hidden, width), BF16),
-            pltpu.SemaphoreType.DMA((3,)),
+            pltpu.SemaphoreType.DMA((3, -(-hidden // LANES))),
         ],
         compiler_params=params(40),
         cost_estimate=pl.CostEstimate(
@@ -298,11 +278,11 @@
     grad_tokens, grad_probs = pl.pallas_call(
         final_kernel,
         out_shape=[sd((rows, width), BF16), sd((top, rows), F32)],
-        in_specs=[VMEM] * 2,
+        in_specs=[VMEM] * 3,
         out_specs=[VMEM] * 2,
         compiler_params=params(4),
         name="final",
-    )(own_sum, home)
+    )(own_sum, home, own_p)
     return grad_tokens, grad_probs.T, grad_gu, grad_down
 
 

time: 62.5 us -> 62.1 us (level)
  waiting for transfers between devices: 5.81 us -> 8.18 us
  blocking collectives: 33.6 us -> 31.3 us
    ppermute x2 -> x3, waiting for transfers between devices: 1.28 us -> 3.7 us  [mirror(): return lax.ppermute(v, ('zh', 'zl'), [(i, 3 - i) for i in range(4)])]
    all_to_all x2, blocking collectives: 33.6 us -> 31.3 us  [within_half(): lax.all_to_all(v.reshape(devices, 2 * capacity, v.shape[1]), ('seq', 'zl'...]
    ppermute x2 -> x3, starting transfers between devices: 6.56 us -> 6.61 us  [mirror(): return lax.ppermute(v, ('zh', 'zl'), [(i, 3 - i) for i in range(4)])]
  transfers between devices with their start and end apart: 4 -> 5, of which waited for: 4 -> 5; matrix products, arithmetic and copies ran while one was open for 0% -> 0% of each run, Pallas kernels for 11% -> 11%
where the time goes in v5:
time: 62.1 us; the launch traced here: 61.8 us
  blocking collectives  31.3 us (50%)
  Pallas kernels  14.8 us (24%)
  waiting for transfers between devices  8.18 us (13%)
  starting transfers between devices  6.81 us (11%)
  between operations  0.68 us (1%)
    all_to_all x2, blocking collectives, within_half(): lax.all_to_all(v.reshape(devices, 2 * capacity, v.shape[1]), ('seq', 'zl'...  31.3 us
    ppermute x3, starting transfers between devices, mirror(): return lax.ppermute(v, ('zh', 'zl'), [(i, 3 - i) for i in range(4)])  6.61 us
    pallas_call x1, Pallas kernels, body(): pl.pallas_call(lambda *r: expert_kernel(parts, *r), out_shape=[sd((slots,...  5.14 us
    ppermute x2, waiting for transfers between devices, across(): lax.ppermute(v, 'slice', [(i, (i + step) % parts) for i in range(parts)])  4.48 us
    pallas_call x1, Pallas kernels, body(): pl.pallas_call(lambda *r: weights_kernel(parts, *r), out_shape=[sd(w_gate...  3.84 us
    ppermute x3, waiting for transfers between devices, mirror(): return lax.ppermute(v, ('zh', 'zl'), [(i, 3 - i) for i in range(4)])  3.7 us
    pallas_call x1, Pallas kernels, body(): pl.pallas_call(stage_kernel, out_shape=pltpu.VMEM(w_gate_up.shape, BF16),...  2.79 us
  transfers between devices with their start and end apart: 5, of which 5 were waited for; matrix products, arithmetic and copies ran while one was open for 0% of the time, Pallas kernels for 11%

profile of v5, /device:TPU:0, one launch (start us, length us, event | category | flops | bytes accessed | tf_op | source)
XLA Modules:
  0.0 61.8 jit_solution(9843059367280924071)
XLA Ops:
  0.6 0.9 %pack.1.r_1_.r_2_ = bf16[16,4224]{1,0:T(8,128)(2,1)S(1)} custom-call(bf16[16,2048]{1,0:T(8,128)(2,1)} %x_hbm.1, bf16[16,2048]{1,0:T(8,128)(2,1)} %dy_hbm.1, s32[6,16]{1,0:T(8,128)} %bitcast.18), custom_call_target="tpu_custom_call" | custom-call | tf_op jit(solution)/shard_map/pack/pallas_call | solution.py:200
  1.6 5.1 %collective-permute-start = (bf16[16,4224]{1,0:T(8,128)(2,1)S(1)}, bf16[16,4224]{1,0:T(8,128)(2,1)S(1)}, u32[]{:S(2)}, u32[]{:S(2)}) collective-permute-start(bf16[16,4224]{1,0:T(8,128)(2,1)S(1)} %pack.1.r_1_.r_2_), channel_id=1, source_target_pairs={{0,6},{2,4},{4,2},{6,0},{1,7},{3,5},{5,3},{7,1},{8,14},{10,12},{12... | collective-permute-start | bytes 405512 | tf_op jit(solution)/shard_map/ppermute | solution.py:194
  6.7 0.1 collective-permute-start.1
  6.7 0.0 copy-start.1
  6.7 0.0 copy-start
  6.8 2.8 %stage.1.r_2_ = bf16[1,2,704,2048]{3,2,1,0:T(8,128)(2,1)S(1)} custom-call(bf16[1,2,704,2048]{3,2,1,0:T(8,128)(2,1)} %src_hbm.1), custom_call_target="tpu_custom_call" | custom-call | bytes 11534336 | tf_op jit(solution)/shard_map/stage/pallas_call | solution.py:210
  9.6 0.8 %collective-permute-done.r_2_.r_3_ = bf16[16,4224]{1,0:T(8,128)(2,1)S(1)} collective-permute-done((bf16[16,4224]{1,0:T(8,128)(2,1)S(1)}, bf16[16,4224]{1,0:T(8,128)(2,1)S(1)}, u32[]{:S(2)}, u32[]{:S(2)}) %collective-permute-start) | collective-permute-done | bytes 135200 | tf_op jit(solution)/shard_map/ppermute | solution.py:194
  10.4 2.0 %collective-permute-done.1 = bf16[16,6]{0,1:T(8,128)(2,1)S(1)} collective-permute-done((bf16[16,6]{0,1:T(8,128)(2,1)}, bf16[16,6]{0,1:T(8,128)(2,1)S(1)}, u32[]{:S(2)}, u32[]{:S(2)}) %collective-permute-start.1) | collective-permute-done | bytes 224 | tf_op jit(solution)/shard_map/ppermute | solution.py:194
  12.4 0.0 copy-done.1
  12.4 0.7 %select.1 = bf16[128,4096]{1,0:T(8,128)(2,1)S(1)} custom-call(s32[1]{0:T(128)} %bitcast.r_0_, bf16[16,4224]{1,0:T(8,128)(2,1)S(1)} %pack.1.r_1_.r_2_, bf16[16,4224]{1,0:T(8,128)(2,1)S(1)} %collective-permute-done.r_2_.r_3_, bf16[6,16]{1,0:T(8,128)(2,1)S(1)} %bitcast.15, bf16[6,16]{1,0:T(8,128)(2,1)S(1)} %bitcast.17), custom_call_target="tpu_custom_call" | custom-call | tf_op jit(solution)/shard_map/select/pallas_call | solution.py:221
  13.1 18.2 %all_to_all.10 = bf16[8,16,4096]{2,1,0:T(8,128)(2,1)S(1)} all-to-all(bf16[8,16,4096]{2,1,0:T(8,128)(2,1)S(1)} %bitcast.9), channel_id=1, replica_groups=mesh['seq'=4,'zh'=2,'zl'=2,'slice'=2] {'seq','zl'}, dimensions={0} | all-to-all | bytes 2097152 | tf_op jit(solution)/shard_map/all_to_all | solution.py:185
  31.3 0.0 collective-permute-start.2
  31.3 2.7 %collective-permute-done.2.r_1_ = bf16[128,4096]{1,0:T(8,128)(2,1)S(1)} collective-permute-done((bf16[128,4096]{1,0:T(8,128)(2,1)S(1)}, bf16[128,4096]{1,0:T(8,128)(2,1)S(1)}, u32[]{:S(2)}, u32[]{:S(2)}) %collective-permute-start.2) | collective-permute-done | bytes 1048608 | tf_op jit(solution)/shard_map/ppermute | solution.py:197
  33.9 0.0 copy-done
  33.9 5.1 %expert.1 = (bf16[128,2176]{1,0:T(8,128)(2,1)S(1)}, bf16[128,2176]{1,0:T(8,128)(2,1)S(1)}, bf16[256,704]{1,0:T(8,128)(2,1)S(1)}, bf16[256,704]{1,0:T(8,128)(2,1)S(1)}, bf16[256,704]{1,0:T(8,128)(2,1)S(1)}) custom-call(bf16[128,4096]{1,0:T(8,128)(2,1)S(1)} %bitcast.11, bf16[128,4096]{1,0:T(8,128)(2,1)S(1)} %collective-permute-done.2.r_1_, ...), custom_call_target="tpu_custom_call" | custom-call | tf_op jit(solution)/shard_map/expert/pallas_call | solution.py:233
  39.1 0.2 collective-permute-start.3
  39.3 1.8 %collective-permute-done.3.r_1_ = bf16[128,2176]{1,0:T(8,128)(2,1)S(1)} collective-permute-done((bf16[128,2176]{1,0:T(8,128)(2,1)S(1)}, bf16[128,2176]{1,0:T(8,128)(2,1)S(1)}, u32[]{:S(2)}, u32[]{:S(2)}) %collective-permute-start.3) | collective-permute-done | bytes 557088 | tf_op jit(solution)/shard_map/ppermute | solution.py:197
  41.1 0.1 add.1
  41.2 13.1 %all_to_all.11 = bf16[8,16,2176]{2,1,0:T(8,128)(2,1)S(1)} all-to-all(bf16[8,16,2176]{2,1,0:T(8,128)(2,1)S(1)} %bitcast.14), channel_id=1, replica_groups=mesh['seq'=4,'zh'=2,'zl'=2,'slice'=2] {'seq','zl'}, dimensions={0} | all-to-all | bytes 1114112 | tf_op jit(solution)/shard_map/all_to_all | solution.py:185
  54.3 0.6 %combine.1 = (f32[16,2176]{1,0:T(8,128)S(1)}, bf16[16,2176]{1,0:T(8,128)(2,1)S(1)}) custom-call(s32[1]{0:T(128)} %bitcast.r_0_, bf16[128,2176]{1,0:T(8,128)(2,1)S(1)} %bitcast.13, bf16[16,4224]{1,0:T(8,128)(2,1)S(1)} %pack.1.r_1_.r_2_, bf16[16,4224]{1,0:T(8,128)(2,1)S(1)} %collective-permute-done.r_2_.r_3_), custom_call_target="tpu_custom_call" | custom-call | tf_op jit(solution)/shard_map/combine/pallas_call | solution.py:269
  55.0 1.4 %collective-permute-start.4 = (bf16[16,2176]{1,0:T(8,128)(2,1)S(1)}, bf16[16,2176]{1,0:T(8,128)(2,1)S(1)}, u32[]{:S(2)}, u32[]{:S(2)}) collective-permute-start(bf16[16,2176]{1,0:T(8,128)(2,1)S(1)} %get-tuple-element.22), channel_id=1, source_target_pairs={{0,6},{2,4},{4,2},{6,0},{1,7},{3,5},{5,3},{7,1},{8,14},{10,12},{12... | collective-permute-start | bytes 208904 | tf_op jit(solution)/shard_map/ppermute | solution.py:194
  56.4 3.8 %weights.1 = (bf16[1,2,704,2048]{3,2,1,0:T(8,128)(2,1)}, bf16[1,704,2048]{2,1,0:T(8,128)(2,1)}) custom-call(bf16[128,4096]{1,0:T(8,128)(2,1)S(1)} %bitcast.12, bf16[128,4096]{1,0:T(8,128)(2,1)S(1)} %collective-permute-done.2.r_1_, bf16[256,704]{1,0:T(8,128)(2,1)S(1)} %get-tuple-element.25.r_2_, bf16[256,704]{1,0:T(8,128)(2,1)S(1)} %get-tuple-element.26.r_3_, ...), custom_call_target="tpu_custom_call" | custom-call | flops 2214592512 | bytes 14417920 | tf_op jit(solution)/shard_map/weights/pallas_call | solution.py:252
  60.2 0.9 %collective-permute-done.4.far_ref = bf16[16,2176]{1,0:T(8,128)(2,1)S(1)} collective-permute-done((bf16[16,2176]{1,0:T(8,128)(2,1)S(1)}, bf16[16,2176]{1,0:T(8,128)(2,1)S(1)}, u32[]{:S(2)}, u32[]{:S(2)}) %collective-permute-start.4) | collective-permute-done | bytes 69664 | tf_op jit(solution)/shard_map/ppermute | solution.py:194
  61.1 0.7 %final.1 = (bf16[16,2048]{1,0:T(8,128)(2,1)}, f32[6,16]{1,0:T(8,128)}) custom-call(f32[16,2176]{1,0:T(8,128)S(1)} %get-tuple-element.21.own_ref, bf16[16,2176]{1,0:T(8,128)(2,1)S(1)} %collective-permute-done.4.far_ref, bf16[6,16]{1,0:T(8,128)(2,1)S(1)} %bitcast.16), custom_call_target="tpu_custom_call" | custom-call | tf_op jit(solution)/shard_map/final/pallas_call | solution.py:278
Async XLA Ops:
  1.6 8.8 %collective-permute-start = (bf16[16,4224]{1,0:T(8,128)(2,1)S(1)}, bf16[16,4224]{1,0:T(8,128)(2,1)S(1)}, u32[]{:S(2)}, u32[]{:S(2)}) collective-permute-start(bf16[16,4224]{1,0:T(8,128)(2,1)S(1)} %pack.1.r_1_.r_2_), channel_id=1, source_target_pairs={{0,6},{2,4},{4,2},{6,0},{1,7},{3,5},{5,3},{7,1},{8,14},{10,12},{12... | collective-permute-start | bytes 405512 | tf_op jit(solution)/shard_map/ppermute | solution.py:194
  6.7 5.7 %collective-permute-start.1 = (bf16[16,6]{0,1:T(8,128)(2,1)}, bf16[16,6]{0,1:T(8,128)(2,1)S(1)}, u32[]{:S(2)}, u32[]{:S(2)}) collective-permute-start(bf16[16,6]{0,1:T(8,128)(2,1)} %param.9), channel_id=1, source_target_pairs={{0,6},{2,4},{4,2},{6,0},{1,7},{3,5},{5,3},{7,1},{8,14},{10,12},{12... | collective-permute-start | bytes 584 | tf_op jit(solution)/shard_map/ppermute | solution.py:194
  6.7 5.6 %copy-start.1 = (bf16[16,6]{0,1:T(8,128)(2,1)S(1)}, bf16[16,6]{0,1:T(8,128)(2,1)}, u32[]{:S(2)}) copy-start(bf16[16,6]{0,1:T(8,128)(2,1)} %param.9) | copy-start | bytes 580
  6.7 27.2 %copy-start = (bf16[1,704,2048]{2,1,0:T(8,128)(2,1)S(1)}, bf16[1,704,2048]{2,1,0:T(8,128)(2,1)}, u32[]{:S(2)}) copy-start(bf16[1,704,2048]{2,1,0:T(8,128)(2,1)} %r_3_.1) | copy-start | bytes 8650756
  31.3 2.7 %collective-permute-start.2 = (bf16[128,4096]{1,0:T(8,128)(2,1)S(1)}, bf16[128,4096]{1,0:T(8,128)(2,1)S(1)}, u32[]{:S(2)}, u32[]{:S(2)}) collective-permute-start(bf16[128,4096]{1,0:T(8,128)(2,1)S(1)} %bitcast.10), channel_id=1, source_target_pairs={{0,1},{1,0},{2,3},{3,2},{4,5},{5,4},{6,7},{7,6},{8,9},{9,8},{10,11... | collective-permute-start | bytes 3145736 | tf_op jit(solution)/shard_map/ppermute | solution.py:197
  39.1 2.0 %collective-permute-start.3 = (bf16[128,2176]{1,0:T(8,128)(2,1)S(1)}, bf16[128,2176]{1,0:T(8,128)(2,1)S(1)}, u32[]{:S(2)}, u32[]{:S(2)}) collective-permute-start(bf16[128,2176]{1,0:T(8,128)(2,1)S(1)} %get-tuple-element.20), channel_id=1, source_target_pairs={{0,1},{1,0},{2,3},{3,2},{4,5},{5,4},{6,7},{7,6},{8,9},{9,8},{10,11... | collective-permute-start | bytes 1671176 | tf_op jit(solution)/shard_map/ppermute | solution.py:197
  55.0 6.2 %collective-permute-start.4 = (bf16[16,2176]{1,0:T(8,128)(2,1)S(1)}, bf16[16,2176]{1,0:T(8,128)(2,1)S(1)}, u32[]{:S(2)}, u32[]{:S(2)}) collective-permute-start(bf16[16,2176]{1,0:T(8,128)(2,1)S(1)} %get-tuple-element.22), channel_id=1, source_target_pairs={{0,6},{2,4},{4,2},{6,0},{1,7},{3,5},{5,3},{7,1},{8,14},{10,12},{12... | collective-permute-start | bytes 208904 | tf_op jit(solution)/shard_map/ppermute | solution.py:194

commit v6 on v4

--- a/solution.py
+++ b/solution.py
@@ -20,23 +20,17 @@
     return (lane == row + start).astype(BF16)
 
 
-def slot_table(meta, top, upper_half, which, capacity, slots):
+def held_slots(meta, top, expert, place):
     rows = meta.shape[0]
-    lane = lax.broadcasted_iota(jnp.int32, (rows, slots), 1)
-    device = lane // (2 * capacity)
-    expert = ((device // 2) * 4 + upper_half * 2 + device % 2).astype(F32)
-    mine = (lane // capacity) % 2 == which
-    place = (lane % capacity).astype(F32)
     match = [meta[:, k : k + 1] == expert for k in range(top)]
-    named = jnp.zeros((rows, slots), F32)
+    named = jnp.zeros(expert.shape, F32)
     for m in match:
         named = named + m.astype(F32)
     earlier = lax.broadcasted_iota(jnp.int32, (rows, rows), 1) < lax.broadcasted_iota(
         jnp.int32, (rows, rows), 0
     )
     rank = dot(earlier.astype(BF16), named.astype(BF16), 1, 0)
-    held = jnp.where(mine & (rank == place), named, 0.0)
-    return match, held
+    return match, jnp.where(rank == place, named, 0.0)
 
 
 def pack_kernel(x_hbm, dy_hbm, ids_hbm, p_hbm, out_ref, ids_ref, p_ref, sems):
@@ -66,32 +60,38 @@
     copy.wait()
 
 
-def select_kernel(top, capacity, half_ref, own_ref, far_ref, out_ref):
-    slots, width = out_ref.shape[0], (out_ref.shape[1] - LANES) // 2
+def select_kernel(top, capacity, half_ref, me_ref, first_ref, second_ref, *out_refs):
+    width, size = (first_ref.shape[1] - LANES) // 2, 2 * capacity
+    lane = lax.broadcasted_iota(jnp.int32, (first_ref.shape[0], len(out_refs) * size), 1)
+    plane = (me_ref[0] // 2) ^ (lane // size)
+    expert = (plane * 4 + half_ref[0] * 2 + me_ref[0] % 2).astype(F32)
+    place = (lane % capacity).astype(F32)
     picks, weighted = [], []
-    for which, ref in enumerate((own_ref, far_ref)):
+    for which, ref in enumerate((first_ref, second_ref)):
         meta = ref[:, 2 * width :].astype(F32)
-        match, held = slot_table(meta, top, half_ref[0], which, capacity, slots)
+        match, held = held_slots(meta, top, expert, place)
+        held = jnp.where((lane // capacity) % 2 == which, held, 0.0)
         weight = jnp.zeros(held.shape, F32)
         for k in range(top):
             weight = weight + jnp.where(match[k], meta[:, top + k : top + k + 1], 0.0)
         picks.append(held)
         weighted.append(held * weight)
     pick = jnp.concatenate(picks, 0).astype(BF16)
-    rows = jnp.concatenate([own_ref[:, : 2 * width], far_ref[:, : 2 * width]], 0)
-    out_ref[:, : 2 * width] = dot(pick, rows, 0, 0).astype(BF16)
+    rows = jnp.concatenate([first_ref[:, : 2 * width], second_ref[:, : 2 * width]], 0)
+    rows = dot(pick, rows, 0, 0).astype(BF16)
     ones = jnp.ones((pick.shape[0], LANES), BF16)
-    weights = jnp.concatenate(weighted, 0).astype(BF16)
-    out_ref[:, 2 * width :] = dot(weights, ones, 0, 0).astype(BF16)
-
-
-def expert_kernel(parts, *refs):
-    got = refs[:parts]
-    wgu_ref, wd_ref = refs[parts : parts + 2]
-    dx_out = refs[parts + 2 : 2 * parts + 2]
-    gg_ref, gu_ref, act_ref = refs[2 * parts + 2 :]
-    width = wd_ref.shape[2]
-    slots = got[0].shape[0]
+    weight = dot(jnp.concatenate(weighted, 0).astype(BF16), ones, 0, 0).astype(BF16)
+    for i, out_ref in enumerate(out_refs):
+        out_ref[:, : 2 * width] = rows[i * size : (i + 1) * size]
+        out_ref[:, 2 * width :] = weight[i * size : (i + 1) * size]
+
+
+def expert_kernel(parts, pieces, *refs):
+    got = refs[:pieces]
+    wgu_ref, wd_ref = refs[pieces : pieces + 2]
+    dx_out = refs[pieces + 2 : pieces + 2 + parts]
+    gg_ref, gu_ref, act_ref = refs[pieces + 2 + parts :]
+    width, slots = wd_ref.shape[2], dx_out[0].shape[0]
     xs = jnp.concatenate([r[:, :width] for r in got], 0)
     dys = jnp.concatenate([r[:, width : 2 * width] for r in got], 0)
     weight = jnp.concatenate([r[:, 2 * width :] for r in got], 0).astype(F32)[:, 0:1]
@@ -118,43 +118,48 @@
 def weights_kernel(parts, *refs):
     got = refs[:parts]
     gg_ref, gu_ref, act_ref, dgu_hbm, dd_hbm, buf, sems = refs[parts:]
-    width = buf.shape[2]
-    copies = [
-        pltpu.make_async_copy(buf.at[0], dgu_hbm.at[0, 0], sems.at[0]),
-        pltpu.make_async_copy(buf.at[1], dgu_hbm.at[0, 1], sems.at[1]),
-        pltpu.make_async_copy(buf.at[2], dd_hbm.at[0], sems.at[2]),
-    ]
+    hidden, width = buf.shape[1:]
     xs = jnp.concatenate([r[:, :width] for r in got], 0)
-    buf[0] = dot(gg_ref[...], xs, 0, 0).astype(BF16)
-    copies[0].start()
-    buf[1] = dot(gu_ref[...], xs, 0, 0).astype(BF16)
-    copies[1].start()
-    scaled = jnp.concatenate(
-        [
-            (r[:, 2 * width : 2 * width + 1].astype(F32) * r[:, width : 2 * width].astype(F32)).astype(BF16)
-            for r in got
-        ],
-        0,
-    )
-    buf[2] = dot(act_ref[...], scaled, 0, 0).astype(BF16)
-    copies[2].start()
+    weight = jnp.concatenate([r[:, 2 * width :] for r in got], 0).astype(F32)[:, 0:1]
+    dys = jnp.concatenate([r[:, width : 2 * width] for r in got], 0)
+    scaled = (weight * dys.astype(F32)).astype(BF16)
+    outs = ((gg_ref, xs, dgu_hbm.at[0, 0]), (gu_ref, xs, dgu_hbm.at[0, 1]), (act_ref, scaled, dd_hbm.at[0]))
+    copies = []
+    for i, (lhs_ref, rhs, out) in enumerate(outs):
+        for j, start in enumerate(range(0, hidden, LANES)):
+            size = min(LANES, hidden - start)
+            buf[i, start : start + size, :] = dot(lhs_ref[:, start : start + size], rhs, 0, 0).astype(BF16)
+            cut = pl.ds(start, size)
+            copies.append(pltpu.make_async_copy(buf.at[i, cut], out.at[cut], sems.at[i, j]))
+            copies[-1].start()
     for c in copies:
         c.wait()
 
 
-def add_kernel(parts, *refs):
+def add_kernel(capacity, me_ref, *refs):
+    out_ref = refs[-1]
     total = refs[0][...].astype(F32)
-    for r in refs[1:parts]:
+    for r in refs[1:-1]:
         total = total + r[...].astype(F32)
-    refs[parts][...] = total.astype(BF16)
+    total = total.astype(BF16)
+    devices = out_ref.shape[0]
+    for i in range(devices):
+        near, far = (total[j * capacity : (j + 1) * capacity] for j in (i, devices + i))
+        out_ref[me_ref[0] ^ i] = jnp.concatenate([near, far], 0)
 
 
 def combine_kernel(top, capacity, half_ref, back_ref, own_ref, far_ref, own_out, far_out):
     slots, width = back_ref.shape[0], back_ref.shape[1] - LANES
-    lane = lax.broadcasted_iota(jnp.int32, (own_ref.shape[0], LANES), 1)
+    rows = own_ref.shape[0]
+    lane = lax.broadcasted_iota(jnp.int32, (rows, LANES), 1)
+    slot = lax.broadcasted_iota(jnp.int32, (rows, slots), 1)
+    device = slot // (2 * capacity)
+    expert = ((device // 2) * 4 + half_ref[0] * 2 + device % 2).astype(F32)
+    place = (slot % capacity).astype(F32)
     for which, (meta_ref, out_ref) in enumerate(((own_ref, own_out), (far_ref, far_out))):
         meta = meta_ref[:, 2 * width :].astype(F32)
-        match, held = slot_table(meta, top, half_ref[0], which, capacity, slots)
+        match, held = held_slots(meta, top, expert, place)
+        held = jnp.where((slot // capacity) % 2 == which, held, 0.0)
         dx = dot(held.astype(BF16), back_ref[:, :width], 1, 0)
         probs = jnp.zeros(lane.shape, F32)
         for k in range(top):
@@ -198,13 +203,17 @@
     sd = jax.ShapeDtypeStruct
 
     def within_half(v):
-        return lax.all_to_all(
-            v.reshape(devices, 2 * capacity, v.shape[1]),
-            ("seq", "zl"),
-            split_axis=0,
-            concat_axis=0,
-            tiled=True,
-        ).reshape(v.shape)
+        return lax.all_to_all(v, ("seq", "zl"), split_axis=0, concat_axis=0, tiled=True)
+
+    def within_plane(pieces):
+        order = [d for d in reversed(range(1, groups))]
+        moved = list(pieces)
+        for d in order:
+            moved[d] = lax.ppermute(pieces[d], "seq", [(i, i ^ d) for i in range(groups)])
+        return moved
+
+    def beside(v):
+        return lax.ppermute(v, "zl", [(0, 1), (1, 0)])
 
     def mirror(v):
         return lax.ppermute(v, ("zh", "zl"), [(i, 3 - i) for i in range(4)])
@@ -213,6 +222,7 @@
         return lax.ppermute(v, "slice", [(i, (i + step) % parts) for i in range(parts)])
 
     half = lax.axis_index("zh").astype(jnp.int32).reshape(1)
+    me = lax.axis_index(("seq", "zl")).astype(jnp.int32).reshape(1)
     own = pl.pallas_call(
         pack_kernel,
         out_shape=pltpu.VMEM((rows, 2 * width + LANES), BF16),
@@ -226,7 +236,24 @@
         compiler_params=params(4),
         name="pack",
     )(*[in_hbm(v) for v in (tokens, out_grads, route_ids.T, route_probs.T)])
-    far = mirror(own)
+    def select(first, second, name):
+        return pl.pallas_call(
+            lambda *r: select_kernel(top, capacity, *r),
+            out_shape=[sd((2 * capacity, 2 * width + LANES), BF16)] * groups,
+            in_specs=[SMEM, SMEM, VMEM, VMEM],
+            out_specs=[VMEM] * groups,
+            compiler_params=params(8),
+            name=name,
+        )(half, me, first, second)
+
+    far, near = mirror(own), beside(own)
+    picked = select(own, near, "near")
+    relayed, _ = lax.optimization_barrier((far, picked))
+    near_rows = within_plane(picked)
+    beyond = beside(relayed)
+    picked = select(far, beyond, "far")
+    first = [across(picked[0], i) for i in range(1, parts)]
+    w_held, *first = lax.optimization_barrier((w_gate_up, *first))
     staged = pl.pallas_call(
         stage_kernel,
         out_shape=pltpu.VMEM(w_gate_up.shape, BF16),
@@ -236,24 +263,20 @@
         compiler_params=params(4),
         cost_estimate=pl.CostEstimate(flops=0, bytes_accessed=8 * hidden * width, transcendentals=0),
         name="stage",
-    )(in_hbm(w_gate_up))
-    far, staged = lax.optimization_barrier((far, staged))
-    picked = pl.pallas_call(
-        lambda *r: select_kernel(top, capacity, *r),
-        out_shape=sd((slots, 2 * width + LANES), BF16),
-        in_specs=[SMEM, VMEM, VMEM],
-        out_specs=VMEM,
-        compiler_params=params(8),
-        name="select",
-    )(half, own, far)
-    mine = within_half(picked)
-    got = [mine] + [across(mine, i) for i in range(1, parts)]
+    )(in_hbm(w_held))
+    far_rows = within_plane(picked)
+    near_rows[3], staged = lax.optimization_barrier((near_rows[3], staged))
+    got = near_rows + far_rows
+    for i in range(1, parts):
+        got += [across(v, i) for v in near_rows]
+        got += [across(v, i) if d else first[i - 1] for d, v in enumerate(far_rows)]
+    pieces = len(got)
 
     big = params(30)
     outs = pl.pallas_call(
-        lambda *r: expert_kernel(parts, *r),
+        lambda *r: expert_kernel(parts, pieces, *r),
         out_shape=[sd((slots, width + LANES), BF16)] * parts + [sd((total, hidden), BF16)] * 3,
-        in_specs=[VMEM] * (parts + 2),
+        in_specs=[VMEM] * (pieces + 2),
         out_specs=[VMEM] * (parts + 3),
         compiler_params=big,
         name="expert",
@@ -261,22 +284,22 @@
     dx_parts, (gg, gu, act) = outs[:parts], outs[parts:]
     returned = [dx_parts[0]] + [across(dx_parts[i], -i) for i in range(1, parts)]
     summed = pl.pallas_call(
-        lambda *r: add_kernel(parts, *r),
-        out_shape=sd((slots, width + LANES), BF16),
-        in_specs=[VMEM] * parts,
+        lambda *r: add_kernel(capacity, *r),
+        out_shape=sd((devices, 2 * capacity, width + LANES), BF16),
+        in_specs=[SMEM] + [VMEM] * parts,
         out_specs=VMEM,
         compiler_params=params(12),
         name="add",
-    )(*returned)
-    back = within_half(summed)
+    )(me, *returned)
+    back = within_half(summed).reshape(slots, width + LANES)
     grad_gu, grad_down = pl.pallas_call(
-        lambda *r: weights_kernel(parts, *r),
+        lambda *r: weights_kernel(pieces, *r),
         out_shape=[sd(w_gate_up.shape, BF16), sd(w_down.shape, BF16)],
-        in_specs=[VMEM] * (parts + 3),
+        in_specs=[VMEM] * (pieces + 3),
         out_specs=[ANY] * 2,
         scratch_shapes=[
             pltpu.VMEM((3, hidden, width), BF16),
-            pltpu.SemaphoreType.DMA((3,)),
+            pltpu.SemaphoreType.DMA((3, -(-hidden // LANES))),
         ],
         compiler_params=params(40),
         cost_estimate=pl.CostEstimate(

time: 62.5 us -> 60.2 us (0.963)
  blocking collectives: 33.6 us -> 13.6 us
  starting transfers between devices: 6.77 us -> 17.2 us
  waiting for transfers between devices: 5.81 us -> 12.9 us
    all_to_all x2 -> x1, blocking collectives: 33.6 us -> 13.6 us  [within_half(): lax.all_to_all(v, ('seq', 'zl'), split_axis=0, concat_axis=0, tiled=True)]
    ppermute x0 -> x8, starting transfers between devices: none -> 10.5 us  [the longest x6 6.82 us: within_plane(): lax.ppermute(pieces[d], 'seq', [(i, i ^ d) for i in range(groups)])]
    ppermute x0 -> x8, waiting for transfers between devices: none -> 5.45 us  [the longest x6 3.4 us: within_plane(): lax.ppermute(pieces[d], 'seq', [(i, i ^ d) for i in range(groups)])]
    ppermute x2, waiting for transfers between devices: 1.28 us -> 4.78 us  [mirror(): return lax.ppermute(v, ('zh', 'zl'), [(i, 3 - i) for i in range(4)])]
    ppermute x2, starting transfers between devices: 6.56 us -> 4.63 us  [mirror(): return lax.ppermute(v, ('zh', 'zl'), [(i, 3 - i) for i in range(4)])]
    ppermute x2 -> x9, starting transfers between devices: 0.21 us -> 2.11 us  [across(): lax.ppermute(v, 'slice', [(i, (i + step) % parts) for i in range(parts)])]
    ppermute x2 -> x9, waiting for transfers between devices: 4.52 us -> 2.67 us  [across(): lax.ppermute(v, 'slice', [(i, (i + step) % parts) for i in range(parts)])]
    pallas_call x4 -> x5, Pallas kernels: 10.4 us -> 10.4 us  [the longest x1 5.26 us: body(): pl.pallas_call(lambda *r: expert_kernel(parts, pieces, *r), out_shape=[sd...]
  transfers between devices with their start and end apart: 4 -> 19, of which waited for: 4 -> 11; matrix products, arithmetic and copies ran while one was open for 0% -> 0% of each run, Pallas kernels for 11% -> 13%
where the time goes in v6:
time: 60.2 us; the launch traced here: 60 us
  starting transfers between devices  17.2 us (29%)
  Pallas kernels  15.5 us (26%)
  blocking collectives  13.6 us (23%)
  waiting for transfers between devices  12.9 us (21%)
  between operations  0.74 us (1%)
    all_to_all x1, blocking collectives, within_half(): lax.all_to_all(v, ('seq', 'zl'), split_axis=0, concat_axis=0, tiled=True)  13.6 us
    ppermute x6, starting transfers between devices, within_plane(): lax.ppermute(pieces[d], 'seq', [(i, i ^ d) for i in range(groups)])  6.82 us
    pallas_call x1, Pallas kernels, body(): pl.pallas_call(lambda *r: expert_kernel(parts, pieces, *r), out_shape=[sd...  5.26 us
    ppermute x2, waiting for transfers between devices, mirror(): return lax.ppermute(v, ('zh', 'zl'), [(i, 3 - i) for i in range(4)])  4.78 us
    ppermute x2, starting transfers between devices, mirror(): return lax.ppermute(v, ('zh', 'zl'), [(i, 3 - i) for i in range(4)])  4.63 us
    pallas_call x1, Pallas kernels, body(): pl.pallas_call(lambda *r: weights_kernel(pieces, *r), out_shape=[sd(w_gat...  3.86 us
    ppermute x2, starting transfers between devices, beside(): return lax.ppermute(v, 'zl', [(0, 1), (1, 0)])  3.66 us
    ppermute x6, waiting for transfers between devices, within_plane(): lax.ppermute(pieces[d], 'seq', [(i, i ^ d) for i in range(groups)])  3.4 us
  transfers between devices with their start and end apart: 19, of which 11 were waited for; matrix products, arithmetic and copies ran while one was open for 0% of the time, Pallas kernels for 13%

profile of v6, /device:TPU:0, one launch (start us, length us, event | category | flops | bytes accessed | tf_op | source)
XLA Modules:
  0.0 60.0 jit_solution(2628782077564698396)
XLA Ops:
  0.6 0.9 %pack.1.r_2_ = bf16[16,4224]{1,0:T(8,128)(2,1)S(1)} custom-call(bf16[16,2048]{1,0:T(8,128)(2,1)} %x_hbm.1, bf16[16,2048]{1,0:T(8,128)(2,1)} %dy_hbm.1, s32[6,16]{1,0:T(8,128)} %bitcast.7, bf16[6,16]{1,0:T(8,128)(2,1)} %bitcast.8), custom_call_target="tpu_custom_call" | custom-call | tf_op jit(solution)/shard_map/pack/pallas_call | solution.py:226
  1.6 3.1 %collective-permute-start = (bf16[16,4224]{1,0:T(8,128)(2,1)S(1)}, bf16[16,4224]{1,0:T(8,128)(2,1)S(1)}, u32[]{:S(2)}, u32[]{:S(2)}) collective-permute-start(bf16[16,4224]{1,0:T(8,128)(2,1)S(1)} %pack.1.r_2_), channel_id=1, source_target_pairs={{0,2},{2,0},{1,3},{3,1},{4,6},{6,4},{5,7},{7,5},{8,10},{10,8},{9,1... | collective-permute-start | bytes 405512 | tf_op jit(solution)/shard_map/ppermute | solution.py:216
  4.7 2.5 %collective-permute-start.4 = (bf16[16,4224]{1,0:T(8,128)(2,1)S(1)}, bf16[16,4224]{1,0:T(8,128)(2,1)S(1)}, u32[]{:S(2)}, u32[]{:S(2)}) collective-permute-start(bf16[16,4224]{1,0:T(8,128)(2,1)S(1)} %pack.1.r_2_), channel_id=1, source_target_pairs={{0,6},{2,4},{4,2},{6,0},{1,7},{3,5},{5,3},{7,1},{8,14},{10,12},{12... | collective-permute-start | bytes 405512 | tf_op jit(solution)/shard_map/ppermute | solution.py:219
  7.1 1.1 %collective-permute-done.r_3_ = bf16[16,4224]{1,0:T(8,128)(2,1)S(1)} collective-permute-done((bf16[16,4224]{1,0:T(8,128)(2,1)S(1)}, bf16[16,4224]{1,0:T(8,128)(2,1)S(1)}, u32[]{:S(2)}, u32[]{:S(2)}) %collective-permute-start) | collective-permute-done | bytes 135200 | tf_op jit(solution)/shard_map/ppermute | solution.py:216
  8.3 0.5 near.1
  8.8 4.7 %collective-permute-done.4.r_2_.r_3_ = bf16[16,4224]{1,0:T(8,128)(2,1)S(1)} collective-permute-done((bf16[16,4224]{1,0:T(8,128)(2,1)S(1)}, bf16[16,4224]{1,0:T(8,128)(2,1)S(1)}, u32[]{:S(2)}, u32[]{:S(2)}) %collective-permute-start.4) | collective-permute-done | bytes 135200 | tf_op jit(solution)/shard_map/ppermute | solution.py:219
  13.4 0.6 collective-permute-start.5
  14.0 1.5 %collective-permute-start.1 = (bf16[16,4224]{1,0:T(8,128)(2,1)S(1)}, bf16[16,4224]{1,0:T(8,128)(2,1)S(1)}, u32[]{:S(2)}, u32[]{:S(2)}) collective-permute-start(bf16[16,4224]{1,0:T(8,128)(2,1)S(1)} %get-tuple-element.29), channel_id=1, source_target_pairs={{0,8},{8,0},{16,24},{24,16},{1,9},{9,1},{17,25},{25,17},{2,10},{10... | collective-permute-start | bytes 405512 | tf_op jit(solution)/shard_map/ppermute | solution.py:212
  15.5 1.5 %collective-permute-start.2 = (bf16[16,4224]{1,0:T(8,128)(2,1)S(1)}, bf16[16,4224]{1,0:T(8,128)(2,1)S(1)}, u32[]{:S(2)}, u32[]{:S(2)}) collective-permute-start(bf16[16,4224]{1,0:T(8,128)(2,1)S(1)} %get-tuple-element.30), channel_id=1, source_target_pairs={{0,16},{8,24},{16,0},{24,8},{1,17},{9,25},{17,1},{25,9},{2,18},{10... | collective-permute-start | bytes 405512 | tf_op jit(solution)/shard_map/ppermute | solution.py:212
  17.5 0.9 %collective-permute-done.5.r_3_ = bf16[16,4224]{1,0:T(8,128)(2,1)S(1)} collective-permute-done((bf16[16,4224]{1,0:T(8,128)(2,1)S(1)}, bf16[16,4224]{1,0:T(8,128)(2,1)S(1)}, u32[]{:S(2)}, u32[]{:S(2)}) %collective-permute-start.5) | collective-permute-done | bytes 135200 | tf_op jit(solution)/shard_map/ppermute | solution.py:216
  19.6 0.6 %collective-permute-done.1.r_1_ = bf16[16,4224]{1,0:T(8,128)(2,1)S(1)} collective-permute-done((bf16[16,4224]{1,0:T(8,128)(2,1)S(1)}, bf16[16,4224]{1,0:T(8,128)(2,1)S(1)}, u32[]{:S(2)}, u32[]{:S(2)}) %collective-permute-start.1) | collective-permute-done | bytes 135200 | tf_op jit(solution)/shard_map/ppermute | solution.py:212
  20.2 0.9 %collective-permute-start.7 = (bf16[16,4224]{1,0:T(8,128)(2,1)S(1)}, bf16[16,4224]{1,0:T(8,128)(2,1)S(1)}, u32[]{:S(2)}, u32[]{:S(2)}) collective-permute-start(bf16[16,4224]{1,0:T(8,128)(2,1)S(1)} %get-tuple-element.36), channel_id=1, source_target_pairs={{0,8},{8,0},{16,24},{24,16},{1,9},{9,1},{17,25},{25,17},{2,10},{10... | collective-permute-start | bytes 405512 | tf_op jit(solution)/shard_map/ppermute | solution.py:212
  21.4 2.4 %collective-permute-start.8 = (bf16[16,4224]{1,0:T(8,128)(2,1)S(1)}, bf16[16,4224]{1,0:T(8,128)(2,1)S(1)}, u32[]{:S(2)}, u32[]{:S(2)}) collective-permute-start(bf16[16,4224]{1,0:T(8,128)(2,1)S(1)} %get-tuple-element.37), channel_id=1, source_target_pairs={{0,16},{8,24},{16,0},{24,8},{1,17},{9,25},{17,1},{25,9},{2,18},{10... | collective-permute-start | bytes 405512 | tf_op jit(solution)/shard_map/ppermute | solution.py:212
  24.0 2.8 %stage.1.r_16_ = bf16[1,2,704,2048]{3,2,1,0:T(8,128)(2,1)S(1)} custom-call(bf16[1,2,704,2048]{3,2,1,0:T(8,128)(2,1)} %src_hbm), custom_call_target="tpu_custom_call" | custom-call | bytes 11534336 | tf_op jit(solution)/shard_map/stage/pallas_call | solution.py:257
  27.4 1.2 %collective-permute-done.8.r_6_ = bf16[16,4224]{1,0:T(8,128)(2,1)S(1)} collective-permute-done((bf16[16,4224]{1,0:T(8,128)(2,1)S(1)}, bf16[16,4224]{1,0:T(8,128)(2,1)S(1)}, u32[]{:S(2)}, u32[]{:S(2)}) %collective-permute-start.8) | collective-permute-done | bytes 135200 | tf_op jit(solution)/shard_map/ppermute | solution.py:212
  28.5 1.3 %collective-permute-done.9.r_7_ = bf16[16,4224]{1,0:T(8,128)(2,1)S(1)} collective-permute-done((bf16[16,4224]{1,0:T(8,128)(2,1)S(1)}, bf16[16,4224]{1,0:T(8,128)(2,1)S(1)}, u32[]{:S(2)}, u32[]{:S(2)}) %collective-permute-start.9) | collective-permute-done | bytes 135200 | tf_op jit(solution)/shard_map/ppermute | solution.py:212
  30.3 0.8 %collective-permute-done.16.r_15_ = bf16[16,4224]{1,0:T(8,128)(2,1)S(1)} collective-permute-done((bf16[16,4224]{1,0:T(8,128)(2,1)S(1)}, bf16[16,4224]{1,0:T(8,128)(2,1)S(1)}, u32[]{:S(2)}, u32[]{:S(2)}) %collective-permute-start.16) | collective-permute-done | bytes 135200 | tf_op jit(solution)/shard_map/ppermute | solution.py:222
  31.3 5.3 %expert.1 = (bf16[128,2176]{1,0:T(8,128)(2,1)S(1)}, bf16[128,2176]{1,0:T(8,128)(2,1)S(1)}, bf16[256,704]{1,0:T(8,128)(2,1)S(1)}, bf16[256,704]{1,0:T(8,128)(2,1)S(1)}, bf16[256,704]{1,0:T(8,128)(2,1)S(1)}) custom-call(bf16[16,4224]{1,0:T(8,128)(2,1)S(1)} %get-tuple-element.28.r_0_, bf16[16,4224]{1,0:T(8,128)(2,1)S(1)} %collective-permute-done.1.r_1_, ...), custom_call_target="tpu_custom_call" | custom-call | tf_op jit(solution)/shard_map/expert/pallas_call | solution.py:276
  37.0 1.6 %collective-permute-done.17.r_2_ = bf16[128,2176]{1,0:T(8,128)(2,1)S(1)} collective-permute-done((bf16[128,2176]{1,0:T(8,128)(2,1)S(1)}, bf16[128,2176]{1,0:T(8,128)(2,1)S(1)}, u32[]{:S(2)}, u32[]{:S(2)}) %collective-permute-start.17) | collective-permute-done | bytes 557088 | tf_op jit(solution)/shard_map/ppermute | solution.py:222
  38.8 13.6 %all_to_all.5 = bf16[8,16,2176]{2,1,0:T(8,128)(2,1)S(1)} all-to-all(bf16[8,16,2176]{2,1,0:T(8,128)(2,1)S(1)} %add.5), channel_id=1, replica_groups=mesh['seq'=4,'zh'=2,'zl'=2,'slice'=2] {'seq','zl'}, dimensions={0} | all-to-all | bytes 1114112 | tf_op jit(solution)/shard_map/all_to_all | solution.py:206
  52.5 0.6 %combine.1 = (f32[16,2176]{1,0:T(8,128)S(1)}, bf16[16,2176]{1,0:T(8,128)(2,1)S(1)}) custom-call(s32[1]{0:T(128)} %bitcast.r_0_, bf16[128,2176]{1,0:T(8,128)(2,1)S(1)} %bitcast.6, bf16[16,4224]{1,0:T(8,128)(2,1)S(1)} %pack.1.r_2_, bf16[16,4224]{1,0:T(8,128)(2,1)S(1)} %collective-permute-done.4.r_2_.r_3_), custom_call_target="tpu_custom_call" | custom-call | tf_op jit(solution)/shard_map/combine/pallas_call | solution.py:312
  53.1 2.2 %collective-permute-start.18 = (bf16[16,2176]{1,0:T(8,128)(2,1)S(1)}, bf16[16,2176]{1,0:T(8,128)(2,1)S(1)}, u32[]{:S(2)}, u32[]{:S(2)}) collective-permute-start(bf16[16,2176]{1,0:T(8,128)(2,1)S(1)} %get-tuple-element.44), channel_id=1, source_target_pairs={{0,6},{2,4},{4,2},{6,0},{1,7},{3,5},{5,3},{7,1},{8,14},{10,12},{12... | collective-permute-start | bytes 208904 | tf_op jit(solution)/shard_map/ppermute | solution.py:219
  55.2 3.9 %weights.1 = (bf16[1,2,704,2048]{3,2,1,0:T(8,128)(2,1)}, bf16[1,704,2048]{2,1,0:T(8,128)(2,1)}) custom-call(bf16[16,4224]{1,0:T(8,128)(2,1)S(1)} %get-tuple-element.28.r_0_, bf16[16,4224]{1,0:T(8,128)(2,1)S(1)} %collective-permute-done.1.r_1_, bf16[16,4224]{1,0:T(8,128)(2,1)S(1)} %collective-permute-done.2.r_2_, ...), custom_call_target="tpu_custom_call" | custom-call | flops 2214592512 | bytes 14417920 | tf_op jit(solution)/shard_map/weights/pallas_call | solution.py:295
  59.2 0.7 %final.1 = (bf16[16,2048]{1,0:T(8,128)(2,1)}, f32[6,16]{1,0:T(8,128)}) custom-call(f32[16,2176]{1,0:T(8,128)S(1)} %get-tuple-element.43.own_ref, bf16[16,2176]{1,0:T(8,128)(2,1)S(1)} %collective-permute-done.18.far_ref), custom_call_target="tpu_custom_call" | custom-call | tf_op jit(solution)/shard_map/final/pallas_call | solution.py:321
  (26 shorter events, 4.0 us)
Async XLA Ops:
  1.6 6.7 %collective-permute-start = (bf16[16,4224]{1,0:T(8,128)(2,1)S(1)}, bf16[16,4224]{1,0:T(8,128)(2,1)S(1)}, u32[]{:S(2)}, u32[]{:S(2)}) collective-permute-start(bf16[16,4224]{1,0:T(8,128)(2,1)S(1)} %pack.1.r_2_), channel_id=1, source_target_pairs={{0,2},{2,0},{1,3},{3,1},{4,6},{6,4},{5,7},{7,5},{8,10},{10,8},{9,1... | collective-permute-start | bytes 405512 | tf_op jit(solution)/shard_map/ppermute | solution.py:216
  4.7 8.8 %collective-permute-start.4 = (bf16[16,4224]{1,0:T(8,128)(2,1)S(1)}, bf16[16,4224]{1,0:T(8,128)(2,1)S(1)}, u32[]{:S(2)}, u32[]{:S(2)}) collective-permute-start(bf16[16,4224]{1,0:T(8,128)(2,1)S(1)} %pack.1.r_2_), channel_id=1, source_target_pairs={{0,6},{2,4},{4,2},{6,0},{1,7},{3,5},{5,3},{7,1},{8,14},{10,12},{12... | collective-permute-start | bytes 405512 | tf_op jit(solution)/shard_map/ppermute | solution.py:219
  13.4 5.0 %collective-permute-start.5 = (bf16[16,4224]{1,0:T(8,128)(2,1)S(1)}, bf16[16,4224]{1,0:T(8,128)(2,1)S(1)}, u32[]{:S(2)}, u32[]{:S(2)}) collective-permute-start(bf16[16,4224]{1,0:T(8,128)(2,1)S(1)} %collective-permute-done.4.r_2_.r_3_), channel_id=1, source_target_pairs={{0,2},{2,0},{1,3},{3,1},{4,6},{6,4},{5,7},{7,5},{8,10},{10,8},{9,1... | collective-permute-start | bytes 405512 | tf_op jit(solution)/shard_map/ppermute | solution.py:216
  14.0 6.2 %collective-permute-start.1 = (bf16[16,4224]{1,0:T(8,128)(2,1)S(1)}, bf16[16,4224]{1,0:T(8,128)(2,1)S(1)}, u32[]{:S(2)}, u32[]{:S(2)}) collective-permute-start(bf16[16,4224]{1,0:T(8,128)(2,1)S(1)} %get-tuple-element.29), channel_id=1, source_target_pairs={{0,8},{8,0},{16,24},{24,16},{1,9},{9,1},{17,25},{25,17},{2,10},{10... | collective-permute-start | bytes 405512 | tf_op jit(solution)/shard_map/ppermute | solution.py:212
  15.5 5.9 %collective-permute-start.2 = (bf16[16,4224]{1,0:T(8,128)(2,1)S(1)}, bf16[16,4224]{1,0:T(8,128)(2,1)S(1)}, u32[]{:S(2)}, u32[]{:S(2)}) collective-permute-start(bf16[16,4224]{1,0:T(8,128)(2,1)S(1)} %get-tuple-element.30), channel_id=1, source_target_pairs={{0,16},{8,24},{16,0},{24,8},{1,17},{9,25},{17,1},{25,9},{2,18},{10... | collective-permute-start | bytes 405512 | tf_op jit(solution)/shard_map/ppermute | solution.py:212
  17.0 6.8 %collective-permute-start.3 = (bf16[16,4224]{1,0:T(8,128)(2,1)S(1)}, bf16[16,4224]{1,0:T(8,128)(2,1)S(1)}, u32[]{:S(2)}, u32[]{:S(2)}) collective-permute-start(bf16[16,4224]{1,0:T(8,128)(2,1)S(1)} %get-tuple-element.31), channel_id=1, source_target_pairs={{0,24},{8,16},{16,8},{24,0},{1,25},{9,17},{17,9},{25,1},{2,26},{10... | collective-permute-start | bytes 405512 | tf_op jit(solution)/shard_map/ppermute | solution.py:212
  19.0 4.9 %collective-permute-start.6 = (bf16[16,4224]{1,0:T(8,128)(2,1)S(1)}, bf16[16,4224]{1,0:T(8,128)(2,1)S(1)}, u32[]{:S(2)}, u32[]{:S(2)}) collective-permute-start(bf16[16,4224]{1,0:T(8,128)(2,1)S(1)} %get-tuple-element.33.r_4_), channel_id=1, source_target_pairs={{0,1},{1,0},{2,3},{3,2},{4,5},{5,4},{6,7},{7,6},{8,9},{9,8},{10,11... | collective-permute-start | bytes 405512 | tf_op jit(solution)/shard_map/ppermute | solution.py:222
  19.1 7.7 %collective-permute-start.10 = (bf16[16,4224]{1,0:T(8,128)(2,1)S(1)}, bf16[16,4224]{1,0:T(8,128)(2,1)S(1)}, u32[]{:S(2)}, u32[]{:S(2)}) collective-permute-start(bf16[16,4224]{1,0:T(8,128)(2,1)S(1)} %get-tuple-element.28.r_0_), channel_id=1, source_target_pairs={{0,1},{1,0},{2,3},{3,2},{4,5},{5,4},{6,7},{7,6},{8,9},{9,8},{10,11... | collective-permute-start | bytes 405512 | tf_op jit(solution)/shard_map/ppermute | solution.py:222
  20.2 7.0 %collective-permute-start.7 = (bf16[16,4224]{1,0:T(8,128)(2,1)S(1)}, bf16[16,4224]{1,0:T(8,128)(2,1)S(1)}, u32[]{:S(2)}, u32[]{:S(2)}) collective-permute-start(bf16[16,4224]{1,0:T(8,128)(2,1)S(1)} %get-tuple-element.36), channel_id=1, source_target_pairs={{0,8},{8,0},{16,24},{24,16},{1,9},{9,1},{17,25},{25,17},{2,10},{10... | collective-permute-start | bytes 405512 | tf_op jit(solution)/shard_map/ppermute | solution.py:212
  21.4 7.1 %collective-permute-start.8 = (bf16[16,4224]{1,0:T(8,128)(2,1)S(1)}, bf16[16,4224]{1,0:T(8,128)(2,1)S(1)}, u32[]{:S(2)}, u32[]{:S(2)}) collective-permute-start(bf16[16,4224]{1,0:T(8,128)(2,1)S(1)} %get-tuple-element.37), channel_id=1, source_target_pairs={{0,16},{8,24},{16,0},{24,8},{1,17},{9,25},{17,1},{25,9},{2,18},{10... | collective-permute-start | bytes 405512 | tf_op jit(solution)/shard_map/ppermute | solution.py:212
  23.9 7.5 %copy-start = (bf16[1,704,2048]{2,1,0:T(8,128)(2,1)S(1)}, bf16[1,704,2048]{2,1,0:T(8,128)(2,1)}, u32[]{:S(2)}) copy-start(bf16[1,704,2048]{2,1,0:T(8,128)(2,1)} %r_17_.1) | copy-start | bytes 8650756
  23.9 5.9 %collective-permute-start.9 = (bf16[16,4224]{1,0:T(8,128)(2,1)S(1)}, bf16[16,4224]{1,0:T(8,128)(2,1)S(1)}, u32[]{:S(2)}, u32[]{:S(2)}) collective-permute-start(bf16[16,4224]{1,0:T(8,128)(2,1)S(1)} %get-tuple-element.38), channel_id=1, source_target_pairs={{0,24},{8,16},{16,8},{24,0},{1,25},{9,17},{17,9},{25,1},{2,26},{10... | collective-permute-start | bytes 405512 | tf_op jit(solution)/shard_map/ppermute | solution.py:212
  23.9 5.9 %collective-permute-start.11 = (bf16[16,4224]{1,0:T(8,128)(2,1)S(1)}, bf16[16,4224]{1,0:T(8,128)(2,1)S(1)}, u32[]{:S(2)}, u32[]{:S(2)}) collective-permute-start(bf16[16,4224]{1,0:T(8,128)(2,1)S(1)} %collective-permute-done.1.r_1_), channel_id=1, source_target_pairs={{0,1},{1,0},{2,3},{3,2},{4,5},{5,4},{6,7},{7,6},{8,9},{9,8},{10,11... | collective-permute-start | bytes 405512 | tf_op jit(solution)/shard_map/ppermute | solution.py:222
  26.8 3.5 %collective-permute-start.12 = (bf16[16,4224]{1,0:T(8,128)(2,1)S(1)}, bf16[16,4224]{1,0:T(8,128)(2,1)S(1)}, u32[]{:S(2)}, u32[]{:S(2)}) collective-permute-start(bf16[16,4224]{1,0:T(8,128)(2,1)S(1)} %collective-permute-done.2.r_2_), channel_id=1, source_target_pairs={{0,1},{1,0},{2,3},{3,2},{4,5},{5,4},{6,7},{7,6},{8,9},{9,8},{10,11... | collective-permute-start | bytes 405512 | tf_op jit(solution)/shard_map/ppermute | solution.py:222
  27.2 3.1 %collective-permute-start.14 = (bf16[16,4224]{1,0:T(8,128)(2,1)S(1)}, bf16[16,4224]{1,0:T(8,128)(2,1)S(1)}, u32[]{:S(2)}, u32[]{:S(2)}) collective-permute-start(bf16[16,4224]{1,0:T(8,128)(2,1)S(1)} %collective-permute-done.7.r_5_), channel_id=1, source_target_pairs={{0,1},{1,0},{2,3},{3,2},{4,5},{5,4},{6,7},{7,6},{8,9},{9,8},{10,11... | collective-permute-start | bytes 405512 | tf_op jit(solution)/shard_map/ppermute | solution.py:222
  28.5 1.8 %collective-permute-start.15 = (bf16[16,4224]{1,0:T(8,128)(2,1)S(1)}, bf16[16,4224]{1,0:T(8,128)(2,1)S(1)}, u32[]{:S(2)}, u32[]{:S(2)}) collective-permute-start(bf16[16,4224]{1,0:T(8,128)(2,1)S(1)} %collective-permute-done.8.r_6_), channel_id=1, source_target_pairs={{0,1},{1,0},{2,3},{3,2},{4,5},{5,4},{6,7},{7,6},{8,9},{9,8},{10,11... | collective-permute-start | bytes 405512 | tf_op jit(solution)/shard_map/ppermute | solution.py:222
  29.8 1.4 %collective-permute-start.16 = (bf16[16,4224]{1,0:T(8,128)(2,1)S(1)}, bf16[16,4224]{1,0:T(8,128)(2,1)S(1)}, u32[]{:S(2)}, u32[]{:S(2)}) collective-permute-start(bf16[16,4224]{1,0:T(8,128)(2,1)S(1)} %collective-permute-done.9.r_7_), channel_id=1, source_target_pairs={{0,1},{1,0},{2,3},{3,2},{4,5},{5,4},{6,7},{7,6},{8,9},{9,8},{10,11... | collective-permute-start | bytes 405512 | tf_op jit(solution)/shard_map/ppermute | solution.py:222
  29.8 1.5 %collective-permute-start.13 = (bf16[16,4224]{1,0:T(8,128)(2,1)S(1)}, bf16[16,4224]{1,0:T(8,128)(2,1)S(1)}, u32[]{:S(2)}, u32[]{:S(2)}) collective-permute-start(bf16[16,4224]{1,0:T(8,128)(2,1)S(1)} %collective-permute-done.3.r_3_), channel_id=1, source_target_pairs={{0,1},{1,0},{2,3},{3,2},{4,5},{5,4},{6,7},{7,6},{8,9},{9,8},{10,11... | collective-permute-start | bytes 405512 | tf_op jit(solution)/shard_map/ppermute | solution.py:222
  36.6 2.0 %collective-permute-start.17 = (bf16[128,2176]{1,0:T(8,128)(2,1)S(1)}, bf16[128,2176]{1,0:T(8,128)(2,1)S(1)}, u32[]{:S(2)}, u32[]{:S(2)}) collective-permute-start(bf16[128,2176]{1,0:T(8,128)(2,1)S(1)} %get-tuple-element.42), channel_id=1, source_target_pairs={{0,1},{1,0},{2,3},{3,2},{4,5},{5,4},{6,7},{7,6},{8,9},{9,8},{10,11... | collective-permute-start | bytes 1671176 | tf_op jit(solution)/shard_map/ppermute | solution.py:222
  53.1 6.2 %collective-permute-start.18 = (bf16[16,2176]{1,0:T(8,128)(2,1)S(1)}, bf16[16,2176]{1,0:T(8,128)(2,1)S(1)}, u32[]{:S(2)}, u32[]{:S(2)}) collective-permute-start(bf16[16,2176]{1,0:T(8,128)(2,1)S(1)} %get-tuple-element.44), channel_id=1, source_target_pairs={{0,6},{2,4},{4,2},{6,0},{1,7},{3,5},{5,3},{7,1},{8,14},{10,12},{12... | collective-permute-start | bytes 208904 | tf_op jit(solution)/shard_map/ppermute | solution.py:219

commit v7 on v6

--- a/solution.py
+++ b/solution.py
@@ -212,6 +212,9 @@
             moved[d] = lax.ppermute(pieces[d], "seq", [(i, i ^ d) for i in range(groups)])
         return moved
 
+    def across_half(v):
+        return lax.ppermute(v, ("zh", "zl"), [(i, i ^ 2) for i in range(4)])
+
     def beside(v):
         return lax.ppermute(v, "zl", [(0, 1), (1, 0)])
 
@@ -246,14 +249,13 @@
             name=name,
         )(half, me, first, second)
 
-    far, near = mirror(own), beside(own)
+    far = mirror(own)
+    near = beside(own)
+    beyond = across_half(own)
     picked = select(own, near, "near")
-    relayed, _ = lax.optimization_barrier((far, picked))
     near_rows = within_plane(picked)
-    beyond = beside(relayed)
     picked = select(far, beyond, "far")
-    first = [across(picked[0], i) for i in range(1, parts)]
-    w_held, *first = lax.optimization_barrier((w_gate_up, *first))
+    w_held, _ = lax.optimization_barrier((w_gate_up, picked))
     staged = pl.pallas_call(
         stage_kernel,
         out_shape=pltpu.VMEM(w_gate_up.shape, BF16),
@@ -269,7 +271,7 @@
     got = near_rows + far_rows
     for i in range(1, parts):
         got += [across(v, i) for v in near_rows]
-        got += [across(v, i) if d else first[i - 1] for d, v in enumerate(far_rows)]
+        got += [across(v, i) for v in far_rows]
     pieces = len(got)
 
     big = params(30)

time: 60.2 us -> 59.1 us (0.982)
    ppermute x2, waiting for transfers between devices: 4.78 us -> 0.02 us  [mirror(): return lax.ppermute(v, ('zh', 'zl'), [(i, 3 - i) for i in range(4)])]
    ppermute x0 -> x1, waiting for transfers between devices: none -> 3.87 us  [across_half(): return lax.ppermute(v, ('zh', 'zl'), [(i, i ^ 2) for i in range(4)])]
    ppermute x0 -> x1, starting transfers between devices: none -> 2.59 us  [across_half(): return lax.ppermute(v, ('zh', 'zl'), [(i, i ^ 2) for i in range(4)])]
    ppermute x2, starting transfers between devices: 4.63 us -> 2.27 us  [mirror(): return lax.ppermute(v, ('zh', 'zl'), [(i, 3 - i) for i in range(4)])]
    ppermute x2 -> x1, waiting for transfers between devices: 2.06 us -> 2.65 us  [beside(): return lax.ppermute(v, 'zl', [(0, 1), (1, 0)])]
    ppermute x2 -> x1, starting transfers between devices: 3.66 us -> 3.09 us  [beside(): return lax.ppermute(v, 'zl', [(0, 1), (1, 0)])]
  transfers between devices with their start and end apart: 19 -> 19, of which waited for: 11 -> 8; matrix products, arithmetic and copies ran while one was open for 0% -> 0% of each run, Pallas kernels for 13% -> 13%
where the time goes in v7:
time: 59.1 us; the launch traced here: 58.9 us
  starting transfers between devices  17 us (29%)
  Pallas kernels  15.6 us (26%)
  blocking collectives  13.3 us (23%)
  waiting for transfers between devices  12.3 us (21%)
  between operations  0.73 us (1%)
    all_to_all x1, blocking collectives, within_half(): lax.all_to_all(v, ('seq', 'zl'), split_axis=0, concat_axis=0, tiled=True)  13.3 us
    ppermute x6, starting transfers between devices, within_plane(): lax.ppermute(pieces[d], 'seq', [(i, i ^ d) for i in range(groups)])  7.11 us
    pallas_call x1, Pallas kernels, body(): pl.pallas_call(lambda *r: expert_kernel(parts, pieces, *r), out_shape=[sd...  5.27 us
    ppermute x1, waiting for transfers between devices, across_half(): return lax.ppermute(v, ('zh', 'zl'), [(i, i ^ 2) for i in range(4)])  3.87 us
    pallas_call x1, Pallas kernels, body(): pl.pallas_call(lambda *r: weights_kernel(pieces, *r), out_shape=[sd(w_gat...  3.86 us
    ppermute x6, waiting for transfers between devices, within_plane(): lax.ppermute(pieces[d], 'seq', [(i, i ^ d) for i in range(groups)])  3.11 us
    ppermute x1, starting transfers between devices, beside(): return lax.ppermute(v, 'zl', [(0, 1), (1, 0)])  3.09 us
    pallas_call x1, Pallas kernels, body(): pl.pallas_call(stage_kernel, out_shape=pltpu.VMEM(w_gate_up.shape, BF16),...  2.89 us
  transfers between devices with their start and end apart: 19, of which 8 were waited for; matrix products, arithmetic and copies ran while one was open for 0% of the time, Pallas kernels for 13%

profile of v7, /device:TPU:0, one launch (start us, length us, event | category | flops | bytes accessed | tf_op | source)
XLA Modules:
  0.0 58.9 jit_solution(11952011655609452761)
XLA Ops:
  0.6 0.9 %pack.1.r_2_ = bf16[16,4224]{1,0:T(8,128)(2,1)S(1)} custom-call(bf16[16,2048]{1,0:T(8,128)(2,1)} %x_hbm.1, bf16[16,2048]{1,0:T(8,128)(2,1)} %dy_hbm.1, s32[6,16]{1,0:T(8,128)} %bitcast.7, bf16[6,16]{1,0:T(8,128)(2,1)} %bitcast.8), custom_call_target="tpu_custom_call" | custom-call | tf_op jit(solution)/shard_map/pack/pallas_call | solution.py:229
  1.6 3.1 %collective-permute-start = (bf16[16,4224]{1,0:T(8,128)(2,1)S(1)}, bf16[16,4224]{1,0:T(8,128)(2,1)S(1)}, u32[]{:S(2)}, u32[]{:S(2)}) collective-permute-start(bf16[16,4224]{1,0:T(8,128)(2,1)S(1)} %pack.1.r_2_), channel_id=1, source_target_pairs={{0,2},{2,0},{1,3},{3,1},{4,6},{6,4},{5,7},{7,5},{8,10},{10,8},{9,1... | collective-permute-start | bytes 405512 | tf_op jit(solution)/shard_map/ppermute | solution.py:219
  4.7 2.6 %collective-permute-start.5 = (bf16[16,4224]{1,0:T(8,128)(2,1)S(1)}, bf16[16,4224]{1,0:T(8,128)(2,1)S(1)}, u32[]{:S(2)}, u32[]{:S(2)}) collective-permute-start(bf16[16,4224]{1,0:T(8,128)(2,1)S(1)} %pack.1.r_2_), channel_id=1, source_target_pairs={{0,4},{2,6},{4,0},{6,2},{1,5},{3,7},{5,1},{7,3},{8,12},{10,14},{12... | collective-permute-start | bytes 405512 | tf_op jit(solution)/shard_map/ppermute | solution.py:216
  7.3 2.6 %collective-permute-done.r_3_ = bf16[16,4224]{1,0:T(8,128)(2,1)S(1)} collective-permute-done((bf16[16,4224]{1,0:T(8,128)(2,1)S(1)}, bf16[16,4224]{1,0:T(8,128)(2,1)S(1)}, u32[]{:S(2)}, u32[]{:S(2)}) %collective-permute-start) | collective-permute-done | bytes 135200 | tf_op jit(solution)/shard_map/ppermute | solution.py:219
  9.9 0.5 near.1
  10.4 1.8 %collective-permute-start.1 = (bf16[16,4224]{1,0:T(8,128)(2,1)S(1)}, bf16[16,4224]{1,0:T(8,128)(2,1)S(1)}, u32[]{:S(2)}, u32[]{:S(2)}) collective-permute-start(bf16[16,4224]{1,0:T(8,128)(2,1)S(1)} %get-tuple-element.27), channel_id=1, source_target_pairs={{0,8},{8,0},{16,24},{24,16},{1,9},{9,1},{17,25},{25,17},{2,10},{10... | collective-permute-start | bytes 405512 | tf_op jit(solution)/shard_map/ppermute | solution.py:212
  12.2 1.5 %collective-permute-start.2 = (bf16[16,4224]{1,0:T(8,128)(2,1)S(1)}, bf16[16,4224]{1,0:T(8,128)(2,1)S(1)}, u32[]{:S(2)}, u32[]{:S(2)}) collective-permute-start(bf16[16,4224]{1,0:T(8,128)(2,1)S(1)} %get-tuple-element.28), channel_id=1, source_target_pairs={{0,16},{8,24},{16,0},{24,8},{1,17},{9,25},{17,1},{25,9},{2,18},{10... | collective-permute-start | bytes 405512 | tf_op jit(solution)/shard_map/ppermute | solution.py:212
  14.0 3.9 %collective-permute-done.5.r_3_ = bf16[16,4224]{1,0:T(8,128)(2,1)S(1)} collective-permute-done((bf16[16,4224]{1,0:T(8,128)(2,1)S(1)}, bf16[16,4224]{1,0:T(8,128)(2,1)S(1)}, u32[]{:S(2)}, u32[]{:S(2)}) %collective-permute-start.5) | collective-permute-done | bytes 135200 | tf_op jit(solution)/shard_map/ppermute | solution.py:216
  17.9 0.5 far.1
  18.4 1.6 %collective-permute-start.6 = (bf16[16,4224]{1,0:T(8,128)(2,1)S(1)}, bf16[16,4224]{1,0:T(8,128)(2,1)S(1)}, u32[]{:S(2)}, u32[]{:S(2)}) collective-permute-start(bf16[16,4224]{1,0:T(8,128)(2,1)S(1)} %get-tuple-element.31), channel_id=1, source_target_pairs={{0,8},{8,0},{16,24},{24,16},{1,9},{9,1},{17,25},{25,17},{2,10},{10... | collective-permute-start | bytes 405512 | tf_op jit(solution)/shard_map/ppermute | solution.py:212
  20.0 1.5 %collective-permute-start.7 = (bf16[16,4224]{1,0:T(8,128)(2,1)S(1)}, bf16[16,4224]{1,0:T(8,128)(2,1)S(1)}, u32[]{:S(2)}, u32[]{:S(2)}) collective-permute-start(bf16[16,4224]{1,0:T(8,128)(2,1)S(1)} %get-tuple-element.32), channel_id=1, source_target_pairs={{0,16},{8,24},{16,0},{24,8},{1,17},{9,25},{17,1},{25,9},{2,18},{10... | collective-permute-start | bytes 405512 | tf_op jit(solution)/shard_map/ppermute | solution.py:212
  21.5 0.5 collective-permute-start.8
  22.0 0.5 collective-permute-start.10
  22.5 2.9 %stage.1.r_16_ = bf16[1,2,704,2048]{3,2,1,0:T(8,128)(2,1)S(1)} custom-call(bf16[1,2,704,2048]{3,2,1,0:T(8,128)(2,1)} %src_hbm), custom_call_target="tpu_custom_call" | custom-call | bytes 11534336 | tf_op jit(solution)/shard_map/stage/pallas_call | solution.py:259
  25.5 3.1 %collective-permute-done.7.r_6_ = bf16[16,4224]{1,0:T(8,128)(2,1)S(1)} collective-permute-done((bf16[16,4224]{1,0:T(8,128)(2,1)S(1)}, bf16[16,4224]{1,0:T(8,128)(2,1)S(1)}, u32[]{:S(2)}, u32[]{:S(2)}) %collective-permute-start.7) | collective-permute-done | bytes 135200 | tf_op jit(solution)/shard_map/ppermute | solution.py:212
  28.6 0.5 collective-permute-start.15
  29.2 0.4 collective-permute-start.12
  30.7 5.3 %expert.1 = (bf16[128,2176]{1,0:T(8,128)(2,1)S(1)}, bf16[128,2176]{1,0:T(8,128)(2,1)S(1)}, bf16[256,704]{1,0:T(8,128)(2,1)S(1)}, bf16[256,704]{1,0:T(8,128)(2,1)S(1)}, bf16[256,704]{1,0:T(8,128)(2,1)S(1)}) custom-call(bf16[16,4224]{1,0:T(8,128)(2,1)S(1)} %get-tuple-element.26.r_0_, bf16[16,4224]{1,0:T(8,128)(2,1)S(1)} %collective-permute-done.1.r_1_, ...), custom_call_target="tpu_custom_call" | custom-call | tf_op jit(solution)/shard_map/expert/pallas_call | solution.py:278
  36.3 1.6 %collective-permute-done.17.r_2_ = bf16[128,2176]{1,0:T(8,128)(2,1)S(1)} collective-permute-done((bf16[128,2176]{1,0:T(8,128)(2,1)S(1)}, bf16[128,2176]{1,0:T(8,128)(2,1)S(1)}, u32[]{:S(2)}, u32[]{:S(2)}) %collective-permute-start.17) | collective-permute-done | bytes 557088 | tf_op jit(solution)/shard_map/ppermute | solution.py:225
  38.2 13.3 %all_to_all.5 = bf16[8,16,2176]{2,1,0:T(8,128)(2,1)S(1)} all-to-all(bf16[8,16,2176]{2,1,0:T(8,128)(2,1)S(1)} %add.5), channel_id=1, replica_groups=mesh['seq'=4,'zh'=2,'zl'=2,'slice'=2] {'seq','zl'}, dimensions={0} | all-to-all | bytes 1114112 | tf_op jit(solution)/shard_map/all_to_all | solution.py:206
  51.4 0.6 %combine.1 = (f32[16,2176]{1,0:T(8,128)S(1)}, bf16[16,2176]{1,0:T(8,128)(2,1)S(1)}) custom-call(s32[1]{0:T(128)} %bitcast.r_0_, bf16[128,2176]{1,0:T(8,128)(2,1)S(1)} %bitcast.6, bf16[16,4224]{1,0:T(8,128)(2,1)S(1)} %pack.1.r_2_, bf16[16,4224]{1,0:T(8,128)(2,1)S(1)} %collective-permute-done.4.r_2_.r_3_), custom_call_target="tpu_custom_call" | custom-call | tf_op jit(solution)/shard_map/combine/pallas_call | solution.py:314
  52.0 2.3 %collective-permute-start.18 = (bf16[16,2176]{1,0:T(8,128)(2,1)S(1)}, bf16[16,2176]{1,0:T(8,128)(2,1)S(1)}, u32[]{:S(2)}, u32[]{:S(2)}) collective-permute-start(bf16[16,2176]{1,0:T(8,128)(2,1)S(1)} %get-tuple-element.40), channel_id=1, source_target_pairs={{0,6},{2,4},{4,2},{6,0},{1,7},{3,5},{5,3},{7,1},{8,14},{10,12},{12... | collective-permute-start | bytes 208904 | tf_op jit(solution)/shard_map/ppermute | solution.py:222
  54.3 3.9 %weights.1 = (bf16[1,2,704,2048]{3,2,1,0:T(8,128)(2,1)}, bf16[1,704,2048]{2,1,0:T(8,128)(2,1)}) custom-call(bf16[16,4224]{1,0:T(8,128)(2,1)S(1)} %get-tuple-element.26.r_0_, bf16[16,4224]{1,0:T(8,128)(2,1)S(1)} %collective-permute-done.1.r_1_, bf16[16,4224]{1,0:T(8,128)(2,1)S(1)} %collective-permute-done.2.r_2_, ...), custom_call_target="tpu_custom_call" | custom-call | flops 2214592512 | bytes 14417920 | tf_op jit(solution)/shard_map/weights/pallas_call | solution.py:297
  58.2 0.7 %final.1 = (bf16[16,2048]{1,0:T(8,128)(2,1)}, f32[6,16]{1,0:T(8,128)}) custom-call(f32[16,2176]{1,0:T(8,128)S(1)} %get-tuple-element.39.own_ref, bf16[16,2176]{1,0:T(8,128)(2,1)S(1)} %collective-permute-done.18.far_ref), custom_call_target="tpu_custom_call" | custom-call | tf_op jit(solution)/shard_map/final/pallas_call | solution.py:323
  (26 shorter events, 2.1 us)
Async XLA Ops:
  1.6 8.3 %collective-permute-start = (bf16[16,4224]{1,0:T(8,128)(2,1)S(1)}, bf16[16,4224]{1,0:T(8,128)(2,1)S(1)}, u32[]{:S(2)}, u32[]{:S(2)}) collective-permute-start(bf16[16,4224]{1,0:T(8,128)(2,1)S(1)} %pack.1.r_2_), channel_id=1, source_target_pairs={{0,2},{2,0},{1,3},{3,1},{4,6},{6,4},{5,7},{7,5},{8,10},{10,8},{9,1... | collective-permute-start | bytes 405512 | tf_op jit(solution)/shard_map/ppermute | solution.py:219
  4.7 13.2 %collective-permute-start.5 = (bf16[16,4224]{1,0:T(8,128)(2,1)S(1)}, bf16[16,4224]{1,0:T(8,128)(2,1)S(1)}, u32[]{:S(2)}, u32[]{:S(2)}) collective-permute-start(bf16[16,4224]{1,0:T(8,128)(2,1)S(1)} %pack.1.r_2_), channel_id=1, source_target_pairs={{0,4},{2,6},{4,0},{6,2},{1,5},{3,7},{5,1},{7,3},{8,12},{10,14},{12... | collective-permute-start | bytes 405512 | tf_op jit(solution)/shard_map/ppermute | solution.py:216
  7.3 10.6 %collective-permute-start.4 = (bf16[16,4224]{1,0:T(8,128)(2,1)S(1)}, bf16[16,4224]{1,0:T(8,128)(2,1)S(1)}, u32[]{:S(2)}, u32[]{:S(2)}) collective-permute-start(bf16[16,4224]{1,0:T(8,128)(2,1)S(1)} %pack.1.r_2_), channel_id=1, source_target_pairs={{0,6},{2,4},{4,2},{6,0},{1,7},{3,5},{5,3},{7,1},{8,14},{10,12},{12... | collective-permute-start | bytes 405512 | tf_op jit(solution)/shard_map/ppermute | solution.py:222
  10.4 9.5 %collective-permute-start.1 = (bf16[16,4224]{1,0:T(8,128)(2,1)S(1)}, bf16[16,4224]{1,0:T(8,128)(2,1)S(1)}, u32[]{:S(2)}, u32[]{:S(2)}) collective-permute-start(bf16[16,4224]{1,0:T(8,128)(2,1)S(1)} %get-tuple-element.27), channel_id=1, source_target_pairs={{0,8},{8,0},{16,24},{24,16},{1,9},{9,1},{17,25},{25,17},{2,10},{10... | collective-permute-start | bytes 405512 | tf_op jit(solution)/shard_map/ppermute | solution.py:212
  12.2 9.3 %collective-permute-start.2 = (bf16[16,4224]{1,0:T(8,128)(2,1)S(1)}, bf16[16,4224]{1,0:T(8,128)(2,1)S(1)}, u32[]{:S(2)}, u32[]{:S(2)}) collective-permute-start(bf16[16,4224]{1,0:T(8,128)(2,1)S(1)} %get-tuple-element.28), channel_id=1, source_target_pairs={{0,16},{8,24},{16,0},{24,8},{1,17},{9,25},{17,1},{25,9},{2,18},{10... | collective-permute-start | bytes 405512 | tf_op jit(solution)/shard_map/ppermute | solution.py:212
  13.7 8.2 %collective-permute-start.3 = (bf16[16,4224]{1,0:T(8,128)(2,1)S(1)}, bf16[16,4224]{1,0:T(8,128)(2,1)S(1)}, u32[]{:S(2)}, u32[]{:S(2)}) collective-permute-start(bf16[16,4224]{1,0:T(8,128)(2,1)S(1)} %get-tuple-element.29), channel_id=1, source_target_pairs={{0,24},{8,16},{16,8},{24,0},{1,25},{9,17},{17,9},{25,1},{2,26},{10... | collective-permute-start | bytes 405512 | tf_op jit(solution)/shard_map/ppermute | solution.py:212
  17.9 4.1 %collective-permute-start.9 = (bf16[16,4224]{1,0:T(8,128)(2,1)S(1)}, bf16[16,4224]{1,0:T(8,128)(2,1)S(1)}, u32[]{:S(2)}, u32[]{:S(2)}) collective-permute-start(bf16[16,4224]{1,0:T(8,128)(2,1)S(1)} %get-tuple-element.26.r_0_), channel_id=1, source_target_pairs={{0,1},{1,0},{2,3},{3,2},{4,5},{5,4},{6,7},{7,6},{8,9},{9,8},{10,11... | collective-permute-start | bytes 405512 | tf_op jit(solution)/shard_map/ppermute | solution.py:225
  18.4 7.0 %collective-permute-start.6 = (bf16[16,4224]{1,0:T(8,128)(2,1)S(1)}, bf16[16,4224]{1,0:T(8,128)(2,1)S(1)}, u32[]{:S(2)}, u32[]{:S(2)}) collective-permute-start(bf16[16,4224]{1,0:T(8,128)(2,1)S(1)} %get-tuple-element.31), channel_id=1, source_target_pairs={{0,8},{8,0},{16,24},{24,16},{1,9},{9,1},{17,25},{25,17},{2,10},{10... | collective-permute-start | bytes 405512 | tf_op jit(solution)/shard_map/ppermute | solution.py:212
  20.0 8.6 %collective-permute-start.7 = (bf16[16,4224]{1,0:T(8,128)(2,1)S(1)}, bf16[16,4224]{1,0:T(8,128)(2,1)S(1)}, u32[]{:S(2)}, u32[]{:S(2)}) collective-permute-start(bf16[16,4224]{1,0:T(8,128)(2,1)S(1)} %get-tuple-element.32), channel_id=1, source_target_pairs={{0,16},{8,24},{16,0},{24,8},{1,17},{9,25},{17,1},{25,9},{2,18},{10... | collective-permute-start | bytes 405512 | tf_op jit(solution)/shard_map/ppermute | solution.py:212
  21.5 7.1 %collective-permute-start.8 = (bf16[16,4224]{1,0:T(8,128)(2,1)S(1)}, bf16[16,4224]{1,0:T(8,128)(2,1)S(1)}, u32[]{:S(2)}, u32[]{:S(2)}) collective-permute-start(bf16[16,4224]{1,0:T(8,128)(2,1)S(1)} %get-tuple-element.33), channel_id=1, source_target_pairs={{0,24},{8,16},{16,8},{24,0},{1,25},{9,17},{17,9},{25,1},{2,26},{10... | collective-permute-start | bytes 405512 | tf_op jit(solution)/shard_map/ppermute | solution.py:212
  22.0 8.7 %copy-start = (bf16[1,704,2048]{2,1,0:T(8,128)(2,1)S(1)}, bf16[1,704,2048]{2,1,0:T(8,128)(2,1)}, u32[]{:S(2)}) copy-start(bf16[1,704,2048]{2,1,0:T(8,128)(2,1)} %r_17_.1) | copy-start | bytes 8650756
  22.0 7.1 %collective-permute-start.13 = (bf16[16,4224]{1,0:T(8,128)(2,1)S(1)}, bf16[16,4224]{1,0:T(8,128)(2,1)S(1)}, u32[]{:S(2)}, u32[]{:S(2)}) collective-permute-start(bf16[16,4224]{1,0:T(8,128)(2,1)S(1)} %get-tuple-element.30.r_4_), channel_id=1, source_target_pairs={{0,1},{1,0},{2,3},{3,2},{4,5},{5,4},{6,7},{7,6},{8,9},{9,8},{10,11... | collective-permute-start | bytes 405512 | tf_op jit(solution)/shard_map/ppermute | solution.py:225
  22.0 7.2 %collective-permute-start.10 = (bf16[16,4224]{1,0:T(8,128)(2,1)S(1)}, bf16[16,4224]{1,0:T(8,128)(2,1)S(1)}, u32[]{:S(2)}, u32[]{:S(2)}) collective-permute-start(bf16[16,4224]{1,0:T(8,128)(2,1)S(1)} %collective-permute-done.1.r_1_), channel_id=1, source_target_pairs={{0,1},{1,0},{2,3},{3,2},{4,5},{5,4},{6,7},{7,6},{8,9},{9,8},{10,11... | collective-permute-start | bytes 405512 | tf_op jit(solution)/shard_map/ppermute | solution.py:225
  25.4 4.2 %collective-permute-start.11 = (bf16[16,4224]{1,0:T(8,128)(2,1)S(1)}, bf16[16,4224]{1,0:T(8,128)(2,1)S(1)}, u32[]{:S(2)}, u32[]{:S(2)}) collective-permute-start(bf16[16,4224]{1,0:T(8,128)(2,1)S(1)} %collective-permute-done.2.r_2_), channel_id=1, source_target_pairs={{0,1},{1,0},{2,3},{3,2},{4,5},{5,4},{6,7},{7,6},{8,9},{9,8},{10,11... | collective-permute-start | bytes 405512 | tf_op jit(solution)/shard_map/ppermute | solution.py:225
  28.6 1.4 %collective-permute-start.14 = (bf16[16,4224]{1,0:T(8,128)(2,1)S(1)}, bf16[16,4224]{1,0:T(8,128)(2,1)S(1)}, u32[]{:S(2)}, u32[]{:S(2)}) collective-permute-start(bf16[16,4224]{1,0:T(8,128)(2,1)S(1)} %collective-permute-done.6.r_5_), channel_id=1, source_target_pairs={{0,1},{1,0},{2,3},{3,2},{4,5},{5,4},{6,7},{7,6},{8,9},{9,8},{10,11... | collective-permute-start | bytes 405512 | tf_op jit(solution)/shard_map/ppermute | solution.py:225
  28.6 1.5 %collective-permute-start.15 = (bf16[16,4224]{1,0:T(8,128)(2,1)S(1)}, bf16[16,4224]{1,0:T(8,128)(2,1)S(1)}, u32[]{:S(2)}, u32[]{:S(2)}) collective-permute-start(bf16[16,4224]{1,0:T(8,128)(2,1)S(1)} %collective-permute-done.7.r_6_), channel_id=1, source_target_pairs={{0,1},{1,0},{2,3},{3,2},{4,5},{5,4},{6,7},{7,6},{8,9},{9,8},{10,11... | collective-permute-start | bytes 405512 | tf_op jit(solution)/shard_map/ppermute | solution.py:225
  29.1 1.4 %collective-permute-start.16 = (bf16[16,4224]{1,0:T(8,128)(2,1)S(1)}, bf16[16,4224]{1,0:T(8,128)(2,1)S(1)}, u32[]{:S(2)}, u32[]{:S(2)}) collective-permute-start(bf16[16,4224]{1,0:T(8,128)(2,1)S(1)} %collective-permute-done.8.r_7_), channel_id=1, source_target_pairs={{0,1},{1,0},{2,3},{3,2},{4,5},{5,4},{6,7},{7,6},{8,9},{9,8},{10,11... | collective-permute-start | bytes 405512 | tf_op jit(solution)/shard_map/ppermute | solution.py:225
  29.2 1.5 %collective-permute-start.12 = (bf16[16,4224]{1,0:T(8,128)(2,1)S(1)}, bf16[16,4224]{1,0:T(8,128)(2,1)S(1)}, u32[]{:S(2)}, u32[]{:S(2)}) collective-permute-start(bf16[16,4224]{1,0:T(8,128)(2,1)S(1)} %collective-permute-done.3.r_3_), channel_id=1, source_target_pairs={{0,1},{1,0},{2,3},{3,2},{4,5},{5,4},{6,7},{7,6},{8,9},{9,8},{10,11... | collective-permute-start | bytes 405512 | tf_op jit(solution)/shard_map/ppermute | solution.py:225
  35.9 2.0 %collective-permute-start.17 = (bf16[128,2176]{1,0:T(8,128)(2,1)S(1)}, bf16[128,2176]{1,0:T(8,128)(2,1)S(1)}, u32[]{:S(2)}, u32[]{:S(2)}) collective-permute-start(bf16[128,2176]{1,0:T(8,128)(2,1)S(1)} %get-tuple-element.38), channel_id=1, source_target_pairs={{0,1},{1,0},{2,3},{3,2},{4,5},{5,4},{6,7},{7,6},{8,9},{9,8},{10,11... | collective-permute-start | bytes 1671176 | tf_op jit(solution)/shard_map/ppermute | solution.py:225
  52.0 6.2 %collective-permute-start.18 = (bf16[16,2176]{1,0:T(8,128)(2,1)S(1)}, bf16[16,2176]{1,0:T(8,128)(2,1)S(1)}, u32[]{:S(2)}, u32[]{:S(2)}) collective-permute-start(bf16[16,2176]{1,0:T(8,128)(2,1)S(1)} %get-tuple-element.40), channel_id=1, source_target_pairs={{0,6},{2,4},{4,2},{6,0},{1,7},{3,5},{5,3},{7,1},{8,14},{10,12},{12... | collective-permute-start | bytes 208904 | tf_op jit(solution)/shard_map/ppermute | solution.py:222

commit v8 on v7

--- a/solution.py
+++ b/solution.py
@@ -136,44 +136,53 @@
         c.wait()
 
 
-def add_kernel(capacity, me_ref, *refs):
-    out_ref = refs[-1]
+def add_kernel(parts, *refs):
+    outs = refs[parts:]
     total = refs[0][...].astype(F32)
-    for r in refs[1:-1]:
+    for r in refs[1:parts]:
         total = total + r[...].astype(F32)
     total = total.astype(BF16)
-    devices = out_ref.shape[0]
-    for i in range(devices):
-        near, far = (total[j * capacity : (j + 1) * capacity] for j in (i, devices + i))
-        out_ref[me_ref[0] ^ i] = jnp.concatenate([near, far], 0)
-
-
-def combine_kernel(top, capacity, half_ref, back_ref, own_ref, far_ref, own_out, far_out):
-    slots, width = back_ref.shape[0], back_ref.shape[1] - LANES
-    rows = own_ref.shape[0]
+    size = outs[0].shape[0]
+    for i, out_ref in enumerate(outs):
+        out_ref[...] = total[i * size : (i + 1) * size]
+
+
+def combine_kernel(top, capacity, pieces, half_ref, me_ref, *refs):
+    back = jnp.concatenate([r[...] for r in refs[:pieces]], 0)
+    metas, outs = refs[pieces : pieces + 2], refs[pieces + 2 :]
+    slots, width = back.shape[0], back.shape[1] - LANES
+    rows = metas[0].shape[0]
     lane = lax.broadcasted_iota(jnp.int32, (rows, LANES), 1)
     slot = lax.broadcasted_iota(jnp.int32, (rows, slots), 1)
-    device = slot // (2 * capacity)
-    expert = ((device // 2) * 4 + half_ref[0] * 2 + device % 2).astype(F32)
+    plane = (me_ref[0] // 2) ^ (slot // (2 * capacity))
+    expert = (plane * 4 + half_ref[0] * 2 + me_ref[0] % 2).astype(F32)
     place = (slot % capacity).astype(F32)
-    for which, (meta_ref, out_ref) in enumerate(((own_ref, own_out), (far_ref, far_out))):
+    masks, routes = [], []
+    for which, meta_ref in enumerate(metas):
         meta = meta_ref[:, 2 * width :].astype(F32)
         match, held = held_slots(meta, top, expert, place)
         held = jnp.where((slot // capacity) % 2 == which, held, 0.0)
-        dx = dot(held.astype(BF16), back_ref[:, :width], 1, 0)
+        masks.append(held)
+        routes += [jnp.where(m, held, 0.0) for m in match]
+    dx = dot(jnp.concatenate(masks, 0).astype(BF16), back[:, :width], 1, 0)
+    scores = dot(jnp.concatenate(routes, 0).astype(BF16), back[:, width:], 1, 0)
+    for i, out_ref in enumerate(outs):
         probs = jnp.zeros(lane.shape, F32)
         for k in range(top):
-            one = jnp.where(match[k], held, 0.0).astype(BF16)
-            probs = jnp.where(lane == k, dot(one, back_ref[:, width:], 1, 0), probs)
-        out_ref[:, :width] = dx.astype(out_ref.dtype)
+            start = (i * top + k) * rows
+            probs = jnp.where(lane == k, scores[start : start + rows], probs)
+        out_ref[:, :width] = dx[i * rows : (i + 1) * rows].astype(out_ref.dtype)
         out_ref[:, width:] = probs.astype(out_ref.dtype)
 
 
-def final_kernel(own_ref, far_ref, dx_ref, dp_ref):
+def final_kernel(own_ref, *refs):
+    dx_ref, dp_ref = refs[-2:]
     width, top = dx_ref.shape[1], dp_ref.shape[0]
-    dx_ref[...] = (own_ref[:, :width] + far_ref[:, :width].astype(F32)).astype(BF16)
-    probs = (own_ref[:, width:] + far_ref[:, width:].astype(F32)).astype(BF16)
-    dp_ref[...] = dot(lane_map(top, 0), probs, 1, 1)
+    total = own_ref[...]
+    for r in refs[:-2]:
+        total = total + r[...].astype(F32)
+    dx_ref[...] = total[:, :width].astype(BF16)
+    dp_ref[...] = dot(lane_map(top, 0), total[:, width:].astype(BF16), 1, 1)
 
 
 def in_hbm(v):
@@ -201,9 +210,6 @@
     slots = devices * 2 * capacity
     total = slots * parts
     sd = jax.ShapeDtypeStruct
-
-    def within_half(v):
-        return lax.all_to_all(v, ("seq", "zl"), split_axis=0, concat_axis=0, tiled=True)
 
     def within_plane(pieces):
         order = [d for d in reversed(range(1, groups))]
@@ -286,14 +292,14 @@
     dx_parts, (gg, gu, act) = outs[:parts], outs[parts:]
     returned = [dx_parts[0]] + [across(dx_parts[i], -i) for i in range(1, parts)]
     summed = pl.pallas_call(
-        lambda *r: add_kernel(capacity, *r),
-        out_shape=sd((devices, 2 * capacity, width + LANES), BF16),
-        in_specs=[SMEM] + [VMEM] * parts,
-        out_specs=VMEM,
+        lambda *r: add_kernel(parts, *r),
+        out_shape=[sd((2 * capacity, width + LANES), BF16)] * (2 * groups),
+        in_specs=[VMEM] * parts,
+        out_specs=[VMEM] * (2 * groups),
         compiler_params=params(12),
         name="add",
-    )(me, *returned)
-    back = within_half(summed).reshape(slots, width + LANES)
+    )(*returned)
+    far_back, near_back = within_plane(summed[groups:]), within_plane(summed[:groups])
     grad_gu, grad_down = pl.pallas_call(
         lambda *r: weights_kernel(pieces, *r),
         out_shape=[sd(w_gate_up.shape, BF16), sd(w_down.shape, BF16)],
@@ -311,23 +317,29 @@
         ),
         name="weights",
     )(*got, gg, gu, act)
-    own_sum, far_sum = pl.pallas_call(
-        lambda *r: combine_kernel(top, capacity, *r),
-        out_shape=[sd((rows, width + LANES), F32), sd((rows, width + LANES), BF16)],
-        in_specs=[SMEM] + [VMEM] * 3,
-        out_specs=[VMEM] * 2,
-        compiler_params=params(8),
-        name="combine",
-    )(half, back, own, far)
-    home = mirror(far_sum)
+
+    def combine(back, blocks, types, name):
+        return pl.pallas_call(
+            lambda *r: combine_kernel(top, capacity, groups, *r),
+            out_shape=[sd((rows, width + LANES), t) for t in types],
+            in_specs=[SMEM] * 2 + [VMEM] * (groups + 2),
+            out_specs=[VMEM] * 2,
+            compiler_params=params(12),
+            name=name,
+        )(half, me, *back, *blocks)
+
+    far_sum, beyond_sum = combine(far_back, (far, beyond), (BF16, BF16), "combine_far")
+    near_back[0], _ = lax.optimization_barrier((near_back[0], far_sum))
+    own_sum, near_sum = combine(near_back, (own, near), (F32, BF16), "combine_near")
+    home = [mirror(far_sum), across_half(beyond_sum), beside(near_sum)]
     grad_tokens, grad_probs = pl.pallas_call(
         final_kernel,
         out_shape=[sd((rows, width), BF16), sd((top, rows), F32)],
-        in_specs=[VMEM] * 2,
+        in_specs=[VMEM] * 4,
         out_specs=[VMEM] * 2,
         compiler_params=params(4),
         name="final",
-    )(own_sum, home)
+    )(own_sum, *home)
     return grad_tokens, grad_probs.T, grad_gu, grad_down
 
 

time: 59.1 us -> 56.3 us (0.953)
  blocking collectives: 13.3 us -> 0 us
  starting transfers between devices: 17 us -> 26.3 us
  waiting for transfers between devices: 12.3 us -> 13.4 us
    all_to_all x1 -> x0, blocking collectives: 13.3 us -> none  [within_half(): lax.all_to_all(v, ('seq', 'zl'), split_axis=0, concat_axis=0, tiled=True)]
    ppermute x6 -> x12, starting transfers between devices: 7.11 us -> 14.1 us  [within_plane(): lax.ppermute(pieces[d], 'seq', [(i, i ^ d) for i in range(groups)])]
    ppermute x1 -> x2, starting transfers between devices: 3.09 us -> 5.25 us  [beside(): return lax.ppermute(v, 'zl', [(0, 1), (1, 0)])]
    ppermute x6 -> x12, waiting for transfers between devices: 3.11 us -> 4.15 us  [within_plane(): lax.ppermute(pieces[d], 'seq', [(i, i ^ d) for i in range(groups)])]
    ppermute x1 -> x2, waiting for transfers between devices: 2.65 us -> 2.65 us  [beside(): return lax.ppermute(v, 'zl', [(0, 1), (1, 0)])]
    ppermute x1 -> x2, starting transfers between devices: 2.59 us -> 2.59 us  [across_half(): return lax.ppermute(v, ('zh', 'zl'), [(i, i ^ 2) for i in range(4)])]
    ppermute x1 -> x2, waiting for transfers between devices: 3.87 us -> 3.87 us  [across_half(): return lax.ppermute(v, ('zh', 'zl'), [(i, i ^ 2) for i in range(4)])]
  transfers between devices with their start and end apart: 19 -> 27, of which waited for: 8 -> 9; matrix products, arithmetic and copies ran while one was open for 0% -> 0% of each run, Pallas kernels for 13% -> 15%
where the time goes in v8:
time: 56.3 us; the launch traced here: 56.1 us
  starting transfers between devices  26.3 us (47%)
  Pallas kernels  15.6 us (28%)
  waiting for transfers between devices  13.4 us (24%)
  between operations  0.77 us (1%)
    ppermute x12, starting transfers between devices, within_plane(): lax.ppermute(pieces[d], 'seq', [(i, i ^ d) for i in range(groups)])  14.1 us
    pallas_call x1, Pallas kernels, body(): pl.pallas_call(lambda *r: expert_kernel(parts, pieces, *r), out_shape=[sd...  5.27 us
    ppermute x2, starting transfers between devices, beside(): return lax.ppermute(v, 'zl', [(0, 1), (1, 0)])  5.25 us
    ppermute x12, waiting for transfers between devices, within_plane(): lax.ppermute(pieces[d], 'seq', [(i, i ^ d) for i in range(groups)])  4.15 us
    ppermute x2, waiting for transfers between devices, across_half(): return lax.ppermute(v, ('zh', 'zl'), [(i, i ^ 2) for i in range(4)])  3.87 us
    pallas_call x1, Pallas kernels, body(): pl.pallas_call(lambda *r: weights_kernel(pieces, *r), out_shape=[sd(w_gat...  3.86 us
    pallas_call x1, Pallas kernels, body(): pl.pallas_call(stage_kernel, out_shape=pltpu.VMEM(w_gate_up.shape, BF16),...  2.89 us
    ppermute x9, waiting for transfers between devices, across(): lax.ppermute(v, 'slice', [(i, (i + step) % parts) for i in range(parts)])  2.67 us
  transfers between devices with their start and end apart: 27, of which 9 were waited for; matrix products, arithmetic and copies ran while one was open for 0% of the time, Pallas kernels for 15%

profile of v8, /device:TPU:0, one launch (start us, length us, event | category | flops | bytes accessed | tf_op | source)
XLA Modules:
  0.0 56.1 jit_solution(9469539743518103252)
XLA Ops:
  0.6 0.9 %pack.1.r_2_.r_6_ = bf16[16,4224]{1,0:T(8,128)(2,1)S(1)} custom-call(bf16[16,2048]{1,0:T(8,128)(2,1)} %x_hbm.1, bf16[16,2048]{1,0:T(8,128)(2,1)} %dy_hbm.1, s32[6,16]{1,0:T(8,128)} %bitcast.5, bf16[6,16]{1,0:T(8,128)(2,1)} %bitcast.6), custom_call_target="tpu_custom_call" | custom-call | tf_op jit(solution)/shard_map/pack/pallas_call | solution.py:235
  1.6 3.1 %collective-permute-start = (bf16[16,4224]{1,0:T(8,128)(2,1)S(1)}, bf16[16,4224]{1,0:T(8,128)(2,1)S(1)}, u32[]{:S(2)}, u32[]{:S(2)}) collective-permute-start(bf16[16,4224]{1,0:T(8,128)(2,1)S(1)} %pack.1.r_2_.r_6_), channel_id=1, source_target_pairs={{0,2},{2,0},{1,3},{3,1},{4,6},{6,4},{5,7},{7,5},{8,10},{10,8},{9,1... | collective-permute-start | bytes 405512 | tf_op jit(solution)/shard_map/ppermute | solution.py:225
  4.7 2.6 %collective-permute-start.5 = (bf16[16,4224]{1,0:T(8,128)(2,1)S(1)}, bf16[16,4224]{1,0:T(8,128)(2,1)S(1)}, u32[]{:S(2)}, u32[]{:S(2)}) collective-permute-start(bf16[16,4224]{1,0:T(8,128)(2,1)S(1)} %pack.1.r_2_.r_6_), channel_id=1, source_target_pairs={{0,4},{2,6},{4,0},{6,2},{1,5},{3,7},{5,1},{7,3},{8,12},{10,14},{12... | collective-permute-start | bytes 405512 | tf_op jit(solution)/shard_map/ppermute | solution.py:222
  7.3 2.6 %collective-permute-done.r_3_.r_7_ = bf16[16,4224]{1,0:T(8,128)(2,1)S(1)} collective-permute-done((bf16[16,4224]{1,0:T(8,128)(2,1)S(1)}, bf16[16,4224]{1,0:T(8,128)(2,1)S(1)}, u32[]{:S(2)}, u32[]{:S(2)}) %collective-permute-start) | collective-permute-done | bytes 135200 | tf_op jit(solution)/shard_map/ppermute | solution.py:225
  10.4 1.8 %collective-permute-start.1 = (bf16[16,4224]{1,0:T(8,128)(2,1)S(1)}, bf16[16,4224]{1,0:T(8,128)(2,1)S(1)}, u32[]{:S(2)}, u32[]{:S(2)}) collective-permute-start(bf16[16,4224]{1,0:T(8,128)(2,1)S(1)} %get-tuple-element.38), channel_id=1, source_target_pairs={{0,8},{8,0},{16,24},{24,16},{1,9},{9,1},{17,25},{25,17},{2,10},{10... | collective-permute-start | bytes 405512 | tf_op jit(solution)/shard_map/ppermute | solution.py:218
  12.2 1.5 %collective-permute-start.2 = (bf16[16,4224]{1,0:T(8,128)(2,1)S(1)}, bf16[16,4224]{1,0:T(8,128)(2,1)S(1)}, u32[]{:S(2)}, u32[]{:S(2)}) collective-permute-start(bf16[16,4224]{1,0:T(8,128)(2,1)S(1)} %get-tuple-element.39), channel_id=1, source_target_pairs={{0,16},{8,24},{16,0},{24,8},{1,17},{9,25},{17,1},{25,9},{2,18},{10... | collective-permute-start | bytes 405512 | tf_op jit(solution)/shard_map/ppermute | solution.py:218
  14.0 3.9 %collective-permute-done.5.r_3_.r_7_ = bf16[16,4224]{1,0:T(8,128)(2,1)S(1)} collective-permute-done((bf16[16,4224]{1,0:T(8,128)(2,1)S(1)}, bf16[16,4224]{1,0:T(8,128)(2,1)S(1)}, u32[]{:S(2)}, u32[]{:S(2)}) %collective-permute-start.5) | collective-permute-done | bytes 135200 | tf_op jit(solution)/shard_map/ppermute | solution.py:222
  18.4 1.6 %collective-permute-start.6 = (bf16[16,4224]{1,0:T(8,128)(2,1)S(1)}, bf16[16,4224]{1,0:T(8,128)(2,1)S(1)}, u32[]{:S(2)}, u32[]{:S(2)}) collective-permute-start(bf16[16,4224]{1,0:T(8,128)(2,1)S(1)} %get-tuple-element.42), channel_id=1, source_target_pairs={{0,8},{8,0},{16,24},{24,16},{1,9},{9,1},{17,25},{25,17},{2,10},{10... | collective-permute-start | bytes 405512 | tf_op jit(solution)/shard_map/ppermute | solution.py:218
  20.0 1.5 %collective-permute-start.7 = (bf16[16,4224]{1,0:T(8,128)(2,1)S(1)}, bf16[16,4224]{1,0:T(8,128)(2,1)S(1)}, u32[]{:S(2)}, u32[]{:S(2)}) collective-permute-start(bf16[16,4224]{1,0:T(8,128)(2,1)S(1)} %get-tuple-element.43), channel_id=1, source_target_pairs={{0,16},{8,24},{16,0},{24,8},{1,17},{9,25},{17,1},{25,9},{2,18},{10... | collective-permute-start | bytes 405512 | tf_op jit(solution)/shard_map/ppermute | solution.py:218
  22.5 2.9 %stage.1.r_16_ = bf16[1,2,704,2048]{3,2,1,0:T(8,128)(2,1)S(1)} custom-call(bf16[1,2,704,2048]{3,2,1,0:T(8,128)(2,1)} %src_hbm), custom_call_target="tpu_custom_call" | custom-call | bytes 11534336 | tf_op jit(solution)/shard_map/stage/pallas_call | solution.py:265
  25.5 3.1 %collective-permute-done.7.r_6_ = bf16[16,4224]{1,0:T(8,128)(2,1)S(1)} collective-permute-done((bf16[16,4224]{1,0:T(8,128)(2,1)S(1)}, bf16[16,4224]{1,0:T(8,128)(2,1)S(1)}, u32[]{:S(2)}, u32[]{:S(2)}) %collective-permute-start.7) | collective-permute-done | bytes 135200 | tf_op jit(solution)/shard_map/ppermute | solution.py:218
  30.7 5.3 %expert.1 = (bf16[128,2176]{1,0:T(8,128)(2,1)S(1)}, bf16[128,2176]{1,0:T(8,128)(2,1)S(1)}, bf16[256,704]{1,0:T(8,128)(2,1)S(1)}, bf16[256,704]{1,0:T(8,128)(2,1)S(1)}, bf16[256,704]{1,0:T(8,128)(2,1)S(1)}) custom-call(bf16[16,4224]{1,0:T(8,128)(2,1)S(1)} %get-tuple-element.37.r_0_, bf16[16,4224]{1,0:T(8,128)(2,1)S(1)} %collective-permute-done.1.r_1_, ...), custom_call_target="tpu_custom_call" | custom-call | tf_op jit(solution)/shard_map/expert/pallas_call | solution.py:284
  36.3 1.6 %collective-permute-done.17.r_1_ = bf16[128,2176]{1,0:T(8,128)(2,1)S(1)} collective-permute-done((bf16[128,2176]{1,0:T(8,128)(2,1)S(1)}, bf16[128,2176]{1,0:T(8,128)(2,1)S(1)}, u32[]{:S(2)}, u32[]{:S(2)}) %collective-permute-start.17) | collective-permute-done | bytes 557088 | tf_op jit(solution)/shard_map/ppermute | solution.py:231
  38.1 1.1 %collective-permute-start.18 = (bf16[16,2176]{1,0:T(8,128)(2,1)S(1)}, bf16[16,2176]{1,0:T(8,128)(2,1)S(1)}, u32[]{:S(2)}, u32[]{:S(2)}) collective-permute-start(bf16[16,2176]{1,0:T(8,128)(2,1)S(1)} %get-tuple-element.52), channel_id=1, source_target_pairs={{0,8},{8,0},{16,24},{24,16},{1,9},{9,1},{17,25},{25,17},{2,10},{10... | collective-permute-start | bytes 208904 | tf_op jit(solution)/shard_map/ppermute | solution.py:218
  39.2 1.0 %collective-permute-start.19 = (bf16[16,2176]{1,0:T(8,128)(2,1)S(1)}, bf16[16,2176]{1,0:T(8,128)(2,1)S(1)}, u32[]{:S(2)}, u32[]{:S(2)}) collective-permute-start(bf16[16,2176]{1,0:T(8,128)(2,1)S(1)} %get-tuple-element.53), channel_id=1, source_target_pairs={{0,16},{8,24},{16,0},{24,8},{1,17},{9,25},{17,1},{25,9},{2,18},{10... | collective-permute-start | bytes 208904 | tf_op jit(solution)/shard_map/ppermute | solution.py:218
  40.2 1.4 %collective-permute-start.20 = (bf16[16,2176]{1,0:T(8,128)(2,1)S(1)}, bf16[16,2176]{1,0:T(8,128)(2,1)S(1)}, u32[]{:S(2)}, u32[]{:S(2)}) collective-permute-start(bf16[16,2176]{1,0:T(8,128)(2,1)S(1)} %get-tuple-element.54), channel_id=1, source_target_pairs={{0,24},{8,16},{16,8},{24,0},{1,25},{9,17},{17,9},{25,1},{2,26},{10... | collective-permute-start | bytes 208904 | tf_op jit(solution)/shard_map/ppermute | solution.py:218
  41.6 1.0 %collective-permute-start.21 = (bf16[16,2176]{1,0:T(8,128)(2,1)S(1)}, bf16[16,2176]{1,0:T(8,128)(2,1)S(1)}, u32[]{:S(2)}, u32[]{:S(2)}) collective-permute-start(bf16[16,2176]{1,0:T(8,128)(2,1)S(1)} %get-tuple-element.57), channel_id=1, source_target_pairs={{0,8},{8,0},{16,24},{24,16},{1,9},{9,1},{17,25},{25,17},{2,10},{10... | collective-permute-start | bytes 208904 | tf_op jit(solution)/shard_map/ppermute | solution.py:218
  42.7 1.0 %collective-permute-start.22 = (bf16[16,2176]{1,0:T(8,128)(2,1)S(1)}, bf16[16,2176]{1,0:T(8,128)(2,1)S(1)}, u32[]{:S(2)}, u32[]{:S(2)}) collective-permute-start(bf16[16,2176]{1,0:T(8,128)(2,1)S(1)} %get-tuple-element.58), channel_id=1, source_target_pairs={{0,16},{8,24},{16,0},{24,8},{1,17},{9,25},{17,1},{25,9},{2,18},{10... | collective-permute-start | bytes 208904 | tf_op jit(solution)/shard_map/ppermute | solution.py:218
  43.7 1.4 %collective-permute-start.23 = (bf16[16,2176]{1,0:T(8,128)(2,1)S(1)}, bf16[16,2176]{1,0:T(8,128)(2,1)S(1)}, u32[]{:S(2)}, u32[]{:S(2)}) collective-permute-start(bf16[16,2176]{1,0:T(8,128)(2,1)S(1)} %get-tuple-element.59), channel_id=1, source_target_pairs={{0,24},{8,16},{16,8},{24,0},{1,25},{9,17},{17,9},{25,1},{2,26},{10... | collective-permute-start | bytes 208904 | tf_op jit(solution)/shard_map/ppermute | solution.py:218
  45.1 1.0 %collective-permute-done.20.r_5_ = bf16[16,2176]{1,0:T(8,128)(2,1)S(1)} collective-permute-done((bf16[16,2176]{1,0:T(8,128)(2,1)S(1)}, bf16[16,2176]{1,0:T(8,128)(2,1)S(1)}, u32[]{:S(2)}, u32[]{:S(2)}) %collective-permute-start.20) | collective-permute-done | bytes 69664 | tf_op jit(solution)/shard_map/ppermute | solution.py:218
  46.5 2.3 %collective-permute-start.24 = (bf16[16,2176]{1,0:T(8,128)(2,1)S(1)}, bf16[16,2176]{1,0:T(8,128)(2,1)S(1)}, u32[]{:S(2)}, u32[]{:S(2)}) collective-permute-start(bf16[16,2176]{1,0:T(8,128)(2,1)S(1)} %get-tuple-element.55), channel_id=1, source_target_pairs={{0,6},{2,4},{4,2},{6,0},{1,7},{3,5},{5,3},{7,1},{8,14},{10,12},{12... | collective-permute-start | bytes 208904 | tf_op jit(solution)/shard_map/ppermute | solution.py:228
  49.3 2.2 %collective-permute-start.26 = (bf16[16,2176]{1,0:T(8,128)(2,1)S(1)}, bf16[16,2176]{1,0:T(8,128)(2,1)S(1)}, u32[]{:S(2)}, u32[]{:S(2)}) collective-permute-start(bf16[16,2176]{1,0:T(8,128)(2,1)S(1)} %get-tuple-element.62), channel_id=1, source_target_pairs={{0,2},{2,0},{1,3},{3,1},{4,6},{6,4},{5,7},{7,5},{8,10},{10,8},{9,1... | collective-permute-start | bytes 208904 | tf_op jit(solution)/shard_map/ppermute | solution.py:225
  51.5 3.9 %weights.1 = (bf16[1,2,704,2048]{3,2,1,0:T(8,128)(2,1)}, bf16[1,704,2048]{2,1,0:T(8,128)(2,1)}) custom-call(bf16[16,4224]{1,0:T(8,128)(2,1)S(1)} %get-tuple-element.37.r_0_, bf16[16,4224]{1,0:T(8,128)(2,1)S(1)} %collective-permute-done.1.r_1_, bf16[16,4224]{1,0:T(8,128)(2,1)S(1)} %collective-permute-done.2.r_2_, ...), custom_call_target="tpu_custom_call" | custom-call | flops 2214592512 | bytes 14417920 | tf_op jit(solution)/shard_map/weights/pallas_call | solution.py:303
  55.4 0.7 %final.1 = (bf16[16,2048]{1,0:T(8,128)(2,1)}, f32[6,16]{1,0:T(8,128)}) custom-call(f32[16,2176]{1,0:T(8,128)S(1)} %get-tuple-element.60.own_ref, bf16[16,2176]{1,0:T(8,128)(2,1)S(1)} %collective-permute-done.24.refs_0_, bf16[16,2176]{1,0:T(8,128)(2,1)S(1)} %collective-permute-done.25.refs_1_, bf16[16,2176]{1,0:T(8,128)(2,1)S(1)} %collective-permute-done.26.refs_2_), custom_call_target="tpu_custom_call" | custom-call | tf_op jit(solution)/shard_map/final/pallas_call | solution.py:335
  (42 shorter events, 5.8 us)
Async XLA Ops:
  1.6 8.3 %collective-permute-start = (bf16[16,4224]{1,0:T(8,128)(2,1)S(1)}, bf16[16,4224]{1,0:T(8,128)(2,1)S(1)}, u32[]{:S(2)}, u32[]{:S(2)}) collective-permute-start(bf16[16,4224]{1,0:T(8,128)(2,1)S(1)} %pack.1.r_2_.r_6_), channel_id=1, source_target_pairs={{0,2},{2,0},{1,3},{3,1},{4,6},{6,4},{5,7},{7,5},{8,10},{10,8},{9,1... | collective-permute-start | bytes 405512 | tf_op jit(solution)/shard_map/ppermute | solution.py:225
  4.7 13.2 %collective-permute-start.5 = (bf16[16,4224]{1,0:T(8,128)(2,1)S(1)}, bf16[16,4224]{1,0:T(8,128)(2,1)S(1)}, u32[]{:S(2)}, u32[]{:S(2)}) collective-permute-start(bf16[16,4224]{1,0:T(8,128)(2,1)S(1)} %pack.1.r_2_.r_6_), channel_id=1, source_target_pairs={{0,4},{2,6},{4,0},{6,2},{1,5},{3,7},{5,1},{7,3},{8,12},{10,14},{12... | collective-permute-start | bytes 405512 | tf_op jit(solution)/shard_map/ppermute | solution.py:222
  7.3 10.6 %collective-permute-start.4 = (bf16[16,4224]{1,0:T(8,128)(2,1)S(1)}, bf16[16,4224]{1,0:T(8,128)(2,1)S(1)}, u32[]{:S(2)}, u32[]{:S(2)}) collective-permute-start(bf16[16,4224]{1,0:T(8,128)(2,1)S(1)} %pack.1.r_2_.r_6_), channel_id=1, source_target_pairs={{0,6},{2,4},{4,2},{6,0},{1,7},{3,5},{5,3},{7,1},{8,14},{10,12},{12... | collective-permute-start | bytes 405512 | tf_op jit(solution)/shard_map/ppermute | solution.py:228
  10.4 9.5 %collective-permute-start.1 = (bf16[16,4224]{1,0:T(8,128)(2,1)S(1)}, bf16[16,4224]{1,0:T(8,128)(2,1)S(1)}, u32[]{:S(2)}, u32[]{:S(2)}) collective-permute-start(bf16[16,4224]{1,0:T(8,128)(2,1)S(1)} %get-tuple-element.38), channel_id=1, source_target_pairs={{0,8},{8,0},{16,24},{24,16},{1,9},{9,1},{17,25},{25,17},{2,10},{10... | collective-permute-start | bytes 405512 | tf_op jit(solution)/shard_map/ppermute | solution.py:218
  12.2 9.3 %collective-permute-start.2 = (bf16[16,4224]{1,0:T(8,128)(2,1)S(1)}, bf16[16,4224]{1,0:T(8,128)(2,1)S(1)}, u32[]{:S(2)}, u32[]{:S(2)}) collective-permute-start(bf16[16,4224]{1,0:T(8,128)(2,1)S(1)} %get-tuple-element.39), channel_id=1, source_target_pairs={{0,16},{8,24},{16,0},{24,8},{1,17},{9,25},{17,1},{25,9},{2,18},{10... | collective-permute-start | bytes 405512 | tf_op jit(solution)/shard_map/ppermute | solution.py:218
  13.7 8.2 %collective-permute-start.3 = (bf16[16,4224]{1,0:T(8,128)(2,1)S(1)}, bf16[16,4224]{1,0:T(8,128)(2,1)S(1)}, u32[]{:S(2)}, u32[]{:S(2)}) collective-permute-start(bf16[16,4224]{1,0:T(8,128)(2,1)S(1)} %get-tuple-element.40), channel_id=1, source_target_pairs={{0,24},{8,16},{16,8},{24,0},{1,25},{9,17},{17,9},{25,1},{2,26},{10... | collective-permute-start | bytes 405512 | tf_op jit(solution)/shard_map/ppermute | solution.py:218
  17.9 4.1 %collective-permute-start.9 = (bf16[16,4224]{1,0:T(8,128)(2,1)S(1)}, bf16[16,4224]{1,0:T(8,128)(2,1)S(1)}, u32[]{:S(2)}, u32[]{:S(2)}) collective-permute-start(bf16[16,4224]{1,0:T(8,128)(2,1)S(1)} %get-tuple-element.37.r_0_), channel_id=1, source_target_pairs={{0,1},{1,0},{2,3},{3,2},{4,5},{5,4},{6,7},{7,6},{8,9},{9,8},{10,11... | collective-permute-start | bytes 405512 | tf_op jit(solution)/shard_map/ppermute | solution.py:231
  18.4 7.0 %collective-permute-start.6 = (bf16[16,4224]{1,0:T(8,128)(2,1)S(1)}, bf16[16,4224]{1,0:T(8,128)(2,1)S(1)}, u32[]{:S(2)}, u32[]{:S(2)}) collective-permute-start(bf16[16,4224]{1,0:T(8,128)(2,1)S(1)} %get-tuple-element.42), channel_id=1, source_target_pairs={{0,8},{8,0},{16,24},{24,16},{1,9},{9,1},{17,25},{25,17},{2,10},{10... | collective-permute-start | bytes 405512 | tf_op jit(solution)/shard_map/ppermute | solution.py:218
  20.0 8.6 %collective-permute-start.7 = (bf16[16,4224]{1,0:T(8,128)(2,1)S(1)}, bf16[16,4224]{1,0:T(8,128)(2,1)S(1)}, u32[]{:S(2)}, u32[]{:S(2)}) collective-permute-start(bf16[16,4224]{1,0:T(8,128)(2,1)S(1)} %get-tuple-element.43), channel_id=1, source_target_pairs={{0,16},{8,24},{16,0},{24,8},{1,17},{9,25},{17,1},{25,9},{2,18},{10... | collective-permute-start | bytes 405512 | tf_op jit(solution)/shard_map/ppermute | solution.py:218
  21.5 7.1 %collective-permute-start.8 = (bf16[16,4224]{1,0:T(8,128)(2,1)S(1)}, bf16[16,4224]{1,0:T(8,128)(2,1)S(1)}, u32[]{:S(2)}, u32[]{:S(2)}) collective-permute-start(bf16[16,4224]{1,0:T(8,128)(2,1)S(1)} %get-tuple-element.44), channel_id=1, source_target_pairs={{0,24},{8,16},{16,8},{24,0},{1,25},{9,17},{17,9},{25,1},{2,26},{10... | collective-permute-start | bytes 405512 | tf_op jit(solution)/shard_map/ppermute | solution.py:218
  22.0 7.1 %collective-permute-start.13 = (bf16[16,4224]{1,0:T(8,128)(2,1)S(1)}, bf16[16,4224]{1,0:T(8,128)(2,1)S(1)}, u32[]{:S(2)}, u32[]{:S(2)}) collective-permute-start(bf16[16,4224]{1,0:T(8,128)(2,1)S(1)} %get-tuple-element.41.r_4_), channel_id=1, source_target_pairs={{0,1},{1,0},{2,3},{3,2},{4,5},{5,4},{6,7},{7,6},{8,9},{9,8},{10,11... | collective-permute-start | bytes 405512 | tf_op jit(solution)/shard_map/ppermute | solution.py:231
  22.0 7.2 %collective-permute-start.10 = (bf16[16,4224]{1,0:T(8,128)(2,1)S(1)}, bf16[16,4224]{1,0:T(8,128)(2,1)S(1)}, u32[]{:S(2)}, u32[]{:S(2)}) collective-permute-start(bf16[16,4224]{1,0:T(8,128)(2,1)S(1)} %collective-permute-done.1.r_1_), channel_id=1, source_target_pairs={{0,1},{1,0},{2,3},{3,2},{4,5},{5,4},{6,7},{7,6},{8,9},{9,8},{10,11... | collective-permute-start | bytes 405512 | tf_op jit(solution)/shard_map/ppermute | solution.py:231
  25.4 4.2 %collective-permute-start.11 = (bf16[16,4224]{1,0:T(8,128)(2,1)S(1)}, bf16[16,4224]{1,0:T(8,128)(2,1)S(1)}, u32[]{:S(2)}, u32[]{:S(2)}) collective-permute-start(bf16[16,4224]{1,0:T(8,128)(2,1)S(1)} %collective-permute-done.2.r_2_), channel_id=1, source_target_pairs={{0,1},{1,0},{2,3},{3,2},{4,5},{5,4},{6,7},{7,6},{8,9},{9,8},{10,11... | collective-permute-start | bytes 405512 | tf_op jit(solution)/shard_map/ppermute | solution.py:231
  28.6 1.5 %collective-permute-start.15 = (bf16[16,4224]{1,0:T(8,128)(2,1)S(1)}, bf16[16,4224]{1,0:T(8,128)(2,1)S(1)}, u32[]{:S(2)}, u32[]{:S(2)}) collective-permute-start(bf16[16,4224]{1,0:T(8,128)(2,1)S(1)} %collective-permute-done.7.r_6_), channel_id=1, source_target_pairs={{0,1},{1,0},{2,3},{3,2},{4,5},{5,4},{6,7},{7,6},{8,9},{9,8},{10,11... | collective-permute-start | bytes 405512 | tf_op jit(solution)/shard_map/ppermute | solution.py:231
  35.9 2.0 %collective-permute-start.17 = (bf16[128,2176]{1,0:T(8,128)(2,1)S(1)}, bf16[128,2176]{1,0:T(8,128)(2,1)S(1)}, u32[]{:S(2)}, u32[]{:S(2)}) collective-permute-start(bf16[128,2176]{1,0:T(8,128)(2,1)S(1)} %get-tuple-element.49), channel_id=1, source_target_pairs={{0,1},{1,0},{2,3},{3,2},{4,5},{5,4},{6,7},{7,6},{8,9},{9,8},{10,11... | collective-permute-start | bytes 1671176 | tf_op jit(solution)/shard_map/ppermute | solution.py:231
  38.1 5.6 %collective-permute-start.18 = (bf16[16,2176]{1,0:T(8,128)(2,1)S(1)}, bf16[16,2176]{1,0:T(8,128)(2,1)S(1)}, u32[]{:S(2)}, u32[]{:S(2)}) collective-permute-start(bf16[16,2176]{1,0:T(8,128)(2,1)S(1)} %get-tuple-element.52), channel_id=1, source_target_pairs={{0,8},{8,0},{16,24},{24,16},{1,9},{9,1},{17,25},{25,17},{2,10},{10... | collective-permute-start | bytes 208904 | tf_op jit(solution)/shard_map/ppermute | solution.py:218
  39.2 5.9 %collective-permute-start.19 = (bf16[16,2176]{1,0:T(8,128)(2,1)S(1)}, bf16[16,2176]{1,0:T(8,128)(2,1)S(1)}, u32[]{:S(2)}, u32[]{:S(2)}) collective-permute-start(bf16[16,2176]{1,0:T(8,128)(2,1)S(1)} %get-tuple-element.53), channel_id=1, source_target_pairs={{0,16},{8,24},{16,0},{24,8},{1,17},{9,25},{17,1},{25,9},{2,18},{10... | collective-permute-start | bytes 208904 | tf_op jit(solution)/shard_map/ppermute | solution.py:218
  40.2 5.9 %collective-permute-start.20 = (bf16[16,2176]{1,0:T(8,128)(2,1)S(1)}, bf16[16,2176]{1,0:T(8,128)(2,1)S(1)}, u32[]{:S(2)}, u32[]{:S(2)}) collective-permute-start(bf16[16,2176]{1,0:T(8,128)(2,1)S(1)} %get-tuple-element.54), channel_id=1, source_target_pairs={{0,24},{8,16},{16,8},{24,0},{1,25},{9,17},{17,9},{25,1},{2,26},{10... | collective-permute-start | bytes 208904 | tf_op jit(solution)/shard_map/ppermute | solution.py:218
  41.6 7.2 %collective-permute-start.21 = (bf16[16,2176]{1,0:T(8,128)(2,1)S(1)}, bf16[16,2176]{1,0:T(8,128)(2,1)S(1)}, u32[]{:S(2)}, u32[]{:S(2)}) collective-permute-start(bf16[16,2176]{1,0:T(8,128)(2,1)S(1)} %get-tuple-element.57), channel_id=1, source_target_pairs={{0,8},{8,0},{16,24},{24,16},{1,9},{9,1},{17,25},{25,17},{2,10},{10... | collective-permute-start | bytes 208904 | tf_op jit(solution)/shard_map/ppermute | solution.py:218
  42.7 6.2 %collective-permute-start.22 = (bf16[16,2176]{1,0:T(8,128)(2,1)S(1)}, bf16[16,2176]{1,0:T(8,128)(2,1)S(1)}, u32[]{:S(2)}, u32[]{:S(2)}) collective-permute-start(bf16[16,2176]{1,0:T(8,128)(2,1)S(1)} %get-tuple-element.58), channel_id=1, source_target_pairs={{0,16},{8,24},{16,0},{24,8},{1,17},{9,25},{17,1},{25,9},{2,18},{10... | collective-permute-start | bytes 208904 | tf_op jit(solution)/shard_map/ppermute | solution.py:218
  43.7 5.2 %collective-permute-start.23 = (bf16[16,2176]{1,0:T(8,128)(2,1)S(1)}, bf16[16,2176]{1,0:T(8,128)(2,1)S(1)}, u32[]{:S(2)}, u32[]{:S(2)}) collective-permute-start(bf16[16,2176]{1,0:T(8,128)(2,1)S(1)} %get-tuple-element.59), channel_id=1, source_target_pairs={{0,24},{8,16},{16,8},{24,0},{1,25},{9,17},{17,9},{25,1},{2,26},{10... | collective-permute-start | bytes 208904 | tf_op jit(solution)/shard_map/ppermute | solution.py:218
  46.5 8.8 %collective-permute-start.24 = (bf16[16,2176]{1,0:T(8,128)(2,1)S(1)}, bf16[16,2176]{1,0:T(8,128)(2,1)S(1)}, u32[]{:S(2)}, u32[]{:S(2)}) collective-permute-start(bf16[16,2176]{1,0:T(8,128)(2,1)S(1)} %get-tuple-element.55), channel_id=1, source_target_pairs={{0,6},{2,4},{4,2},{6,0},{1,7},{3,5},{5,3},{7,1},{8,14},{10,12},{12... | collective-permute-start | bytes 208904 | tf_op jit(solution)/shard_map/ppermute | solution.py:228
  48.9 6.4 %collective-permute-start.25 = (bf16[16,2176]{1,0:T(8,128)(2,1)S(1)}, bf16[16,2176]{1,0:T(8,128)(2,1)S(1)}, u32[]{:S(2)}, u32[]{:S(2)}) collective-permute-start(bf16[16,2176]{1,0:T(8,128)(2,1)S(1)} %get-tuple-element.61), channel_id=1, source_target_pairs={{0,4},{2,6},{4,0},{6,2},{1,5},{3,7},{5,1},{7,3},{8,12},{10,14},{12... | collective-permute-start | bytes 208904 | tf_op jit(solution)/shard_map/ppermute | solution.py:222
  49.3 6.1 %collective-permute-start.26 = (bf16[16,2176]{1,0:T(8,128)(2,1)S(1)}, bf16[16,2176]{1,0:T(8,128)(2,1)S(1)}, u32[]{:S(2)}, u32[]{:S(2)}) collective-permute-start(bf16[16,2176]{1,0:T(8,128)(2,1)S(1)} %get-tuple-element.62), channel_id=1, source_target_pairs={{0,2},{2,0},{1,3},{3,1},{4,6},{6,4},{5,7},{7,5},{8,10},{10,8},{9,1... | collective-permute-start | bytes 208904 | tf_op jit(solution)/shard_map/ppermute | solution.py:225
  (4 other events, 12.9 us)

commit v9 on v8

--- a/solution.py
+++ b/solution.py
@@ -115,24 +115,34 @@
         dx_out[i][:, width:] = score_col[i * slots : (i + 1) * slots]
 
 
-def weights_kernel(parts, *refs):
-    got = refs[:parts]
-    gg_ref, gu_ref, act_ref, dgu_hbm, dd_hbm, buf, sems = refs[parts:]
-    hidden, width = buf.shape[1:]
-    xs = jnp.concatenate([r[:, :width] for r in got], 0)
+def leave_in_chunks(lhs_ref, rhs, buf, out, sems):
+    hidden, copies = buf.shape[0], []
+    for j, start in enumerate(range(0, hidden, LANES)):
+        cut = pl.ds(start, min(LANES, hidden - start))
+        stop = min(start + LANES, hidden)
+        buf[start:stop, :] = dot(lhs_ref[:, start:stop], rhs, 0, 0).astype(BF16)
+        copies.append(pltpu.make_async_copy(buf.at[cut], out.at[cut], sems.at[j]))
+        copies[-1].start()
+    return copies
+
+
+def gate_up_kernel(pieces, *refs):
+    gg_ref, gu_ref, out_hbm, buf, sems = refs[pieces:]
+    xs = jnp.concatenate([r[:, : buf.shape[2]] for r in refs[:pieces]], 0)
+    copies = []
+    for i, lhs_ref in enumerate((gg_ref, gu_ref)):
+        copies += leave_in_chunks(lhs_ref, xs, buf.at[i], out_hbm.at[0, i], sems.at[i])
+    for c in copies:
+        c.wait()
+
+
+def down_kernel(pieces, *refs):
+    act_ref, out_hbm, buf, sems = refs[pieces:]
+    got, width = refs[:pieces], buf.shape[1]
     weight = jnp.concatenate([r[:, 2 * width :] for r in got], 0).astype(F32)[:, 0:1]
     dys = jnp.concatenate([r[:, width : 2 * width] for r in got], 0)
     scaled = (weight * dys.astype(F32)).astype(BF16)
-    outs = ((gg_ref, xs, dgu_hbm.at[0, 0]), (gu_ref, xs, dgu_hbm.at[0, 1]), (act_ref, scaled, dd_hbm.at[0]))
-    copies = []
-    for i, (lhs_ref, rhs, out) in enumerate(outs):
-        for j, start in enumerate(range(0, hidden, LANES)):
-            size = min(LANES, hidden - start)
-            buf[i, start : start + size, :] = dot(lhs_ref[:, start : start + size], rhs, 0, 0).astype(BF16)
-            cut = pl.ds(start, size)
-            copies.append(pltpu.make_async_copy(buf.at[i, cut], out.at[cut], sems.at[i, j]))
-            copies[-1].start()
-    for c in copies:
+    for c in leave_in_chunks(act_ref, scaled, buf, out_hbm.at[0], sems):
         c.wait()
 
 
@@ -291,6 +301,19 @@
     )(*got, staged, w_down)
     dx_parts, (gg, gu, act) = outs[:parts], outs[parts:]
     returned = [dx_parts[0]] + [across(dx_parts[i], -i) for i in range(1, parts)]
+    grad_down = pl.pallas_call(
+        lambda *r: down_kernel(pieces, *r),
+        out_shape=sd(w_down.shape, BF16),
+        in_specs=[VMEM] * (pieces + 1),
+        out_specs=ANY,
+        scratch_shapes=[pltpu.VMEM((hidden, width), BF16), pltpu.SemaphoreType.DMA((-(-hidden // LANES),))],
+        compiler_params=params(30),
+        cost_estimate=pl.CostEstimate(
+            flops=2 * hidden * total * width, bytes_accessed=4 * hidden * width, transcendentals=0
+        ),
+        name="down",
+    )(*got, act)
+    returned[0], grad_down = lax.optimization_barrier((returned[0], grad_down))
     summed = pl.pallas_call(
         lambda *r: add_kernel(parts, *r),
         out_shape=[sd((2 * capacity, width + LANES), BF16)] * (2 * groups),
@@ -300,23 +323,19 @@
         name="add",
     )(*returned)
     far_back, near_back = within_plane(summed[groups:]), within_plane(summed[:groups])
-    grad_gu, grad_down = pl.pallas_call(
-        lambda *r: weights_kernel(pieces, *r),
-        out_shape=[sd(w_gate_up.shape, BF16), sd(w_down.shape, BF16)],
-        in_specs=[VMEM] * (pieces + 3),
-        out_specs=[ANY] * 2,
-        scratch_shapes=[
-            pltpu.VMEM((3, hidden, width), BF16),
-            pltpu.SemaphoreType.DMA((3, -(-hidden // LANES))),
-        ],
-        compiler_params=params(40),
+    chunks = -(-hidden // LANES)
+    grad_gu = pl.pallas_call(
+        lambda *r: gate_up_kernel(pieces, *r),
+        out_shape=sd(w_gate_up.shape, BF16),
+        in_specs=[VMEM] * (pieces + 2),
+        out_specs=ANY,
+        scratch_shapes=[pltpu.VMEM((2, hidden, width), BF16), pltpu.SemaphoreType.DMA((2, chunks))],
+        compiler_params=params(30),
         cost_estimate=pl.CostEstimate(
-            flops=6 * hidden * total * width,
-            bytes_accessed=10 * hidden * width,
-            transcendentals=0,
+            flops=4 * hidden * total * width, bytes_accessed=8 * hidden * width, transcendentals=0
         ),
-        name="weights",
-    )(*got, gg, gu, act)
+        name="gate_up",
+    )(*got, gg, gu)
 
     def combine(back, blocks, types, name):
         return pl.pallas_call(

time: 56.3 us -> 55.9 us (level)
  waiting for transfers between devices: 13.4 us -> 12 us
  Pallas kernels: 15.6 us -> 16.7 us
    ppermute x9, waiting for transfers between devices: 2.67 us -> 1.04 us  [across(): lax.ppermute(v, 'slice', [(i, (i + step) % parts) for i in range(parts)])]
    pallas_call x1 -> x2, Pallas kernels: 3.86 us -> 4.99 us  [the longest x1 2.93 us: body(): pl.pallas_call(lambda *r: gate_up_kernel(pieces, *r), out_shape=sd(w_gate...]
  transfers between devices with their start and end apart: 27 -> 27, of which waited for: 9 -> 10; matrix products, arithmetic and copies ran while one was open for 0% -> 0% of each run, Pallas kernels for 15% -> 17%
where the time goes in v9:
time: 55.9 us; the launch traced here: 55.7 us
  starting transfers between devices  26.2 us (47%)
  Pallas kernels  16.7 us (30%)
  waiting for transfers between devices  12 us (21%)
  between operations  0.77 us (1%)
    ppermute x12, starting transfers between devices, within_plane(): lax.ppermute(pieces[d], 'seq', [(i, i ^ d) for i in range(groups)])  14.1 us
    pallas_call x1, Pallas kernels, body(): pl.pallas_call(lambda *r: expert_kernel(parts, pieces, *r), out_shape=[sd...  5.26 us
    ppermute x2, starting transfers between devices, beside(): return lax.ppermute(v, 'zl', [(0, 1), (1, 0)])  5.14 us
    ppermute x12, waiting for transfers between devices, within_plane(): lax.ppermute(pieces[d], 'seq', [(i, i ^ d) for i in range(groups)])  4.16 us
    ppermute x2, waiting for transfers between devices, across_half(): return lax.ppermute(v, ('zh', 'zl'), [(i, i ^ 2) for i in range(4)])  4.15 us
    pallas_call x1, Pallas kernels, body(): pl.pallas_call(lambda *r: gate_up_kernel(pieces, *r), out_shape=sd(w_gate...  2.93 us
    pallas_call x1, Pallas kernels, body(): pl.pallas_call(stage_kernel, out_shape=pltpu.VMEM(w_gate_up.shape, BF16),...  2.89 us
    ppermute x2, waiting for transfers between devices, beside(): return lax.ppermute(v, 'zl', [(0, 1), (1, 0)])  2.65 us
  transfers between devices with their start and end apart: 27, of which 10 were waited for; matrix products, arithmetic and copies ran while one was open for 0% of the time, Pallas kernels for 17%

profile of v9, /device:TPU:0, one launch (start us, length us, event | category | flops | bytes accessed | tf_op | source)
XLA Modules:
  0.0 55.7 jit_solution(6543293977242861773)
XLA Ops:
  0.6 0.9 %pack.1.r_2_.r_6_ = bf16[16,4224]{1,0:T(8,128)(2,1)S(1)} custom-call(bf16[16,2048]{1,0:T(8,128)(2,1)} %x_hbm.1, bf16[16,2048]{1,0:T(8,128)(2,1)} %dy_hbm.1, s32[6,16]{1,0:T(8,128)} %bitcast.5, bf16[6,16]{1,0:T(8,128)(2,1)} %bitcast.6), custom_call_target="tpu_custom_call" | custom-call | tf_op jit(solution)/shard_map/pack/pallas_call | solution.py:245
  1.6 3.1 %collective-permute-start = (bf16[16,4224]{1,0:T(8,128)(2,1)S(1)}, bf16[16,4224]{1,0:T(8,128)(2,1)S(1)}, u32[]{:S(2)}, u32[]{:S(2)}) collective-permute-start(bf16[16,4224]{1,0:T(8,128)(2,1)S(1)} %pack.1.r_2_.r_6_), channel_id=1, source_target_pairs={{0,2},{2,0},{1,3},{3,1},{4,6},{6,4},{5,7},{7,5},{8,10},{10,8},{9,1... | collective-permute-start | bytes 405512 | tf_op jit(solution)/shard_map/ppermute | solution.py:235
  4.7 2.6 %collective-permute-start.5 = (bf16[16,4224]{1,0:T(8,128)(2,1)S(1)}, bf16[16,4224]{1,0:T(8,128)(2,1)S(1)}, u32[]{:S(2)}, u32[]{:S(2)}) collective-permute-start(bf16[16,4224]{1,0:T(8,128)(2,1)S(1)} %pack.1.r_2_.r_6_), channel_id=1, source_target_pairs={{0,4},{2,6},{4,0},{6,2},{1,5},{3,7},{5,1},{7,3},{8,12},{10,14},{12... | collective-permute-start | bytes 405512 | tf_op jit(solution)/shard_map/ppermute | solution.py:232
  7.3 2.6 %collective-permute-done.r_3_.r_7_ = bf16[16,4224]{1,0:T(8,128)(2,1)S(1)} collective-permute-done((bf16[16,4224]{1,0:T(8,128)(2,1)S(1)}, bf16[16,4224]{1,0:T(8,128)(2,1)S(1)}, u32[]{:S(2)}, u32[]{:S(2)}) %collective-permute-start) | collective-permute-done | bytes 135200 | tf_op jit(solution)/shard_map/ppermute | solution.py:235
  10.4 1.8 %collective-permute-start.1 = (bf16[16,4224]{1,0:T(8,128)(2,1)S(1)}, bf16[16,4224]{1,0:T(8,128)(2,1)S(1)}, u32[]{:S(2)}, u32[]{:S(2)}) collective-permute-start(bf16[16,4224]{1,0:T(8,128)(2,1)S(1)} %get-tuple-element.38), channel_id=1, source_target_pairs={{0,8},{8,0},{16,24},{24,16},{1,9},{9,1},{17,25},{25,17},{2,10},{10... | collective-permute-start | bytes 405512 | tf_op jit(solution)/shard_map/ppermute | solution.py:228
  12.2 1.5 %collective-permute-start.2 = (bf16[16,4224]{1,0:T(8,128)(2,1)S(1)}, bf16[16,4224]{1,0:T(8,128)(2,1)S(1)}, u32[]{:S(2)}, u32[]{:S(2)}) collective-permute-start(bf16[16,4224]{1,0:T(8,128)(2,1)S(1)} %get-tuple-element.39), channel_id=1, source_target_pairs={{0,16},{8,24},{16,0},{24,8},{1,17},{9,25},{17,1},{25,9},{2,18},{10... | collective-permute-start | bytes 405512 | tf_op jit(solution)/shard_map/ppermute | solution.py:228
  14.0 3.9 %collective-permute-done.5.r_3_.r_7_ = bf16[16,4224]{1,0:T(8,128)(2,1)S(1)} collective-permute-done((bf16[16,4224]{1,0:T(8,128)(2,1)S(1)}, bf16[16,4224]{1,0:T(8,128)(2,1)S(1)}, u32[]{:S(2)}, u32[]{:S(2)}) %collective-permute-start.5) | collective-permute-done | bytes 135200 | tf_op jit(solution)/shard_map/ppermute | solution.py:232
  18.4 1.6 %collective-permute-start.6 = (bf16[16,4224]{1,0:T(8,128)(2,1)S(1)}, bf16[16,4224]{1,0:T(8,128)(2,1)S(1)}, u32[]{:S(2)}, u32[]{:S(2)}) collective-permute-start(bf16[16,4224]{1,0:T(8,128)(2,1)S(1)} %get-tuple-element.42), channel_id=1, source_target_pairs={{0,8},{8,0},{16,24},{24,16},{1,9},{9,1},{17,25},{25,17},{2,10},{10... | collective-permute-start | bytes 405512 | tf_op jit(solution)/shard_map/ppermute | solution.py:228
  20.0 1.5 %collective-permute-start.7 = (bf16[16,4224]{1,0:T(8,128)(2,1)S(1)}, bf16[16,4224]{1,0:T(8,128)(2,1)S(1)}, u32[]{:S(2)}, u32[]{:S(2)}) collective-permute-start(bf16[16,4224]{1,0:T(8,128)(2,1)S(1)} %get-tuple-element.43), channel_id=1, source_target_pairs={{0,16},{8,24},{16,0},{24,8},{1,17},{9,25},{17,1},{25,9},{2,18},{10... | collective-permute-start | bytes 405512 | tf_op jit(solution)/shard_map/ppermute | solution.py:228
  22.5 2.9 %stage.1.r_16_ = bf16[1,2,704,2048]{3,2,1,0:T(8,128)(2,1)S(1)} custom-call(bf16[1,2,704,2048]{3,2,1,0:T(8,128)(2,1)} %src_hbm), custom_call_target="tpu_custom_call" | custom-call | bytes 11534336 | tf_op jit(solution)/shard_map/stage/pallas_call | solution.py:275
  25.5 3.1 %collective-permute-done.7.r_6_ = bf16[16,4224]{1,0:T(8,128)(2,1)S(1)} collective-permute-done((bf16[16,4224]{1,0:T(8,128)(2,1)S(1)}, bf16[16,4224]{1,0:T(8,128)(2,1)S(1)}, u32[]{:S(2)}, u32[]{:S(2)}) %collective-permute-start.7) | collective-permute-done | bytes 135200 | tf_op jit(solution)/shard_map/ppermute | solution.py:228
  30.7 5.3 %expert.1 = (bf16[128,2176]{1,0:T(8,128)(2,1)S(1)}, bf16[128,2176]{1,0:T(8,128)(2,1)S(1)}, bf16[256,704]{1,0:T(8,128)(2,1)S(1)}, bf16[256,704]{1,0:T(8,128)(2,1)S(1)}, bf16[256,704]{1,0:T(8,128)(2,1)S(1)}) custom-call(bf16[16,4224]{1,0:T(8,128)(2,1)S(1)} %get-tuple-element.37.r_0_, bf16[16,4224]{1,0:T(8,128)(2,1)S(1)} %collective-permute-done.1.r_1_, ...), custom_call_target="tpu_custom_call" | custom-call | tf_op jit(solution)/shard_map/expert/pallas_call | solution.py:294
  36.3 2.1 %down.1 = bf16[1,704,2048]{2,1,0:T(8,128)(2,1)} custom-call(bf16[16,4224]{1,0:T(8,128)(2,1)S(1)} %get-tuple-element.37.r_0_, bf16[16,4224]{1,0:T(8,128)(2,1)S(1)} %collective-permute-done.1.r_1_, bf16[16,4224]{1,0:T(8,128)(2,1)S(1)} %collective-permute-done.2.r_2_, bf16[16,4224]{1,0:T(8,128)(2,1)S(1)} %collective-permute-done.3.r_3_, ...), custom_call_target="tpu_custom_call" | custom-call | flops 738197504 | bytes 5767168 | tf_op jit(solution)/shard_map/down/pallas_call | solution.py:304
  38.5 1.0 %collective-permute-start.18 = (bf16[16,2176]{1,0:T(8,128)(2,1)S(1)}, bf16[16,2176]{1,0:T(8,128)(2,1)S(1)}, u32[]{:S(2)}, u32[]{:S(2)}) collective-permute-start(bf16[16,2176]{1,0:T(8,128)(2,1)S(1)} %get-tuple-element.54), channel_id=1, source_target_pairs={{0,8},{8,0},{16,24},{24,16},{1,9},{9,1},{17,25},{25,17},{2,10},{10... | collective-permute-start | bytes 208904 | tf_op jit(solution)/shard_map/ppermute | solution.py:228
  39.5 1.1 %collective-permute-start.19 = (bf16[16,2176]{1,0:T(8,128)(2,1)S(1)}, bf16[16,2176]{1,0:T(8,128)(2,1)S(1)}, u32[]{:S(2)}, u32[]{:S(2)}) collective-permute-start(bf16[16,2176]{1,0:T(8,128)(2,1)S(1)} %get-tuple-element.55), channel_id=1, source_target_pairs={{0,16},{8,24},{16,0},{24,8},{1,17},{9,25},{17,1},{25,9},{2,18},{10... | collective-permute-start | bytes 208904 | tf_op jit(solution)/shard_map/ppermute | solution.py:228
  40.6 1.4 %collective-permute-start.20 = (bf16[16,2176]{1,0:T(8,128)(2,1)S(1)}, bf16[16,2176]{1,0:T(8,128)(2,1)S(1)}, u32[]{:S(2)}, u32[]{:S(2)}) collective-permute-start(bf16[16,2176]{1,0:T(8,128)(2,1)S(1)} %get-tuple-element.56), channel_id=1, source_target_pairs={{0,24},{8,16},{16,8},{24,0},{1,25},{9,17},{17,9},{25,1},{2,26},{10... | collective-permute-start | bytes 208904 | tf_op jit(solution)/shard_map/ppermute | solution.py:228
  42.1 0.9 %collective-permute-start.21 = (bf16[16,2176]{1,0:T(8,128)(2,1)S(1)}, bf16[16,2176]{1,0:T(8,128)(2,1)S(1)}, u32[]{:S(2)}, u32[]{:S(2)}) collective-permute-start(bf16[16,2176]{1,0:T(8,128)(2,1)S(1)} %get-tuple-element.59), channel_id=1, source_target_pairs={{0,8},{8,0},{16,24},{24,16},{1,9},{9,1},{17,25},{25,17},{2,10},{10... | collective-permute-start | bytes 208904 | tf_op jit(solution)/shard_map/ppermute | solution.py:228
  43.0 1.1 %collective-permute-start.22 = (bf16[16,2176]{1,0:T(8,128)(2,1)S(1)}, bf16[16,2176]{1,0:T(8,128)(2,1)S(1)}, u32[]{:S(2)}, u32[]{:S(2)}) collective-permute-start(bf16[16,2176]{1,0:T(8,128)(2,1)S(1)} %get-tuple-element.60), channel_id=1, source_target_pairs={{0,16},{8,24},{16,0},{24,8},{1,17},{9,25},{17,1},{25,9},{2,18},{10... | collective-permute-start | bytes 208904 | tf_op jit(solution)/shard_map/ppermute | solution.py:228
  44.1 1.4 %collective-permute-start.23 = (bf16[16,2176]{1,0:T(8,128)(2,1)S(1)}, bf16[16,2176]{1,0:T(8,128)(2,1)S(1)}, u32[]{:S(2)}, u32[]{:S(2)}) collective-permute-start(bf16[16,2176]{1,0:T(8,128)(2,1)S(1)} %get-tuple-element.61), channel_id=1, source_target_pairs={{0,24},{8,16},{16,8},{24,0},{1,25},{9,17},{17,9},{25,1},{2,26},{10... | collective-permute-start | bytes 208904 | tf_op jit(solution)/shard_map/ppermute | solution.py:228
  45.6 0.9 %collective-permute-done.20.r_5_ = bf16[16,2176]{1,0:T(8,128)(2,1)S(1)} collective-permute-done((bf16[16,2176]{1,0:T(8,128)(2,1)S(1)}, bf16[16,2176]{1,0:T(8,128)(2,1)S(1)}, u32[]{:S(2)}, u32[]{:S(2)}) %collective-permute-start.20) | collective-permute-done | bytes 69664 | tf_op jit(solution)/shard_map/ppermute | solution.py:228
  46.9 2.3 %collective-permute-start.24 = (bf16[16,2176]{1,0:T(8,128)(2,1)S(1)}, bf16[16,2176]{1,0:T(8,128)(2,1)S(1)}, u32[]{:S(2)}, u32[]{:S(2)}) collective-permute-start(bf16[16,2176]{1,0:T(8,128)(2,1)S(1)} %get-tuple-element.57), channel_id=1, source_target_pairs={{0,6},{2,4},{4,2},{6,0},{1,7},{3,5},{5,3},{7,1},{8,14},{10,12},{12... | collective-permute-start | bytes 208904 | tf_op jit(solution)/shard_map/ppermute | solution.py:238
  49.7 2.0 %collective-permute-start.26 = (bf16[16,2176]{1,0:T(8,128)(2,1)S(1)}, bf16[16,2176]{1,0:T(8,128)(2,1)S(1)}, u32[]{:S(2)}, u32[]{:S(2)}) collective-permute-start(bf16[16,2176]{1,0:T(8,128)(2,1)S(1)} %get-tuple-element.64), channel_id=1, source_target_pairs={{0,2},{2,0},{1,3},{3,1},{4,6},{6,4},{5,7},{7,5},{8,10},{10,8},{9,1... | collective-permute-start | bytes 208904 | tf_op jit(solution)/shard_map/ppermute | solution.py:235
  51.8 2.9 %gate_up.1 = bf16[1,2,704,2048]{3,2,1,0:T(8,128)(2,1)} custom-call(bf16[16,4224]{1,0:T(8,128)(2,1)S(1)} %get-tuple-element.37.r_0_, bf16[16,4224]{1,0:T(8,128)(2,1)S(1)} %collective-permute-done.1.r_1_, bf16[16,4224]{1,0:T(8,128)(2,1)S(1)} %collective-permute-done.2.r_2_, bf16[16,4224]{1,0:T(8,128)(2,1)S(1)} %collective-permute-done.3.r_3_, ...), custom_call_target="tpu_custom_call" | custom-call | flops 1476395008 | bytes 11534336 | tf_op jit(solution)/shard_map/gate_up/pallas_call | solution.py:327
  55.0 0.7 %final.1 = (bf16[16,2048]{1,0:T(8,128)(2,1)}, f32[6,16]{1,0:T(8,128)}) custom-call(f32[16,2176]{1,0:T(8,128)S(1)} %get-tuple-element.62.own_ref, bf16[16,2176]{1,0:T(8,128)(2,1)S(1)} %collective-permute-done.24.refs_0_, bf16[16,2176]{1,0:T(8,128)(2,1)S(1)} %collective-permute-done.25.refs_1_, bf16[16,2176]{1,0:T(8,128)(2,1)S(1)} %collective-permute-done.26.refs_2_), custom_call_target="tpu_custom_call" | custom-call | tf_op jit(solution)/shard_map/final/pallas_call | solution.py:354
  (43 shorter events, 6.2 us)
Async XLA Ops:
  1.6 8.3 %collective-permute-start = (bf16[16,4224]{1,0:T(8,128)(2,1)S(1)}, bf16[16,4224]{1,0:T(8,128)(2,1)S(1)}, u32[]{:S(2)}, u32[]{:S(2)}) collective-permute-start(bf16[16,4224]{1,0:T(8,128)(2,1)S(1)} %pack.1.r_2_.r_6_), channel_id=1, source_target_pairs={{0,2},{2,0},{1,3},{3,1},{4,6},{6,4},{5,7},{7,5},{8,10},{10,8},{9,1... | collective-permute-start | bytes 405512 | tf_op jit(solution)/shard_map/ppermute | solution.py:235
  4.7 13.2 %collective-permute-start.5 = (bf16[16,4224]{1,0:T(8,128)(2,1)S(1)}, bf16[16,4224]{1,0:T(8,128)(2,1)S(1)}, u32[]{:S(2)}, u32[]{:S(2)}) collective-permute-start(bf16[16,4224]{1,0:T(8,128)(2,1)S(1)} %pack.1.r_2_.r_6_), channel_id=1, source_target_pairs={{0,4},{2,6},{4,0},{6,2},{1,5},{3,7},{5,1},{7,3},{8,12},{10,14},{12... | collective-permute-start | bytes 405512 | tf_op jit(solution)/shard_map/ppermute | solution.py:232
  7.3 10.6 %collective-permute-start.4 = (bf16[16,4224]{1,0:T(8,128)(2,1)S(1)}, bf16[16,4224]{1,0:T(8,128)(2,1)S(1)}, u32[]{:S(2)}, u32[]{:S(2)}) collective-permute-start(bf16[16,4224]{1,0:T(8,128)(2,1)S(1)} %pack.1.r_2_.r_6_), channel_id=1, source_target_pairs={{0,6},{2,4},{4,2},{6,0},{1,7},{3,5},{5,3},{7,1},{8,14},{10,12},{12... | collective-permute-start | bytes 405512 | tf_op jit(solution)/shard_map/ppermute | solution.py:238
  10.4 9.5 %collective-permute-start.1 = (bf16[16,4224]{1,0:T(8,128)(2,1)S(1)}, bf16[16,4224]{1,0:T(8,128)(2,1)S(1)}, u32[]{:S(2)}, u32[]{:S(2)}) collective-permute-start(bf16[16,4224]{1,0:T(8,128)(2,1)S(1)} %get-tuple-element.38), channel_id=1, source_target_pairs={{0,8},{8,0},{16,24},{24,16},{1,9},{9,1},{17,25},{25,17},{2,10},{10... | collective-permute-start | bytes 405512 | tf_op jit(solution)/shard_map/ppermute | solution.py:228
  12.2 9.3 %collective-permute-start.2 = (bf16[16,4224]{1,0:T(8,128)(2,1)S(1)}, bf16[16,4224]{1,0:T(8,128)(2,1)S(1)}, u32[]{:S(2)}, u32[]{:S(2)}) collective-permute-start(bf16[16,4224]{1,0:T(8,128)(2,1)S(1)} %get-tuple-element.39), channel_id=1, source_target_pairs={{0,16},{8,24},{16,0},{24,8},{1,17},{9,25},{17,1},{25,9},{2,18},{10... | collective-permute-start | bytes 405512 | tf_op jit(solution)/shard_map/ppermute | solution.py:228
  13.7 8.2 %collective-permute-start.3 = (bf16[16,4224]{1,0:T(8,128)(2,1)S(1)}, bf16[16,4224]{1,0:T(8,128)(2,1)S(1)}, u32[]{:S(2)}, u32[]{:S(2)}) collective-permute-start(bf16[16,4224]{1,0:T(8,128)(2,1)S(1)} %get-tuple-element.40), channel_id=1, source_target_pairs={{0,24},{8,16},{16,8},{24,0},{1,25},{9,17},{17,9},{25,1},{2,26},{10... | collective-permute-start | bytes 405512 | tf_op jit(solution)/shard_map/ppermute | solution.py:228
  17.9 4.1 %collective-permute-start.9 = (bf16[16,4224]{1,0:T(8,128)(2,1)S(1)}, bf16[16,4224]{1,0:T(8,128)(2,1)S(1)}, u32[]{:S(2)}, u32[]{:S(2)}) collective-permute-start(bf16[16,4224]{1,0:T(8,128)(2,1)S(1)} %get-tuple-element.37.r_0_), channel_id=1, source_target_pairs={{0,1},{1,0},{2,3},{3,2},{4,5},{5,4},{6,7},{7,6},{8,9},{9,8},{10,11... | collective-permute-start | bytes 405512 | tf_op jit(solution)/shard_map/ppermute | solution.py:241
  18.4 7.0 %collective-permute-start.6 = (bf16[16,4224]{1,0:T(8,128)(2,1)S(1)}, bf16[16,4224]{1,0:T(8,128)(2,1)S(1)}, u32[]{:S(2)}, u32[]{:S(2)}) collective-permute-start(bf16[16,4224]{1,0:T(8,128)(2,1)S(1)} %get-tuple-element.42), channel_id=1, source_target_pairs={{0,8},{8,0},{16,24},{24,16},{1,9},{9,1},{17,25},{25,17},{2,10},{10... | collective-permute-start | bytes 405512 | tf_op jit(solution)/shard_map/ppermute | solution.py:228
  20.0 8.6 %collective-permute-start.7 = (bf16[16,4224]{1,0:T(8,128)(2,1)S(1)}, bf16[16,4224]{1,0:T(8,128)(2,1)S(1)}, u32[]{:S(2)}, u32[]{:S(2)}) collective-permute-start(bf16[16,4224]{1,0:T(8,128)(2,1)S(1)} %get-tuple-element.43), channel_id=1, source_target_pairs={{0,16},{8,24},{16,0},{24,8},{1,17},{9,25},{17,1},{25,9},{2,18},{10... | collective-permute-start | bytes 405512 | tf_op jit(solution)/shard_map/ppermute | solution.py:228
  21.5 7.1 %collective-permute-start.8 = (bf16[16,4224]{1,0:T(8,128)(2,1)S(1)}, bf16[16,4224]{1,0:T(8,128)(2,1)S(1)}, u32[]{:S(2)}, u32[]{:S(2)}) collective-permute-start(bf16[16,4224]{1,0:T(8,128)(2,1)S(1)} %get-tuple-element.44), channel_id=1, source_target_pairs={{0,24},{8,16},{16,8},{24,0},{1,25},{9,17},{17,9},{25,1},{2,26},{10... | collective-permute-start | bytes 405512 | tf_op jit(solution)/shard_map/ppermute | solution.py:228
  22.0 7.1 %collective-permute-start.13 = (bf16[16,4224]{1,0:T(8,128)(2,1)S(1)}, bf16[16,4224]{1,0:T(8,128)(2,1)S(1)}, u32[]{:S(2)}, u32[]{:S(2)}) collective-permute-start(bf16[16,4224]{1,0:T(8,128)(2,1)S(1)} %get-tuple-element.41.r_4_), channel_id=1, source_target_pairs={{0,1},{1,0},{2,3},{3,2},{4,5},{5,4},{6,7},{7,6},{8,9},{9,8},{10,11... | collective-permute-start | bytes 405512 | tf_op jit(solution)/shard_map/ppermute | solution.py:241
  22.0 7.2 %collective-permute-start.10 = (bf16[16,4224]{1,0:T(8,128)(2,1)S(1)}, bf16[16,4224]{1,0:T(8,128)(2,1)S(1)}, u32[]{:S(2)}, u32[]{:S(2)}) collective-permute-start(bf16[16,4224]{1,0:T(8,128)(2,1)S(1)} %collective-permute-done.1.r_1_), channel_id=1, source_target_pairs={{0,1},{1,0},{2,3},{3,2},{4,5},{5,4},{6,7},{7,6},{8,9},{9,8},{10,11... | collective-permute-start | bytes 405512 | tf_op jit(solution)/shard_map/ppermute | solution.py:241
  25.4 4.2 %collective-permute-start.11 = (bf16[16,4224]{1,0:T(8,128)(2,1)S(1)}, bf16[16,4224]{1,0:T(8,128)(2,1)S(1)}, u32[]{:S(2)}, u32[]{:S(2)}) collective-permute-start(bf16[16,4224]{1,0:T(8,128)(2,1)S(1)} %collective-permute-done.2.r_2_), channel_id=1, source_target_pairs={{0,1},{1,0},{2,3},{3,2},{4,5},{5,4},{6,7},{7,6},{8,9},{9,8},{10,11... | collective-permute-start | bytes 405512 | tf_op jit(solution)/shard_map/ppermute | solution.py:241
  28.6 1.5 %collective-permute-start.15 = (bf16[16,4224]{1,0:T(8,128)(2,1)S(1)}, bf16[16,4224]{1,0:T(8,128)(2,1)S(1)}, u32[]{:S(2)}, u32[]{:S(2)}) collective-permute-start(bf16[16,4224]{1,0:T(8,128)(2,1)S(1)} %collective-permute-done.7.r_6_), channel_id=1, source_target_pairs={{0,1},{1,0},{2,3},{3,2},{4,5},{5,4},{6,7},{7,6},{8,9},{9,8},{10,11... | collective-permute-start | bytes 405512 | tf_op jit(solution)/shard_map/ppermute | solution.py:241
  35.9 2.5 %collective-permute-start.17 = (bf16[128,2176]{1,0:T(8,128)(2,1)S(1)}, bf16[128,2176]{1,0:T(8,128)(2,1)S(1)}, u32[]{:S(2)}, u32[]{:S(2)}) collective-permute-start(bf16[128,2176]{1,0:T(8,128)(2,1)S(1)} %get-tuple-element.51), channel_id=1, source_target_pairs={{0,1},{1,0},{2,3},{3,2},{4,5},{5,4},{6,7},{7,6},{8,9},{9,8},{10,11... | collective-permute-start | bytes 1671176 | tf_op jit(solution)/shard_map/ppermute | solution.py:241
  38.5 5.6 %collective-permute-start.18 = (bf16[16,2176]{1,0:T(8,128)(2,1)S(1)}, bf16[16,2176]{1,0:T(8,128)(2,1)S(1)}, u32[]{:S(2)}, u32[]{:S(2)}) collective-permute-start(bf16[16,2176]{1,0:T(8,128)(2,1)S(1)} %get-tuple-element.54), channel_id=1, source_target_pairs={{0,8},{8,0},{16,24},{24,16},{1,9},{9,1},{17,25},{25,17},{2,10},{10... | collective-permute-start | bytes 208904 | tf_op jit(solution)/shard_map/ppermute | solution.py:228
  39.5 6.1 %collective-permute-start.19 = (bf16[16,2176]{1,0:T(8,128)(2,1)S(1)}, bf16[16,2176]{1,0:T(8,128)(2,1)S(1)}, u32[]{:S(2)}, u32[]{:S(2)}) collective-permute-start(bf16[16,2176]{1,0:T(8,128)(2,1)S(1)} %get-tuple-element.55), channel_id=1, source_target_pairs={{0,16},{8,24},{16,0},{24,8},{1,17},{9,25},{17,1},{25,9},{2,18},{10... | collective-permute-start | bytes 208904 | tf_op jit(solution)/shard_map/ppermute | solution.py:228
  40.6 5.8 %collective-permute-start.20 = (bf16[16,2176]{1,0:T(8,128)(2,1)S(1)}, bf16[16,2176]{1,0:T(8,128)(2,1)S(1)}, u32[]{:S(2)}, u32[]{:S(2)}) collective-permute-start(bf16[16,2176]{1,0:T(8,128)(2,1)S(1)} %get-tuple-element.56), channel_id=1, source_target_pairs={{0,24},{8,16},{16,8},{24,0},{1,25},{9,17},{17,9},{25,1},{2,26},{10... | collective-permute-start | bytes 208904 | tf_op jit(solution)/shard_map/ppermute | solution.py:228
  42.1 7.1 %collective-permute-start.21 = (bf16[16,2176]{1,0:T(8,128)(2,1)S(1)}, bf16[16,2176]{1,0:T(8,128)(2,1)S(1)}, u32[]{:S(2)}, u32[]{:S(2)}) collective-permute-start(bf16[16,2176]{1,0:T(8,128)(2,1)S(1)} %get-tuple-element.59), channel_id=1, source_target_pairs={{0,8},{8,0},{16,24},{24,16},{1,9},{9,1},{17,25},{25,17},{2,10},{10... | collective-permute-start | bytes 208904 | tf_op jit(solution)/shard_map/ppermute | solution.py:228
  43.0 6.2 %collective-permute-start.22 = (bf16[16,2176]{1,0:T(8,128)(2,1)S(1)}, bf16[16,2176]{1,0:T(8,128)(2,1)S(1)}, u32[]{:S(2)}, u32[]{:S(2)}) collective-permute-start(bf16[16,2176]{1,0:T(8,128)(2,1)S(1)} %get-tuple-element.60), channel_id=1, source_target_pairs={{0,16},{8,24},{16,0},{24,8},{1,17},{9,25},{17,1},{25,9},{2,18},{10... | collective-permute-start | bytes 208904 | tf_op jit(solution)/shard_map/ppermute | solution.py:228
  44.1 5.2 %collective-permute-start.23 = (bf16[16,2176]{1,0:T(8,128)(2,1)S(1)}, bf16[16,2176]{1,0:T(8,128)(2,1)S(1)}, u32[]{:S(2)}, u32[]{:S(2)}) collective-permute-start(bf16[16,2176]{1,0:T(8,128)(2,1)S(1)} %get-tuple-element.61), channel_id=1, source_target_pairs={{0,24},{8,16},{16,8},{24,0},{1,25},{9,17},{17,9},{25,1},{2,26},{10... | collective-permute-start | bytes 208904 | tf_op jit(solution)/shard_map/ppermute | solution.py:228
  46.9 8.1 %collective-permute-start.24 = (bf16[16,2176]{1,0:T(8,128)(2,1)S(1)}, bf16[16,2176]{1,0:T(8,128)(2,1)S(1)}, u32[]{:S(2)}, u32[]{:S(2)}) collective-permute-start(bf16[16,2176]{1,0:T(8,128)(2,1)S(1)} %get-tuple-element.57), channel_id=1, source_target_pairs={{0,6},{2,4},{4,2},{6,0},{1,7},{3,5},{5,3},{7,1},{8,14},{10,12},{12... | collective-permute-start | bytes 208904 | tf_op jit(solution)/shard_map/ppermute | solution.py:238
  49.2 5.8 %collective-permute-start.25 = (bf16[16,2176]{1,0:T(8,128)(2,1)S(1)}, bf16[16,2176]{1,0:T(8,128)(2,1)S(1)}, u32[]{:S(2)}, u32[]{:S(2)}) collective-permute-start(bf16[16,2176]{1,0:T(8,128)(2,1)S(1)} %get-tuple-element.63), channel_id=1, source_target_pairs={{0,4},{2,6},{4,0},{6,2},{1,5},{3,7},{5,1},{7,3},{8,12},{10,14},{12... | collective-permute-start | bytes 208904 | tf_op jit(solution)/shard_map/ppermute | solution.py:232
  49.7 5.3 %collective-permute-start.26 = (bf16[16,2176]{1,0:T(8,128)(2,1)S(1)}, bf16[16,2176]{1,0:T(8,128)(2,1)S(1)}, u32[]{:S(2)}, u32[]{:S(2)}) collective-permute-start(bf16[16,2176]{1,0:T(8,128)(2,1)S(1)} %get-tuple-element.64), channel_id=1, source_target_pairs={{0,2},{2,0},{1,3},{3,1},{4,6},{6,4},{5,7},{7,5},{8,10},{10,8},{9,1... | collective-permute-start | bytes 208904 | tf_op jit(solution)/shard_map/ppermute | solution.py:235
  (4 other events, 12.9 us)
